TPU v7x, 32 devices: a whole 2x2x4 slice. The times are simulated.
32 devices in a mesh: dx: 4 (over z), dy: 8 (over y, x, core).
Axes of the slice: x: 2, y: 2, z: 4, core: 2. Of those that a mesh axis runs over, the one named last changes fastest.
Arguments:
- dust: bfloat16 [131072, 256], P(('dx', 'dy')), may hold values from 0.19921875 to 2
- classes: int32 [131072], P(('dx', 'dy')), may hold values from 0 to 7
- kernels: bfloat16 [8, 2, 128, 128], replicated, may hold values from -0.5 to 0.5
- export_ids: int32 [32, 4, 1024], P(('dx', 'dy')), may hold values from 0 to 4095
- faces: int32 [6, 131072], P(None, ('dx', 'dy')), may hold values from 0 to 8191, as said below
- face_coef: float32 [6, 131072], P(None, ('dx', 'dy')), may hold values from 0.04 to 0.16
- mig_ids: int32 [1024, 16], P(('dx', 'dy')), may hold values from 0 to 4095, as said below
- mig_counts: int32 [32, 32], P(('dx', 'dy')), may hold values from 0 to 16, as said below
Outputs:
- dust_next: bfloat16 [131072, 256], P(('dx', 'dy'))
- arrivals: bfloat16 [16384, 256], P(('dx', 'dy'))
Inputs may be any that keep to these rules, and one draw needn't show every extreme that they name: Entries below 4096 name cells of the same domain, entries from 4096 on name its received rows in the order of the steps; each cell has 4 to 6 faces and its other slots name the cell itself. `mig_ids`: the 512 entries of one domain's rows are distinct local cells. `mig_counts`: one destination, drawn from the seed, receives 16 cells from every domain.
All inputs are finite; a program needn't handle non-finite values.
Results may differ from a plain program's by a relative error of at most 0.0054.
Values may be sent and summed in bfloat16 or wider, within the bound.
No kernel may reach another device: no remote copies, remote signals or barrier semaphores. Data moves between devices by JAX's collectives and lax.ppermute only.
A program may use at most 64 MiB of HBM per device.

v0:
```python
import jax
import jax.numpy as jnp
from jax import lax
from jax.sharding import PartitionSpec as P

SUBSTEPS = 6


def passed_along(block, axis, distance):
    devices = range(lax.axis_size(axis))
    route = [((i - distance) % len(devices), i) for i in devices]
    return lax.ppermute(block, axis, route)


def coagulate(dust_rows, dust_classes, kernels):
    row_count = dust_rows.shape[0]
    class_count = kernels.shape[0]
    species = kernels.shape[1]
    bins = kernels.shape[2]
    block_rows = 2048
    block_count = row_count // block_rows
    class_ids = jnp.arange(class_count, dtype=jnp.int32)

    def run_block(pieces):
        piece_rows, piece_classes = pieces
        selector = (piece_classes[:, None] == class_ids[None, :]).astype(jnp.bfloat16)
        grain_state = piece_rows.astype(jnp.float32).reshape(block_rows, species, bins)
        for substep in range(SUBSTEPS):
            operand = grain_state.astype(jnp.bfloat16)
            spread = operand[:, :, None, :] * selector[:, None, :, None]
            product = jnp.einsum(
                "rskb,ksbc->rsc", spread, kernels, preferred_element_type=jnp.float32
            )
            mean_square = jnp.mean(grain_state * grain_state, axis=2, keepdims=True)
            grain_state = grain_state + product * (mean_square / (1.0 + mean_square))
        return grain_state.reshape(block_rows, species * bins).astype(jnp.bfloat16)

    blocked = lax.map(
        run_block,
        (
            dust_rows.reshape(block_count, block_rows, species * bins),
            dust_classes.reshape(block_count, block_rows),
        ),
    )
    return blocked.reshape(row_count, species * bins)


def body(dust, classes, kernels, export_ids, faces, face_coef, mig_ids, mig_counts):
    row_width = dust.shape[1]
    export_rows = export_ids.reshape(4, export_ids.shape[2])
    export_count = export_rows.shape[1]
    coag = coagulate(dust, classes, kernels)
    outbound = jnp.take(coag, export_rows.reshape(4 * export_count), axis=0).reshape(
        4, export_count, row_width
    )
    received = []
    for direction, offset in ((0, 1), (1, -1)):
        received.append(passed_along(outbound[direction], "dx", offset))
    for direction, offset in ((2, 1), (3, -1)):
        received.append(passed_along(outbound[direction], "dy", offset))
    ghosts = jnp.concatenate(received, axis=0)
    extended = jnp.concatenate([coag, ghosts], axis=0)
    own_rows = coag.astype(jnp.float32)
    flux_sum = own_rows
    for face in range(faces.shape[0]):
        neighbour = jnp.take(extended, faces[face], axis=0).astype(jnp.float32)
        flux_sum = flux_sum + face_coef[face][:, None] * (neighbour - own_rows)
    updated = flux_sum.astype(jnp.bfloat16)
    domains = mig_counts.shape[1]
    capacity = mig_ids.shape[1]
    filled = jnp.arange(capacity, dtype=jnp.int32)[None, :] < mig_counts[0][:, None]
    picked = jnp.take(updated, mig_ids.reshape(domains * capacity), axis=0).reshape(
        domains, capacity, row_width
    )
    leaving = jnp.where(filled[:, :, None], picked, jnp.zeros_like(picked))
    arrived = lax.all_to_all(leaving, ("dx", "dy"), split_axis=0, concat_axis=0, tiled=True)
    arrivals = arrived.reshape(domains * capacity, row_width)
    return (updated, arrivals)


def solution(mesh):
    return jax.shard_map(
        body,
        mesh=mesh,
        in_specs=(
            P(("dx", "dy"), None),
            P(("dx", "dy")),
            P(),
            P(("dx", "dy"), None, None),
            P(None, ("dx", "dy")),
            P(None, ("dx", "dy")),
            P(("dx", "dy"), None),
            P(("dx", "dy"), None),
        ),
        out_specs=(P(("dx", "dy"), None), P(("dx", "dy"), None)),
        check_vma=False,
    )
```

profile of v0, /device:TPU:0, one launch (start us, length us, event | category | flops | bytes accessed | tf_op | source)
XLA Modules:
  0.0 315.7 jit_solution(7137956452919442197)
XLA Ops:
  0.6 2.1 copy.26
  2.7 0.7 reshape.238
  3.4 114.8 %while.11 = (s32[]{:T(128)}, bf16[2,2048,256]{2,1,0:T(8,128)(2,1)S(1)}, bf16[2,2048,256]{2,1,0:T(8,128)(2,1)}, s32[2,2048]{1,0:T(2,128)S(1)}, bf16[8,2,128,128]{2,3,0,1:T(8,128)(2,1)}, /*index=5*/s32[]{:T(128)}) while((s32[]{:T(128)}, bf16[2,2048,256]{2,1,0:T(8,128)(2,1)S(1)}, bf16[2,2048,256]{2,1,0:T(8,128)(2,1)}, ...), condition=%wide.region_7.8_spmd.clone, body=%wide.region_0.7_spmd.clone.sunk | while | flops 6484475904 | bytes 60416080 | solution.py:38
  3.5 2.3 constant_dynamic-slice_fusion.4
  5.8 1.5 copy.52
  7.2 1.3 copy.53
  8.6 0.2 fusion.129
  8.8 6.9 %multiply_reduce_fusion.10 = (f32[2048,2]{0,1:T(2,128)S(1)}, bf16[2048,2,128]{0,2,1:T(8,128)(2,1)}, f32[2048,2,128]{0,2,1:T(8,128)}) fusion(f32[2048,2]{0,1:T(2,128)S(1)} %add_divide_fusion.12, bf16[8,2,128,128]{2,3,0,1:T(8,128)(2,1)} %get-tuple-element.188, bf16[2048,8]{0,1:T(8,128)(2,1)S(1)} %fusion.130, bf16[2048,2,128]{2,0,1:T(8,128)(2,1)} %copy.53, ...), kind=kOutput, calls=%fused_computation.58.clone.1 | convolution fusion | flops 1081077760 | bytes 5832704 | tf_op jit(solution)/shard_map/while/body/eval_jaxpr/rskb,ksbc->rsc/dot_general | solution.py:31
  15.8 1.6 copy.54
  17.4 7.1 %multiply_reduce_fusion.11 = (f32[2048,2]{0,1:T(2,128)S(1)}, bf16[2048,2,128]{0,2,1:T(8,128)(2,1)}, f32[2048,2,128]{0,2,1:T(8,128)}) fusion(f32[2048,2,128]{0,2,1:T(8,128)} %get-tuple-element.157, f32[2048,2]{0,1:T(2,128)S(1)} %add_divide_fusion.13, bf16[8,2,128,128]{2,3,0,1:T(8,128)(2,1)} %get-tuple-element.188, ...), kind=kOutput, calls=%fused_computation.57.clone.1 | convolution fusion | flops 1080553472 | bytes 6881280 | tf_op jit(solution)/shard_map/while/body/eval_jaxpr/rskb,ksbc->rsc/dot_general | solution.py:31
  24.5 1.6 copy.55
  26.2 7.1 %multiply_reduce_fusion.12 = (f32[2048,2]{0,1:T(2,128)S(1)}, bf16[2048,2,128]{0,2,1:T(8,128)(2,1)}, f32[2048,2,128]{0,2,1:T(8,128)}) fusion(f32[2048,2,128]{0,2,1:T(8,128)} %get-tuple-element.160, f32[2048,2]{0,1:T(2,128)S(1)} %add_divide_fusion.14, bf16[8,2,128,128]{2,3,0,1:T(8,128)(2,1)} %get-tuple-element.188, ...), kind=kOutput, calls=%fused_computation.56.clone.1 | convolution fusion | flops 1080553472 | bytes 6881280 | tf_op jit(solution)/shard_map/while/body/eval_jaxpr/rskb,ksbc->rsc/dot_general | solution.py:31
  33.3 1.6 copy.56
  35.0 7.1 %multiply_reduce_fusion.13 = (f32[2048,2]{0,1:T(2,128)S(1)}, bf16[2048,2,128]{0,2,1:T(8,128)(2,1)}, f32[2048,2,128]{0,2,1:T(8,128)}) fusion(f32[2048,2,128]{0,2,1:T(8,128)} %get-tuple-element.163, f32[2048,2]{0,1:T(2,128)S(1)} %add_divide_fusion.15, bf16[8,2,128,128]{2,3,0,1:T(8,128)(2,1)} %get-tuple-element.188, ...), kind=kOutput, calls=%fused_computation.55.clone.1 | convolution fusion | flops 1080553472 | bytes 6881280 | tf_op jit(solution)/shard_map/while/body/eval_jaxpr/rskb,ksbc->rsc/dot_general | solution.py:31
  42.1 1.6 copy.57
  43.8 7.1 %multiply_reduce_fusion.14 = (f32[2048,2]{0,1:T(2,128)S(1)}, bf16[2048,2,128]{0,2,1:T(8,128)(2,1)}, f32[2048,2,128]{0,2,1:T(8,128)}) fusion(f32[2048,2,128]{0,2,1:T(8,128)} %get-tuple-element.166, f32[2048,2]{0,1:T(2,128)S(1)} %add_divide_fusion.16, bf16[8,2,128,128]{2,3,0,1:T(8,128)(2,1)} %get-tuple-element.188, ...), kind=kOutput, calls=%fused_computation.54.clone.1 | convolution fusion | flops 1080553472 | bytes 6881280 | tf_op jit(solution)/shard_map/while/body/eval_jaxpr/rskb,ksbc->rsc/dot_general | solution.py:31
  50.9 1.6 copy.58
  52.6 6.7 %fusion.131 = bf16[2048,2,128]{0,2,1:T(8,128)(2,1)} fusion(f32[2048,2,128]{0,2,1:T(8,128)} %get-tuple-element.169, bf16[8,2,128,128]{2,3,0,1:T(8,128)(2,1)} %get-tuple-element.188, bf16[2048,2,128]{2,0,1:T(8,128)(2,1)S(1)} %copy.58, bf16[2048,8]{0,1:T(8,128)(2,1)S(1)} %fusion.130, f32[2048,2]{0,1:T(2,128)S(1)} %add_divide_fusion.17), kind=kOutput, calls=%fused_computation.52.clone.1 | convolution fusion | flops 1079508992 | bytes 4767744 | tf_op jit(solution)/shard_map/while/body/eval_jaxpr/rskb,ksbc->rsc/dot_general | solution.py:31
  59.3 1.5 copy.59
  60.8 0.1 constant_dynamic-update-slice_fusion.7
  60.9 2.3 constant_dynamic-slice_fusion.4
  63.2 1.5 copy.52
  64.7 1.3 copy.53
  66.0 0.2 fusion.129
  66.2 6.9 %multiply_reduce_fusion.10 = (f32[2048,2]{0,1:T(2,128)S(1)}, bf16[2048,2,128]{0,2,1:T(8,128)(2,1)}, f32[2048,2,128]{0,2,1:T(8,128)}) fusion(f32[2048,2]{0,1:T(2,128)S(1)} %add_divide_fusion.12, bf16[8,2,128,128]{2,3,0,1:T(8,128)(2,1)} %get-tuple-element.188, bf16[2048,8]{0,1:T(8,128)(2,1)S(1)} %fusion.130, bf16[2048,2,128]{2,0,1:T(8,128)(2,1)} %copy.53, ...), kind=kOutput, calls=%fused_computation.58.clone.1 | convolution fusion | flops 1081077760 | bytes 5832704 | tf_op jit(solution)/shard_map/while/body/eval_jaxpr/rskb,ksbc->rsc/dot_general | solution.py:31
  73.2 1.6 copy.54
  74.8 7.1 %multiply_reduce_fusion.11 = (f32[2048,2]{0,1:T(2,128)S(1)}, bf16[2048,2,128]{0,2,1:T(8,128)(2,1)}, f32[2048,2,128]{0,2,1:T(8,128)}) fusion(f32[2048,2,128]{0,2,1:T(8,128)} %get-tuple-element.157, f32[2048,2]{0,1:T(2,128)S(1)} %add_divide_fusion.13, bf16[8,2,128,128]{2,3,0,1:T(8,128)(2,1)} %get-tuple-element.188, ...), kind=kOutput, calls=%fused_computation.57.clone.1 | convolution fusion | flops 1080553472 | bytes 6881280 | tf_op jit(solution)/shard_map/while/body/eval_jaxpr/rskb,ksbc->rsc/dot_general | solution.py:31
  82.0 1.6 copy.55
  83.6 7.1 %multiply_reduce_fusion.12 = (f32[2048,2]{0,1:T(2,128)S(1)}, bf16[2048,2,128]{0,2,1:T(8,128)(2,1)}, f32[2048,2,128]{0,2,1:T(8,128)}) fusion(f32[2048,2,128]{0,2,1:T(8,128)} %get-tuple-element.160, f32[2048,2]{0,1:T(2,128)S(1)} %add_divide_fusion.14, bf16[8,2,128,128]{2,3,0,1:T(8,128)(2,1)} %get-tuple-element.188, ...), kind=kOutput, calls=%fused_computation.56.clone.1 | convolution fusion | flops 1080553472 | bytes 6881280 | tf_op jit(solution)/shard_map/while/body/eval_jaxpr/rskb,ksbc->rsc/dot_general | solution.py:31
  90.8 1.6 copy.56
  92.4 7.1 %multiply_reduce_fusion.13 = (f32[2048,2]{0,1:T(2,128)S(1)}, bf16[2048,2,128]{0,2,1:T(8,128)(2,1)}, f32[2048,2,128]{0,2,1:T(8,128)}) fusion(f32[2048,2,128]{0,2,1:T(8,128)} %get-tuple-element.163, f32[2048,2]{0,1:T(2,128)S(1)} %add_divide_fusion.15, bf16[8,2,128,128]{2,3,0,1:T(8,128)(2,1)} %get-tuple-element.188, ...), kind=kOutput, calls=%fused_computation.55.clone.1 | convolution fusion | flops 1080553472 | bytes 6881280 | tf_op jit(solution)/shard_map/while/body/eval_jaxpr/rskb,ksbc->rsc/dot_general | solution.py:31
  99.5 1.6 copy.57
  101.2 7.1 %multiply_reduce_fusion.14 = (f32[2048,2]{0,1:T(2,128)S(1)}, bf16[2048,2,128]{0,2,1:T(8,128)(2,1)}, f32[2048,2,128]{0,2,1:T(8,128)}) fusion(f32[2048,2,128]{0,2,1:T(8,128)} %get-tuple-element.166, f32[2048,2]{0,1:T(2,128)S(1)} %add_divide_fusion.16, bf16[8,2,128,128]{2,3,0,1:T(8,128)(2,1)} %get-tuple-element.188, ...), kind=kOutput, calls=%fused_computation.54.clone.1 | convolution fusion | flops 1080553472 | bytes 6881280 | tf_op jit(solution)/shard_map/while/body/eval_jaxpr/rskb,ksbc->rsc/dot_general | solution.py:31
  108.3 1.6 copy.58
  110.0 6.7 %fusion.131 = bf16[2048,2,128]{0,2,1:T(8,128)(2,1)} fusion(f32[2048,2,128]{0,2,1:T(8,128)} %get-tuple-element.169, bf16[8,2,128,128]{2,3,0,1:T(8,128)(2,1)} %get-tuple-element.188, bf16[2048,2,128]{2,0,1:T(8,128)(2,1)S(1)} %copy.58, bf16[2048,8]{0,1:T(8,128)(2,1)S(1)} %fusion.130, f32[2048,2]{0,1:T(2,128)S(1)} %add_divide_fusion.17), kind=kOutput, calls=%fused_computation.52.clone.1 | convolution fusion | flops 1079508992 | bytes 4767744 | tf_op jit(solution)/shard_map/while/body/eval_jaxpr/rskb,ksbc->rsc/dot_general | solution.py:31
  116.7 1.5 copy.59
  118.2 0.1 constant_dynamic-update-slice_fusion.7
  118.4 17.0 %gather_fusion = bf16[4096,256]{1,0:T(8,128)(2,1)} fusion(bf16[4096,256]{1,0:T(8,128)(2,1)S(1)} %bitcast.116, s32[4096]{0:T(1024)S(1)} %broadcast_clamp_fusion), kind=kCustom, calls=%fused_computation.6 | custom fusion | bytes 4210688 | tf_op jit(solution)/shard_map/jit(_take)/gather | solution.py:53
  135.4 1.9 broadcast_select_fusion
  137.3 1.3 fusion.103
  138.7 3.0 collective-permute-start
  141.7 2.0 collective-permute-start.1
  143.8 2.9 collective-permute-start.3
  146.6 1.5 constant_dynamic-update-slice_fusion.5
  148.4 0.1 iota_compare_fusion.1
  148.6 0.1 reshape.240
  148.7 0.1 copy.28
  148.8 8.1 %collective-permute-done = bf16[1024,256]{1,0:T(8,128)(2,1)} collective-permute-done((bf16[1024,256]{1,0:T(8,128)(2,1)}, bf16[1024,256]{1,0:T(8,128)(2,1)}, u32[]{:S(2)}, u32[]{:S(2)}) %collective-permute-start) | collective-permute-done | bytes 524320 | tf_op jit(solution)/shard_map/ppermute | solution.py:12
  156.9 1.9 constant_dynamic-update-slice_fusion.4
  158.7 7.9 %collective-permute-done.1 = bf16[1024,256]{1,0:T(8,128)(2,1)} collective-permute-done((bf16[1024,256]{1,0:T(8,128)(2,1)}, bf16[1024,256]{1,0:T(8,128)(2,1)}, u32[]{:S(2)}, u32[]{:S(2)}) %collective-permute-start.1) | collective-permute-done | bytes 524320 | tf_op jit(solution)/shard_map/ppermute | solution.py:12
  166.7 1.9 constant_dynamic-update-slice_fusion.3
  168.5 0.8 constant_dynamic-update-slice_fusion.2
  169.4 0.8 constant_dynamic-update-slice_fusion.1
  170.2 18.7 %gather_fusion.4 = bf16[4096,256]{1,0:T(8,128)(2,1)} fusion(bf16[8192,256]{1,0:T(8,128)(2,1)} %constant_dynamic-update-slice_fusion.1, s32[4096]{0:T(1024)S(1)} %get-tuple-element.101), kind=kCustom, calls=%fused_computation.2.clone | custom fusion | bytes 4210688 | tf_op jit(solution)/shard_map/jit(_take)/gather | solution.py:66
  188.9 18.6 %gather_fusion.5 = bf16[4096,256]{1,0:T(8,128)(2,1)} fusion(bf16[8192,256]{1,0:T(8,128)(2,1)} %constant_dynamic-update-slice_fusion.1, s32[4096]{0:T(1024)S(1)} %get-tuple-element.102), kind=kCustom, calls=%fused_computation.3.clone | custom fusion | bytes 4210688 | tf_op jit(solution)/shard_map/jit(_take)/gather | solution.py:66
  207.5 18.7 %gather_fusion.6 = bf16[4096,256]{1,0:T(8,128)(2,1)} fusion(bf16[8192,256]{1,0:T(8,128)(2,1)} %constant_dynamic-update-slice_fusion.1, s32[4096]{0:T(1024)S(1)} %get-tuple-element.103), kind=kCustom, calls=%fused_computation.4.clone | custom fusion | bytes 4210688 | tf_op jit(solution)/shard_map/jit(_take)/gather | solution.py:66
  226.2 18.7 %gather_fusion.2 = bf16[4096,256]{1,0:T(8,128)(2,1)} fusion(bf16[8192,256]{1,0:T(8,128)(2,1)} %constant_dynamic-update-slice_fusion.1, s32[4096]{0:T(1024)S(1)} %get-tuple-element.99), kind=kCustom, calls=%fused_computation.clone | custom fusion | bytes 4210688 | tf_op jit(solution)/shard_map/jit(_take)/gather | solution.py:66
  244.8 18.7 %gather_fusion.3 = bf16[4096,256]{1,0:T(8,128)(2,1)} fusion(bf16[8192,256]{1,0:T(8,128)(2,1)} %constant_dynamic-update-slice_fusion.1, s32[4096]{0:T(1024)S(1)} %get-tuple-element.100), kind=kCustom, calls=%fused_computation.1.clone | custom fusion | bytes 4210688 | tf_op jit(solution)/shard_map/jit(_take)/gather | solution.py:66
  263.5 18.7 %gather_fusion.7 = bf16[4096,256]{1,0:T(8,128)(2,1)} fusion(bf16[8192,256]{1,0:T(8,128)(2,1)} %constant_dynamic-update-slice_fusion.1, s32[4096]{0:T(1024)S(1)} %get-tuple-element.104), kind=kCustom, calls=%fused_computation.5.clone | custom fusion | bytes 4210688 | tf_op jit(solution)/shard_map/jit(_take)/gather | solution.py:66
  282.2 12.3 %fusion.91 = bf16[4096,256]{1,0:T(8,128)(2,1)} fusion(bf16[4096,256]{1,0:T(8,128)(2,1)} %gather_fusion.7, bf16[4096,256]{1,0:T(8,128)(2,1)} %gather_fusion.6, bf16[4096,256]{1,0:T(8,128)(2,1)} %gather_fusion.5, bf16[4096,256]{1,0:T(8,128)(2,1)} %gather_fusion.4, bf16[4096,256]{1,0:T(8,128)(2,1)} %gather_fusion.3, bf16[4096,256]{1,0:T(8,128)(2,1)} %gather_fusion.2, ...), kind=kLoop, calls=%fused_computation.83 | loop fusion | flops 33554432 | bytes 16900096 | tf_op jit(solution)/shard_map/convert_element_type | solution.py:68
  294.5 3.4 %gather_fusion.1 = bf16[512,256]{1,0:T(8,128)(2,1)S(1)} fusion(bf16[4096,256]{1,0:T(8,128)(2,1)} %fusion.91, s32[1024]{0:T(1024)S(1)} %pad_clamp_fusion), kind=kCustom, calls=%fused_computation.7 | custom fusion | bytes 526336 | tf_op jit(solution)/shard_map/jit(_take)/gather | solution.py:72
  297.9 0.2 select_select_fusion
  298.1 16.8 %all_to_all.5 = bf16[32,16,256]{2,1,0:T(8,128)(2,1)S(1)} all-to-all(bf16[32,16,256]{2,1,0:T(8,128)(2,1)S(1)} %select_select_fusion), channel_id=1, replica_groups=mesh['dx'=4,'dy'=8] {'dx','dy'}, dimensions={0} | all-to-all | bytes 524288 | tf_op jit(solution)/shard_map/all_to_all | solution.py:76
  314.9 0.7 copy.74
  (46 shorter events, 0.7 us)
Async XLA Ops:
  3.4 114.8 %copy-start.2 = (s32[1,4,1024]{2,1,0:T(4,128)S(1)}, s32[1,4,1024]{2,1,0:T(4,128)}, u32[]{:S(2)}) copy-start(s32[1,4,1024]{2,1,0:T(4,128)} %param.15) | copy-start | bytes 49156
  138.7 18.2 %collective-permute-start = (bf16[1024,256]{1,0:T(8,128)(2,1)}, bf16[1024,256]{1,0:T(8,128)(2,1)}, u32[]{:S(2)}, u32[]{:S(2)}) collective-permute-start(bf16[1024,256]{1,0:T(8,128)(2,1)} %get-tuple-element.86), channel_id=1, source_target_pairs={{24,0},{0,8},{8,16},{16,24},{25,1},{1,9},{9,17},{17,25},{26,2},{2,... | collective-permute-start | bytes 1572872 | tf_op jit(solution)/shard_map/ppermute | solution.py:12
  141.7 24.9 %collective-permute-start.1 = (bf16[1024,256]{1,0:T(8,128)(2,1)}, bf16[1024,256]{1,0:T(8,128)(2,1)}, u32[]{:S(2)}, u32[]{:S(2)}) collective-permute-start(bf16[1024,256]{1,0:T(8,128)(2,1)} %get-tuple-element.85), channel_id=1, source_target_pairs={{8,0},{16,8},{24,16},{0,24},{9,1},{17,9},{25,17},{1,25},{10,2},{18... | collective-permute-start | bytes 1572872 | tf_op jit(solution)/shard_map/ppermute | solution.py:12
  143.7 24.8 %collective-permute-start.2 = (bf16[1024,256]{1,0:T(8,128)(2,1)}, bf16[1024,256]{1,0:T(8,128)(2,1)S(1)}, u32[]{:S(2)}, u32[]{:S(2)}) collective-permute-start(bf16[1024,256]{1,0:T(8,128)(2,1)} %get-tuple-element.84), channel_id=1, source_target_pairs={{7,0},{0,1},{1,2},{2,3},{3,4},{4,5},{5,6},{6,7},{15,8},{8,9},{9,10... | collective-permute-start | bytes 1572872 | tf_op jit(solution)/shard_map/ppermute | solution.py:12
  143.7 4.4 %copy-start = (s32[6,4096]{1,0:T(8,128)S(1)}, s32[6,4096]{1,0:T(8,128)}, u32[]{:S(2)}) copy-start(s32[6,4096]{1,0:T(8,128)} %param.16) | copy-start | bytes 294916
  143.7 4.6 %copy-start.1 = (f32[6,4096]{1,0:T(8,128)S(1)}, f32[6,4096]{1,0:T(8,128)}, u32[]{:S(2)}) copy-start(f32[6,4096]{1,0:T(8,128)} %param.17) | copy-start | bytes 294916
  143.8 4.7 %copy-start.3 = (s32[32,16]{0,1:T(8,128)S(1)}, s32[32,16]{0,1:T(8,128)}, u32[]{:S(2)}) copy-start(s32[32,16]{0,1:T(8,128)} %param.18) | copy-start | bytes 6148
  143.8 4.7 %copy-start.4 = (s32[1,32]{1,0:T(1,128)S(1)}, s32[1,32]{1,0:T(1,128)}, u32[]{:S(2)}) copy-start(s32[1,32]{1,0:T(1,128)} %param.19) | copy-start | bytes 388
  143.8 25.6 %collective-permute-start.3 = (bf16[1024,256]{1,0:T(8,128)(2,1)}, bf16[1024,256]{1,0:T(8,128)(2,1)S(1)}, u32[]{:S(2)}, u32[]{:S(2)}) collective-permute-start(bf16[1024,256]{1,0:T(8,128)(2,1)} %get-tuple-element.83), channel_id=1, source_target_pairs={{1,0},{2,1},{3,2},{4,3},{5,4},{6,5},{7,6},{0,7},{9,8},{10,9},{11,1... | collective-permute-start | bytes 1572872 | tf_op jit(solution)/shard_map/ppermute | solution.py:12
where the time goes:
time: 318 us; the launch traced here: 316 us
  local copies, waits for them, and re-layouts  174 us (55%)
  matrix products  84.4 us (27%)
  blocking collectives  16.8 us (5%)
  waiting for transfers between devices  16 us (5%)
  other arithmetic  15.4 us (5%)
  starting transfers between devices  7.91 us (2%)
    gather x6, local copies, waits for them, and re-layouts, body(): neighbour = jnp.take(extended, faces[face], axis=0).astype(jnp.float32)  112 us
    dot_general x12, matrix products, run_block(): jnp.einsum('rskb,ksbc->rsc', spread, kernels, preferred_element_type=jnp....  84.4 us
    gather x1, local copies, waits for them, and re-layouts, body(): jnp.take(coag, export_rows.reshape(4 * export_count), axis=0)  17 us
    all_to_all x1, blocking collectives, body(): lax.all_to_all(leaving, ('dx', 'dy'), split_axis=0, concat_axis=0, tiled=...  16.8 us
    convert_element_type x10, local copies, waits for them, and re-layouts, run_block(): operand = grain_state.astype(jnp.bfloat16)  16.2 us
    ppermute x4, waiting for transfers between devices, passed_along(): return lax.ppermute(block, axis, route)  16 us
    convert_element_type x1, other arithmetic, body(): updated = flux_sum.astype(jnp.bfloat16)  12.3 us
    unnamed x18, local copies, waits for them, and re-layouts  8.95 us
  transfers between devices with their start and end apart: 4, of which 2 were waited for; matrix products, arithmetic and copies ran while one was open for 2% of the time, Pallas kernels for 0%

commit v1 on v0

v1 whole, which is shorter than its diff:
```python
import functools

import jax
import jax.numpy as jnp
from jax import lax
from jax.experimental import pallas as pl
from jax.experimental.pallas import tpu as pltpu
from jax.sharding import PartitionSpec as P

SUBSTEPS = 6
LANES = 128
GROUP = 8
TILE = 128
TOGETHER = 4
CHUNK = 16
F32 = jnp.float32
BF16 = jnp.bfloat16
I32 = jnp.int32
MIB = 1 << 20


def passed_along(block, axis, distance):
    devices = range(lax.axis_size(axis))
    route = [((i - distance) % len(devices), i) for i in devices]
    return lax.ppermute(block, axis, route)


def iota2(shape, dim):
    return lax.broadcasted_iota(I32, shape, dim)


def dot(a, b):
    return jnp.dot(a, b, preferred_element_type=F32)


def rows2(start):
    return pl.ds(pl.multiple_of(start, 2), 2)


def spread_rows(src, table, first, count):
    step = 64

    def one(i, carry):
        block = src[pl.ds(pl.multiple_of(i * step, step), step), :].astype(F32)
        at = 2 * first + i * (2 * step)
        table[pl.ds(pl.multiple_of(at, 8), step, stride=2), :] = block[:, :LANES]
        table[pl.ds(at + 1, step, stride=2), :] = block[:, LANES:]
        return carry

    lax.fori_loop(0, count // step, one, 0)


def class_places(cls, class_count, tile):
    rows = cls.shape[0]
    shift = rows.bit_length() - 1
    wide = class_count * rows
    member = jnp.concatenate([(cls == c).astype(F32) for c in range(class_count)], axis=0)
    member16 = member.astype(BF16)
    before = (iota2((LANES, LANES), 0) < iota2((LANES, LANES), 1)).astype(F32).astype(BF16)
    in_row = dot(member16, before)
    row_total = dot(member16, jnp.ones((LANES, LANES), BF16)).astype(BF16)
    a, b = iota2((wide, wide), 0), iota2((wide, wide), 1)
    same = (a >> shift) == (b >> shift)
    earlier_rows = jnp.logical_and(same, b < a).astype(F32).astype(BF16)
    row_start = dot(earlier_rows, row_total)
    class_total = dot(same.astype(F32).astype(BF16), row_total)
    tiles = ((class_total.astype(I32) + (tile - 1)) >> (tile.bit_length() - 1)).astype(F32)
    earlier = jnp.logical_and((b >> shift) < (a >> shift), (b & (rows - 1)) == 0)
    first_tile = dot(earlier.astype(F32).astype(BF16), tiles.astype(BF16))
    place = member * (first_tile * float(tile) + row_start + in_row)
    total = place[:rows]
    for c in range(1, class_count):
        total = total + place[c * rows:(c + 1) * rows]
    last_tile = (first_tile + tiles).astype(I32)
    lane = iota2((8, LANES), 1)
    tile_class = jnp.zeros((8, LANES), I32)
    for c in range(class_count - 1):
        tile_class = tile_class + (last_tile[c * rows:c * rows + 8] <= lane).astype(I32)
    tile_count = last_tile[wide - 8:]
    return (2.0 * total).astype(I32), tile_class, tile_count


def substeps(state, weights, averager):
    for _ in range(SUBSTEPS):
        operand = state.astype(BF16)
        product = dot(operand, weights)
        mean_square = dot(operand * operand, averager)
        share = pl.reciprocal(1.0 + mean_square, approx=True)
        state = state + product * (1.0 - share)
    return state


def own_kernel(cells, cls_ref, step_ref, exp_ref, dust, kern, out, outbound, table, sorted_rows, weights, averager,
               places_v, places, stage, sem):
    class_count = kern.shape[0]
    rows = cells // LANES
    place, tile_class, tile_count = class_places(cls_ref[...], class_count, TILE)
    places_v[0:rows, :] = place
    places_v[rows:rows + 8, :] = tile_class
    places_v[rows + 8:rows + 16, :] = tile_count
    copy = pltpu.make_async_copy(places_v, places, sem)
    copy.start()
    spread_rows(dust, table, 0, cells)
    zero = jnp.zeros((LANES, LANES), BF16)
    mean = jnp.full((LANES, LANES), 1.0 / LANES, BF16)
    for s in range(2):
        averager[s * LANES:(s + 1) * LANES, s * LANES:(s + 1) * LANES] = mean
        averager[s * LANES:(s + 1) * LANES, (1 - s) * LANES:(2 - s) * LANES] = zero
    for c in range(class_count):
        for s in range(2):
            weights[c, s * LANES:(s + 1) * LANES, s * LANES:(s + 1) * LANES] = kern[c, s]
            weights[c, s * LANES:(s + 1) * LANES, (1 - s) * LANES:(2 - s) * LANES] = zero
    steps = [step_ref[k] for k in range(GROUP)]
    copy.wait()

    def scatter(r, carry):
        for j in range(LANES // GROUP):
            group = places.at[r, pl.ds(j * GROUP, GROUP)]
            for k in range(GROUP):
                at = (r * LANES + j * GROUP + k) * 2
                sorted_rows[rows2(group[steps[k]]), :] = table[rows2(at), :]
        return carry

    lax.fori_loop(0, rows, scatter, 0)
    total_tiles = places[rows + 8, 0]

    def tiles(i, carry):
        states, firsts = [], []
        for m in range(TOGETHER):
            first = (i * TOGETHER + m) * (2 * TILE)
            one = sorted_rows[pl.ds(pl.multiple_of(first, 8), TILE, stride=2), :]
            two = sorted_rows[pl.ds(first + 1, TILE, stride=2), :]
            states.append(jnp.concatenate([one, two], axis=1))
            firsts.append(first)
        mats = [weights[jnp.minimum(places[rows, i * TOGETHER + m], class_count - 1)] for m in range(TOGETHER)]
        avg = averager[...]
        for m in range(TOGETHER):
            done = substeps(states[m], mats[m], avg).astype(BF16).astype(F32)
            sorted_rows[pl.ds(pl.multiple_of(firsts[m], 8), TILE, stride=2), :] = done[:, :LANES]
            sorted_rows[pl.ds(firsts[m] + 1, TILE, stride=2), :] = done[:, LANES:]
        return carry

    lax.fori_loop(0, (total_tiles + (TOGETHER - 1)) // TOGETHER, tiles, 0)

    def gather(r, carry):
        for j in range(LANES // GROUP):
            group = places.at[r, pl.ds(j * GROUP, GROUP)]
            for k in range(GROUP):
                at = (r * LANES + j * GROUP + k) * 2
                out[rows2(at), :] = sorted_rows[rows2(group[steps[k]]), :]
        return carry

    lax.fori_loop(0, rows, gather, 0)
    export = outbound.shape[0]
    span = 64

    def send(i, carry):
        for j in range(span // GROUP):
            group = exp_ref.at[pl.ds(i * span + j * GROUP, GROUP)]
            for k in range(GROUP):
                stage[rows2((j * GROUP + k) * 2), :] = out[rows2(group[steps[k]]), :]
        at = pl.ds(pl.multiple_of(i * span, span), span)
        outbound[at, 0:LANES] = stage[pl.ds(0, span, stride=2), :].astype(BF16)
        outbound[at, LANES:2 * LANES] = stage[pl.ds(1, span, stride=2), :].astype(BF16)
        return carry

    lax.fori_loop(0, export // span, send, 0)


def vmem():
    return pl.BlockSpec(memory_space=pltpu.VMEM)


def smem():
    return pl.BlockSpec(memory_space=pltpu.SMEM)


def own_cells(dust, classes, kernels, export2, steps):
    cells = dust.shape[0]
    rows = cells // LANES
    class_count = kernels.shape[0]
    most = (cells // TILE + class_count + TOGETHER - 1) // TOGETHER * TOGETHER
    return pl.pallas_call(
        functools.partial(own_kernel, cells),
        out_shape=(
            jax.ShapeDtypeStruct((2 * cells, LANES), F32),
            jax.ShapeDtypeStruct((export2.shape[0], 2 * LANES), BF16),
        ),
        in_specs=[vmem(), smem(), smem(), vmem(), vmem()],
        out_specs=(vmem(), vmem()),
        scratch_shapes=[
            pltpu.VMEM((2 * cells, LANES), F32),
            pltpu.VMEM((2 * most * TILE, LANES), F32),
            pltpu.VMEM((class_count, 2 * LANES, 2 * LANES), BF16),
            pltpu.VMEM((2 * LANES, 2 * LANES), BF16),
            pltpu.VMEM((rows + 16, LANES), I32),
            pltpu.SMEM((rows + 16, LANES), I32),
            pltpu.VMEM((128, LANES), F32),
            pltpu.SemaphoreType.DMA,
        ],
        compiler_params=pltpu.CompilerParams(vmem_limit_bytes=40 * MIB),
        cost_estimate=pl.CostEstimate(flops=9_000_000_000, bytes_accessed=12 * MIB, transcendentals=0),
        name="coagulate_own",
    )(classes.reshape(rows, LANES), steps, export2, dust, kernels)


def fill_table(own, ghosts, table, sem):
    cells2 = own.shape[0]
    copy = pltpu.make_async_copy(own, table.at[pl.ds(0, cells2)], sem)
    copy.start()
    first = cells2 // 2
    for ghost in ghosts:
        spread_rows(ghost, table, first, ghost.shape[0])
        first = first + ghost.shape[0]
    copy.wait()


def diffused(own1, own2, coef, stage, face_count):
    one, two = own1, own2
    for f in range(face_count):
        c = jnp.broadcast_to(coef[:, f:f + 1], (CHUNK, LANES))
        one = one + c * (stage[pl.ds(2 * f * CHUNK, CHUNK, stride=2), :] - own1)
        two = two + c * (stage[pl.ds(2 * f * CHUNK + 1, CHUNK, stride=2), :] - own2)
    return one.astype(BF16), two.astype(BF16)


def mig_kernel(face_count, cells, faces, mig, own, g0, g1, g2, g3, coef, out, table, stage, own_stage, coef_stage, sem):
    fill_table(own, (g0, g1, g2, g3), table, sem)

    def chunk(i, carry):
        for u in range(CHUNK):
            c = mig[i * CHUNK + u]
            own_stage[rows2(2 * u), :] = table[rows2(2 * c), :]
            coef_stage[pl.ds(u, 1), :] = coef[pl.ds(c, 1), :]
            for f in range(face_count):
                row = faces.at[pl.ds(f * cells, cells)][c]
                stage[rows2((f * CHUNK + u) * 2), :] = table[rows2(row), :]
        one, two = diffused(own_stage[pl.ds(0, CHUNK, stride=2), :], own_stage[pl.ds(1, CHUNK, stride=2), :],
                            coef_stage[...], stage, face_count)
        at = pl.ds(pl.multiple_of(i * CHUNK, CHUNK), CHUNK)
        out[at, 0:LANES] = one
        out[at, LANES:2 * LANES] = two
        return carry

    lax.fori_loop(0, out.shape[0] // CHUNK, chunk, 0)


def all_kernel(face_count, cells, faces, steps_ref, own, g0, g1, g2, g3, coef, out, table, stage_a, stage_b, sem):
    fill_table(own, (g0, g1, g2, g3), table, sem)
    steps = [steps_ref[k] for k in range(GROUP)]

    def pull(i, stage):
        for f in range(face_count):
            for j in range(CHUNK // GROUP):
                group = faces.at[pl.ds(i * CHUNK + (f * cells + j * GROUP), GROUP)]
                for k in range(GROUP):
                    stage[rows2((f * CHUNK + j * GROUP + k) * 2), :] = table[rows2(group[steps[k]]), :]

    def push(i, stage):
        first = i * (2 * CHUNK)
        one, two = diffused(
            table[pl.ds(pl.multiple_of(first, 8), CHUNK, stride=2), :],
            table[pl.ds(first + 1, CHUNK, stride=2), :],
            coef[pl.ds(pl.multiple_of(i * CHUNK, CHUNK), CHUNK), :], stage, face_count)
        at = pl.ds(pl.multiple_of(i * CHUNK, CHUNK), CHUNK)
        out[at, 0:LANES] = one
        out[at, LANES:2 * LANES] = two

    pull(0, stage_a)
    chunks = cells // CHUNK

    def pair(i, carry):
        push(2 * i, stage_a)
        pull(2 * i + 1, stage_b)
        push(2 * i + 1, stage_b)
        pull(jnp.minimum(2 * i + 2, chunks - 1), stage_a)
        return carry

    lax.fori_loop(0, chunks // 2, pair, 0)


def diffuse_leaving(faces2, mig, own, ghosts, coef, face_count):
    cells = own.shape[0] // 2
    ghost_rows = sum(g.shape[0] for g in ghosts)
    return pl.pallas_call(
        functools.partial(mig_kernel, face_count, cells),
        out_shape=jax.ShapeDtypeStruct((mig.shape[0], 2 * LANES), BF16),
        in_specs=[smem(), smem(), pl.BlockSpec(memory_space=pl.ANY)] + [vmem()] * 5,
        out_specs=vmem(),
        scratch_shapes=[
            pltpu.VMEM((2 * (cells + ghost_rows), LANES), F32),
            pltpu.VMEM((2 * face_count * CHUNK, LANES), F32),
            pltpu.VMEM((2 * CHUNK, LANES), F32),
            pltpu.VMEM((CHUNK, face_count), F32),
            pltpu.SemaphoreType.DMA,
        ],
        compiler_params=pltpu.CompilerParams(vmem_limit_bytes=30 * MIB),
        cost_estimate=pl.CostEstimate(flops=500_000_000, bytes_accessed=8 * MIB, transcendentals=0),
        name="diffuse_leaving",
    )(faces2, mig, own, *ghosts, coef)


def diffuse_all(faces2, steps, own, ghosts, coef, face_count):
    cells = own.shape[0] // 2
    ghost_rows = sum(g.shape[0] for g in ghosts)
    return pl.pallas_call(
        functools.partial(all_kernel, face_count, cells),
        out_shape=jax.ShapeDtypeStruct((cells, 2 * LANES), BF16),
        in_specs=[smem(), smem(), pl.BlockSpec(memory_space=pl.ANY)] + [vmem()] * 5,
        out_specs=vmem(),
        scratch_shapes=[
            pltpu.VMEM((2 * (cells + ghost_rows), LANES), F32),
            pltpu.VMEM((2 * face_count * CHUNK, LANES), F32),
            pltpu.VMEM((2 * face_count * CHUNK, LANES), F32),
            pltpu.SemaphoreType.DMA,
        ],
        compiler_params=pltpu.CompilerParams(vmem_limit_bytes=30 * MIB),
        cost_estimate=pl.CostEstimate(flops=10_000_000_000, bytes_accessed=30 * MIB, transcendentals=0),
        name="diffuse_all",
    )(faces2, steps, own, *ghosts, coef)


def body(dust, classes, kernels, export_ids, faces, face_coef, mig_ids, mig_counts):
    row_width = dust.shape[1]
    face_count = faces.shape[0]
    export_count = export_ids.shape[2]
    steps = jnp.arange(GROUP, dtype=I32)
    export2 = (export_ids * 2).reshape(4 * export_count)
    own, outbound = own_cells(dust, classes, kernels, export2, steps)
    blocks = outbound.reshape(4, export_count, row_width)
    ghosts = []
    for direction, offset in ((0, 1), (1, -1)):
        ghosts.append(passed_along(blocks[direction], "dx", offset))
    for direction, offset in ((2, 1), (3, -1)):
        ghosts.append(passed_along(blocks[direction], "dy", offset))
    faces2 = (faces * 2).reshape(-1)
    coef = face_coef.T
    domains = mig_counts.shape[1]
    capacity = mig_ids.shape[1]
    picked = diffuse_leaving(faces2, mig_ids.reshape(-1), own, ghosts, coef, face_count)
    filled = jnp.arange(capacity, dtype=I32)[None, :] < mig_counts[0][:, None]
    picked = picked.reshape(domains, capacity, row_width)
    leaving = jnp.where(filled[:, :, None], picked, jnp.zeros_like(picked))
    arrived = lax.all_to_all(leaving, ("dx", "dy"), split_axis=0, concat_axis=0, tiled=True)
    updated = diffuse_all(faces2, steps, own, ghosts, coef, face_count)
    return (updated, arrived.reshape(domains * capacity, row_width))


def solution(mesh):
    return jax.shard_map(
        body,
        mesh=mesh,
        in_specs=(
            P(("dx", "dy"), None),
            P(("dx", "dy")),
            P(),
            P(("dx", "dy"), None, None),
            P(None, ("dx", "dy")),
            P(None, ("dx", "dy")),
            P(("dx", "dy"), None),
            P(("dx", "dy"), None),
        ),
        out_specs=(P(("dx", "dy"), None), P(("dx", "dy"), None)),
        check_vma=False,
    )
```

time: 318 us -> 117 us (0.37)
  local copies, waits for them, and re-layouts: 174 us -> 11.8 us
  matrix products: 84.4 us -> 0 us
  Pallas kernels: 0 us -> 68.7 us
  blocking collectives: 16.8 us -> 0 us
  other arithmetic: 15.4 us -> 1.65 us
  starting transfers between devices: 7.91 us -> 14.2 us
  waiting for transfers between devices: 16 us -> 19.2 us
    gather x8 -> x0, local copies, waits for them, and re-layouts: 132 us -> none  [the longest x6 112 us: body(): neighbour = jnp.take(extended, faces[face], axis=0).astype(jnp.float32)]
    dot_general x12 -> x0, matrix products: 84.4 us -> none  [run_block(): jnp.einsum('rskb,ksbc->rsc', spread, kernels, preferred_element_type=jnp....]
    pallas_call x0 -> x3, Pallas kernels: none -> 68.7 us  [the longest x1 40.4 us: own_cells(): pl.pallas_call(functools.partial(own_kernel, cells), out_shape=(jax.Shape...]
    all_to_all x1 -> x0, blocking collectives: 16.8 us -> none  [body(): lax.all_to_all(leaving, ('dx', 'dy'), split_axis=0, concat_axis=0, tiled=...]
    convert_element_type x10 -> x0, local copies, waits for them, and re-layouts: 16.2 us -> none  [run_block(): operand = grain_state.astype(jnp.bfloat16)]
    convert_element_type x3 -> x0, other arithmetic: 12.3 us -> none  [the longest x1 12.3 us: body(): updated = flux_sum.astype(jnp.bfloat16)]
    dynamic_slice x6 -> x0, local copies, waits for them, and re-layouts: 7.52 us -> none  [coagulate(): lax.map(run_block, (dust_rows.reshape(block_count, block_rows, species *...]
    all_to_all x0 -> x1, starting transfers between devices: none -> 6.53 us  [body(): lax.all_to_all(leaving, ('dx', 'dy'), split_axis=0, concat_axis=0, tiled=...]
  transfers between devices with their start and end apart: 4 -> 5, of which waited for: 2 -> 2; matrix products, arithmetic and copies ran while one was open for 2% -> 1% of each run, Pallas kernels for 0% -> 19%
where the time goes in v1:
time: 117 us; the launch traced here: 116 us
  Pallas kernels  68.7 us (59%)
  waiting for transfers between devices  19.2 us (16%)
  starting transfers between devices  14.2 us (12%)
  local copies, waits for them, and re-layouts  11.8 us (10%)
  other arithmetic  1.65 us (1%)
    pallas_call x1, Pallas kernels, own_cells(): pl.pallas_call(functools.partial(own_kernel, cells), out_shape=(jax.Shape...  40.4 us
    pallas_call x1, Pallas kernels, diffuse_all(): pl.pallas_call(functools.partial(all_kernel, face_count, cells), out_shap...  22.1 us
    ppermute x4, waiting for transfers between devices, passed_along(): return lax.ppermute(block, axis, route)  19.2 us
    unnamed x24, local copies, waits for them, and re-layouts  10.4 us
    ppermute x4, starting transfers between devices, passed_along(): return lax.ppermute(block, axis, route)  7.7 us
    all_to_all x1, starting transfers between devices, body(): lax.all_to_all(leaving, ('dx', 'dy'), split_axis=0, concat_axis=0, tiled=...  6.53 us
    pallas_call x1, Pallas kernels, diffuse_leaving(): pl.pallas_call(functools.partial(mig_kernel, face_count, cells), out_shap...  6.23 us
  transfers between devices with their start and end apart: 5, of which 2 were waited for; matrix products, arithmetic and copies ran while one was open for 1% of the time, Pallas kernels for 19%

profile of v1, /device:TPU:0, one launch (start us, length us, event | category | flops | bytes accessed | tf_op | source)
XLA Modules:
  0.0 116.4 jit_solution(3598862395163138353)
XLA Ops:
  0.6 0.7 multiply_bitcast_fusion
  1.4 0.0 copy-start.3
  1.4 1.6 %copy-done.3 = bf16[4096,256]{1,0:T(8,128)(2,1)S(1)} copy-done((bf16[4096,256]{1,0:T(8,128)(2,1)S(1)}, bf16[4096,256]{1,0:T(8,128)(2,1)}, u32[]{:S(2)}) %copy-start.3) | copy-done | bytes 2097176
  3.0 0.0 copy-start.4
  3.0 1.0 copy-done.4
  4.0 0.0 copy-start.5
  4.0 0.7 copy-done.5
  4.7 40.4 %coagulate_own.1 = (f32[8192,128]{1,0:T(8,128)S(1)}, bf16[4096,256]{1,0:T(8,128)(2,1)S(1)}) custom-call(s32[32,128]{1,0:T(8,128)S(1)} %bitcast.14, s32[8]{0:T(128)S(1)} %iota.13.step_ref, s32[4096]{0:T(1024)S(1)} %bitcast.13, bf16[4096,256]{1,0:T(8,128)(2,1)S(1)} %copy-done.3, bf16[8,2,128,128]{3,2,1,0:T(8,128)(2,1)S(1)} %copy-done.4), custom_call_target="tpu_custom_call" | custom-call | flops 8999999488 | bytes 12582912 | tf_op jit(solution)/shard_map/coagulate_own/pallas_call | solution.py:183
  45.1 0.0 copy-start
  45.1 0.0 copy-start.7
  45.1 0.0 copy-start.6
  45.1 1.3 %fusion = (bf16[1024,256]{1,0:T(8,128)(2,1)}, bf16[1024,256]{1,0:T(8,128)(2,1)}, bf16[1024,256]{1,0:T(8,128)(2,1)}, bf16[1024,256]{1,0:T(8,128)(2,1)}) fusion(bf16[4096,256]{1,0:T(8,128)(2,1)S(1)} %get-tuple-element.5), kind=kLoop, calls=%fused_computation.5 | loop fusion | bytes 4194304 | tf_op jit(solution)/shard_map/slice | solution.py:335
  46.4 1.2 %copy-done = f32[8192,128]{1,0:T(8,128)} copy-done((f32[8192,128]{1,0:T(8,128)}, f32[8192,128]{1,0:T(8,128)S(1)}, u32[]{:S(2)}) %copy-start) | copy-done | bytes 4194328
  47.7 0.0 copy-start.8
  47.7 0.0 copy-start.9
  47.7 3.0 %collective-permute-start = (bf16[1024,256]{1,0:T(8,128)(2,1)}, bf16[1024,256]{1,0:T(8,128)(2,1)S(1)}, u32[]{:S(2)}, u32[]{:S(2)}) collective-permute-start(bf16[1024,256]{1,0:T(8,128)(2,1)} %get-tuple-element.9), channel_id=1, source_target_pairs={{24,0},{0,8},{8,16},{16,24},{25,1},{1,9},{9,17},{17,25},{26,2},{2,... | collective-permute-start | bytes 1572872 | tf_op jit(solution)/shard_map/ppermute | solution.py:25
  50.7 2.0 %collective-permute-start.1 = (bf16[1024,256]{1,0:T(8,128)(2,1)}, bf16[1024,256]{1,0:T(8,128)(2,1)S(1)}, u32[]{:S(2)}, u32[]{:S(2)}) collective-permute-start(bf16[1024,256]{1,0:T(8,128)(2,1)} %get-tuple-element.8), channel_id=1, source_target_pairs={{8,0},{16,8},{24,16},{0,24},{9,1},{17,9},{25,17},{1,25},{10,2},{18... | collective-permute-start | bytes 1572872 | tf_op jit(solution)/shard_map/ppermute | solution.py:25
  52.7 0.0 collective-permute-start.2
  52.7 2.6 %collective-permute-start.3 = (bf16[1024,256]{1,0:T(8,128)(2,1)}, bf16[1024,256]{1,0:T(8,128)(2,1)}, u32[]{:S(2)}, u32[]{:S(2)}) collective-permute-start(bf16[1024,256]{1,0:T(8,128)(2,1)} %get-tuple-element.6), channel_id=1, source_target_pairs={{1,0},{2,1},{3,2},{4,3},{5,4},{6,5},{7,6},{0,7},{9,8},{10,9},{11,1... | collective-permute-start | bytes 1572872 | tf_op jit(solution)/shard_map/ppermute | solution.py:25
  55.4 0.0 copy-done.7
  55.4 0.0 copy-done.6
  55.4 0.6 copy.11
  56.0 0.1 reshape.55.faces
  56.1 0.0 copy-done.8
  56.1 0.1 copy.12
  56.2 0.1 reshape.58.mig
  56.3 0.0 copy-done.9
  56.3 0.1 iota_compare_fusion
  56.4 9.4 %collective-permute-done.g0 = bf16[1024,256]{1,0:T(8,128)(2,1)S(1)} collective-permute-done((bf16[1024,256]{1,0:T(8,128)(2,1)}, bf16[1024,256]{1,0:T(8,128)(2,1)S(1)}, u32[]{:S(2)}, u32[]{:S(2)}) %collective-permute-start) | collective-permute-done | bytes 524320 | tf_op jit(solution)/shard_map/ppermute | solution.py:25
  65.7 9.8 %collective-permute-done.1.g1 = bf16[1024,256]{1,0:T(8,128)(2,1)S(1)} collective-permute-done((bf16[1024,256]{1,0:T(8,128)(2,1)}, bf16[1024,256]{1,0:T(8,128)(2,1)S(1)}, u32[]{:S(2)}, u32[]{:S(2)}) %collective-permute-start.1) | collective-permute-done | bytes 524320 | tf_op jit(solution)/shard_map/ppermute | solution.py:25
  75.5 0.0 collective-permute-done.2.g2
  75.5 0.0 collective-permute-done.3.g3
  75.5 0.0 copy-start.1
  75.5 2.2 %copy-done.1 = f32[8192,128]{1,0:T(8,128)S(1)} copy-done((f32[8192,128]{1,0:T(8,128)S(1)}, f32[8192,128]{1,0:T(8,128)}, u32[]{:S(2)}) %copy-start.1) | copy-done | bytes 4194328
  77.7 6.2 %diffuse_leaving.1 = bf16[512,256]{1,0:T(8,128)(2,1)S(1)} custom-call(s32[24576]{0:T(1024)S(1)} %reshape.55.faces, s32[512]{0:T(512)S(1)} %reshape.58.mig, f32[8192,128]{1,0:T(8,128)S(1)} %copy-done.1, bf16[1024,256]{1,0:T(8,128)(2,1)S(1)} %collective-permute-done.g0, bf16[1024,256]{1,0:T(8,128)(2,1)S(1)} %collective-permute-done.1.g1, ...), custom_call_target="tpu_custom_call" | custom-call | flops 500000000 | bytes 8388608 | tf_op jit(solution)/shard_map/diffuse_leaving/pallas_call | solution.py:285
  84.0 0.8 broadcast_select_fusion
  84.8 6.5 %all-to-all-start = ((bf16[32,16,256]{2,1,0:T(8,128)(2,1)}), bf16[32,16,256]{2,1,0:T(8,128)(2,1)S(1)}, u32[]{:S(2)}, u32[]{:S(2)}) async-start(bf16[32,16,256]{2,1,0:T(8,128)(2,1)} %broadcast_select_fusion), calls=%async_computation | async-start | bytes 524288 | tf_op jit(solution)/shard_map/all_to_all | solution.py:344
  91.3 0.0 copy-start.2
  91.4 2.2 %copy-done.2 = f32[8192,128]{1,0:T(8,128)S(1)} copy-done((f32[8192,128]{1,0:T(8,128)S(1)}, f32[8192,128]{1,0:T(8,128)}, u32[]{:S(2)}) %copy-start.2) | copy-done | bytes 4194328
  93.5 22.1 %diffuse_all.1 = bf16[4096,256]{1,0:T(8,128)(2,1)} custom-call(s32[24576]{0:T(1024)S(1)} %reshape.55.faces, s32[8]{0:T(128)S(1)} %iota.12.steps_ref, f32[8192,128]{1,0:T(8,128)S(1)} %copy-done.2, bf16[1024,256]{1,0:T(8,128)(2,1)S(1)} %collective-permute-done.g0, bf16[1024,256]{1,0:T(8,128)(2,1)S(1)} %collective-permute-done.1.g1, ...), custom_call_target="tpu_custom_call" | custom-call | flops 10000000000 | bytes 31457280 | tf_op jit(solution)/shard_map/diffuse_all/pallas_call | solution.py:306
  115.7 0.0 all-to-all-done
  115.7 0.7 copy.17
  (4 shorter events, 0.0 us)
Async XLA Ops:
  1.4 1.6 %copy-start.3 = (bf16[4096,256]{1,0:T(8,128)(2,1)S(1)}, bf16[4096,256]{1,0:T(8,128)(2,1)}, u32[]{:S(2)}) copy-start(bf16[4096,256]{1,0:T(8,128)(2,1)} %dust.1) | copy-start | bytes 6291460
  3.0 1.0 copy-start.4
  4.0 0.7 copy-start.5
  45.1 2.6 %copy-start = (f32[8192,128]{1,0:T(8,128)}, f32[8192,128]{1,0:T(8,128)S(1)}, u32[]{:S(2)}) copy-start(f32[8192,128]{1,0:T(8,128)S(1)} %get-tuple-element.4.own) | copy-start | bytes 12582916
  45.1 10.3 %copy-start.7 = (s32[6,4096]{1,0:T(8,128)S(1)}, s32[6,4096]{1,0:T(8,128)}, u32[]{:S(2)}) copy-start(s32[6,4096]{1,0:T(8,128)} %param.12) | copy-start | bytes 294916
  45.1 10.3 %copy-start.6 = (f32[6,4096]{1,0:T(8,128)S(1)}, f32[6,4096]{1,0:T(8,128)}, u32[]{:S(2)}) copy-start(f32[6,4096]{1,0:T(8,128)} %param.13) | copy-start | bytes 294916
  47.7 8.4 %copy-start.8 = (s32[32,16]{0,1:T(8,128)S(1)}, s32[32,16]{0,1:T(8,128)}, u32[]{:S(2)}) copy-start(s32[32,16]{0,1:T(8,128)} %param.14) | copy-start | bytes 6148
  47.7 8.6 %copy-start.9 = (s32[1,32]{1,0:T(1,128)S(1)}, s32[1,32]{1,0:T(1,128)}, u32[]{:S(2)}) copy-start(s32[1,32]{1,0:T(1,128)} %param.15) | copy-start | bytes 388
  47.7 18.1 %collective-permute-start = (bf16[1024,256]{1,0:T(8,128)(2,1)}, bf16[1024,256]{1,0:T(8,128)(2,1)S(1)}, u32[]{:S(2)}, u32[]{:S(2)}) collective-permute-start(bf16[1024,256]{1,0:T(8,128)(2,1)} %get-tuple-element.9), channel_id=1, source_target_pairs={{24,0},{0,8},{8,16},{16,24},{25,1},{1,9},{9,17},{17,25},{26,2},{2,... | collective-permute-start | bytes 1572872 | tf_op jit(solution)/shard_map/ppermute | solution.py:25
  50.7 24.8 %collective-permute-start.1 = (bf16[1024,256]{1,0:T(8,128)(2,1)}, bf16[1024,256]{1,0:T(8,128)(2,1)S(1)}, u32[]{:S(2)}, u32[]{:S(2)}) collective-permute-start(bf16[1024,256]{1,0:T(8,128)(2,1)} %get-tuple-element.8), channel_id=1, source_target_pairs={{8,0},{16,8},{24,16},{0,24},{9,1},{17,9},{25,17},{1,25},{10,2},{18... | collective-permute-start | bytes 1572872 | tf_op jit(solution)/shard_map/ppermute | solution.py:25
  52.7 22.8 %collective-permute-start.2 = (bf16[1024,256]{1,0:T(8,128)(2,1)}, bf16[1024,256]{1,0:T(8,128)(2,1)}, u32[]{:S(2)}, u32[]{:S(2)}) collective-permute-start(bf16[1024,256]{1,0:T(8,128)(2,1)} %get-tuple-element.7), channel_id=1, source_target_pairs={{7,0},{0,1},{1,2},{2,3},{3,4},{4,5},{5,6},{6,7},{15,8},{8,9},{9,10... | collective-permute-start | bytes 1572872 | tf_op jit(solution)/shard_map/ppermute | solution.py:25
  52.7 22.8 %collective-permute-start.3 = (bf16[1024,256]{1,0:T(8,128)(2,1)}, bf16[1024,256]{1,0:T(8,128)(2,1)}, u32[]{:S(2)}, u32[]{:S(2)}) collective-permute-start(bf16[1024,256]{1,0:T(8,128)(2,1)} %get-tuple-element.6), channel_id=1, source_target_pairs={{1,0},{2,1},{3,2},{4,3},{5,4},{6,5},{7,6},{0,7},{9,8},{10,9},{11,1... | collective-permute-start | bytes 1572872 | tf_op jit(solution)/shard_map/ppermute | solution.py:25
  75.5 2.2 %copy-start.1 = (f32[8192,128]{1,0:T(8,128)S(1)}, f32[8192,128]{1,0:T(8,128)}, u32[]{:S(2)}) copy-start(f32[8192,128]{1,0:T(8,128)} %copy-done) | copy-start | bytes 12582916
  84.8 30.9 %all-to-all-start = ((bf16[32,16,256]{2,1,0:T(8,128)(2,1)}), bf16[32,16,256]{2,1,0:T(8,128)(2,1)S(1)}, u32[]{:S(2)}, u32[]{:S(2)}) async-start(bf16[32,16,256]{2,1,0:T(8,128)(2,1)} %broadcast_select_fusion), calls=%async_computation | async-start | bytes 524288 | tf_op jit(solution)/shard_map/all_to_all | solution.py:344
  91.3 2.2 %copy-start.2 = (f32[8192,128]{1,0:T(8,128)S(1)}, f32[8192,128]{1,0:T(8,128)}, u32[]{:S(2)}) copy-start(f32[8192,128]{1,0:T(8,128)} %copy-done) | copy-start | bytes 12582916

commit v2 on v1

v2 whole, which is shorter than its diff:
```python
import functools

import jax
import jax.numpy as jnp
from jax import lax
from jax.experimental import pallas as pl
from jax.experimental.pallas import tpu as pltpu
from jax.sharding import PartitionSpec as P

SUBSTEPS = 6
LANES = 128
GROUP = 8
TILE = 576
CHUNK = 16
F32 = jnp.float32
BF16 = jnp.bfloat16
I32 = jnp.int32
MIB = 1 << 20
VMEM_MIB = 60


def passed_along(block, axis, distance):
    devices = range(lax.axis_size(axis))
    route = [((i - distance) % len(devices), i) for i in devices]
    return lax.ppermute(block, axis, route)


def iota2(shape, dim):
    return lax.broadcasted_iota(I32, shape, dim)


def small_numbers(none_negative):
    unit = jnp.minimum(none_negative, 0) + 1
    return [unit * k for k in range(GROUP)]


def lines_of(source, lines, times):
    per_row = source.shape[1] // LANES
    for r in range(source.shape[0]):
        for i in range(per_row):
            at = r * per_row + i
            lines[at:at + 1, :] = source[r:r + 1, i * LANES:(i + 1) * LANES] * times


def dot(a, b):
    return jnp.dot(a, b, preferred_element_type=F32)


def rows2(start):
    return pl.ds(pl.multiple_of(start, 2), 2)


def spread_rows(src, table, first, count):
    step = 256

    def one(i, carry):
        block = src[pl.ds(pl.multiple_of(i * step, step), step), :].astype(F32)
        at = 2 * first + i * (2 * step)
        table[pl.ds(pl.multiple_of(at, 8), step, stride=2), :] = block[:, :LANES]
        table[pl.ds(at + 1, step, stride=2), :] = block[:, LANES:]
        return carry

    lax.fori_loop(0, count // step, one, 0)


def class_places(cls, class_count, tile):
    rows = cls.shape[0]
    shift = rows.bit_length() - 1
    wide = class_count * rows
    member = jnp.concatenate([(cls == c).astype(F32) for c in range(class_count)], axis=0)
    member16 = member.astype(BF16)
    before = (iota2((LANES, LANES), 0) < iota2((LANES, LANES), 1)).astype(F32).astype(BF16)
    in_row = dot(member16, before)
    row_total = dot(member16, jnp.ones((LANES, LANES), BF16)).astype(BF16)
    a, b = iota2((wide, wide), 0), iota2((wide, wide), 1)
    same = (a >> shift) == (b >> shift)
    earlier_rows = jnp.logical_and(same, b < a).astype(F32).astype(BF16)
    row_start = dot(earlier_rows, row_total)
    class_total = dot(same.astype(F32).astype(BF16), row_total)
    tiles = ((class_total + (tile - 0.5)) * (1.0 / tile)).astype(I32).astype(F32)
    earlier = jnp.logical_and((b >> shift) < (a >> shift), (b & (rows - 1)) == 0)
    first_tile = dot(earlier.astype(F32).astype(BF16), tiles.astype(BF16))
    place = member * (first_tile * float(tile) + row_start + in_row)
    total = place[:rows]
    for c in range(1, class_count):
        total = total + place[c * rows:(c + 1) * rows]
    last_tile = (first_tile + tiles).astype(I32)
    lane = iota2((8, LANES), 1)
    tile_class = jnp.zeros((8, LANES), I32)
    for c in range(class_count - 1):
        tile_class = tile_class + (last_tile[c * rows:c * rows + 8] <= lane).astype(I32)
    tile_count = last_tile[wide - 8:]
    return (2.0 * total).astype(I32), tile_class, tile_count


def substeps(state, weights):
    one, two = state[:, :LANES], state[:, LANES:]
    bins = float(LANES)
    for _ in range(SUBSTEPS):
        operand = jnp.concatenate([one, two], axis=1).astype(BF16)
        square_one = jnp.sum(one * one, axis=1, keepdims=True)
        square_two = jnp.sum(two * two, axis=1, keepdims=True)
        product = dot(operand, weights)
        one = one + product[:, :LANES] * (1.0 / bins - pl.reciprocal(bins + square_one, approx=True))
        two = two + product[:, LANES:] * (1.0 / bins - pl.reciprocal(bins + square_two, approx=True))
    return one.astype(BF16), two.astype(BF16)


def send_rows(ids, line, steps, table, outbound, stages):
    span = stages[0].shape[0] // 2
    spans = outbound.shape[0] // span

    def pull(i, stage):
        for j in range(span // GROUP):
            group = ids.at[line + i, pl.ds(j * GROUP, GROUP)]
            for k in range(GROUP):
                stage[rows2((j * GROUP + k) * 2), :] = table[rows2(group[steps[k]]), :]

    def push(i, stage):
        at = pl.ds(pl.multiple_of(i * span, span), span)
        outbound[at, 0:LANES] = stage[pl.ds(0, span, stride=2), :].astype(BF16)
        outbound[at, LANES:2 * LANES] = stage[pl.ds(1, span, stride=2), :].astype(BF16)

    pull(0, stages[0])

    def pair(i, carry):
        push(2 * i, stages[0])
        pull(2 * i + 1, stages[1])
        push(2 * i + 1, stages[1])
        pull(jnp.minimum(2 * i + 2, spans - 1), stages[0])
        return carry

    lax.fori_loop(0, spans // 2, pair, 0)


def own_kernel(cells, cls_ref, exp_ref, dust_any, kern_any, out_any, out_up, out_down, out_left, out_right,
               out, dust, kern, sorted_rows, weights, places_v, places, exp_v, exp_s, stage_a, stage_b, sem, dust_sems, kern_sem, exp_sem):
    class_count = kern.shape[0]
    rows = cells // LANES
    parts = dust_sems.shape[0]
    part = cells // parts
    kern_copy = pltpu.make_async_copy(kern_any, kern, kern_sem)
    kern_copy.start()
    dust_copies = []
    for p in range(parts):
        at = pl.ds(p * part, part)
        dust_copies.append(pltpu.make_async_copy(dust_any.at[at], dust.at[at], dust_sems.at[p]))
        dust_copies[-1].start()
    export_lines = exp_ref.shape[2] // LANES
    lines_of(exp_ref.at[0], exp_v, 2)
    exp_copy = pltpu.make_async_copy(exp_v, exp_s, exp_sem)
    exp_copy.start()
    place, tile_class, tile_count = class_places(cls_ref[...], class_count, TILE)
    places_v[0:rows, :] = place
    places_v[rows:rows + 8, :] = tile_class
    places_v[rows + 8:rows + 16, :] = tile_count
    copy = pltpu.make_async_copy(places_v, places, sem)
    copy.start()
    zero = jnp.zeros((LANES, LANES), BF16)
    kern_copy.wait()
    for c in range(class_count):
        for s in range(2):
            own = kern[c, s].astype(F32) * float(LANES)
            weights[c, s * LANES:(s + 1) * LANES, s * LANES:(s + 1) * LANES] = own.astype(BF16)
            weights[c, s * LANES:(s + 1) * LANES, (1 - s) * LANES:(2 - s) * LANES] = zero
    for dust_copy in dust_copies:
        dust_copy.wait()
    copy.wait()
    exp_copy.wait()
    steps = small_numbers(places[0, 0])

    def widen(r, stage):
        block = dust[pl.ds(pl.multiple_of(r * LANES, LANES), LANES), :].astype(F32)
        stage[pl.ds(0, LANES, stride=2), :] = block[:, :LANES]
        stage[pl.ds(1, LANES, stride=2), :] = block[:, LANES:]

    def scatter(r, stage):
        for j in range(LANES // GROUP):
            group = places.at[r, pl.ds(j * GROUP, GROUP)]
            for k in range(GROUP):
                sorted_rows[rows2(group[steps[k]]), :] = stage[rows2((j * GROUP + k) * 2), :]

    widen(0, stage_a)

    def pair(i, carry):
        scatter(2 * i, stage_a)
        widen(2 * i + 1, stage_b)
        scatter(2 * i + 1, stage_b)
        widen(jnp.minimum(2 * i + 2, rows - 1), stage_a)
        return carry

    lax.fori_loop(0, rows // 2, pair, 0)

    def tile(i, carry):
        first = i * (2 * TILE)
        at_one = pl.ds(pl.multiple_of(first, 8), TILE, stride=2)
        at_two = pl.ds(first + 1, TILE, stride=2)
        state = jnp.concatenate([sorted_rows[at_one, :], sorted_rows[at_two, :]], axis=1)
        one, two = substeps(state, weights[places[rows, i]])
        sorted_rows[at_one, :] = one.astype(F32)
        sorted_rows[at_two, :] = two.astype(F32)
        return carry

    lax.fori_loop(0, places[rows + 8, 0], tile, 0)

    def gather(r, carry):
        for j in range(LANES // GROUP):
            group = places.at[r, pl.ds(j * GROUP, GROUP)]
            for k in range(GROUP):
                at = (r * LANES + j * GROUP + k) * 2
                out[rows2(at), :] = sorted_rows[rows2(group[steps[k]]), :]
        return carry

    lax.fori_loop(0, rows, gather, 0)
    out_copy = pltpu.make_async_copy(out, out_any, sem)
    out_copy.start()
    for k, block in enumerate((out_up, out_down, out_left, out_right)):
        send_rows(exp_s, k * export_lines, steps, out, block, (stage_a, stage_b))
    out_copy.wait()


def vmem():
    return pl.BlockSpec(memory_space=pltpu.VMEM)


def smem():
    return pl.BlockSpec(memory_space=pltpu.SMEM)


def hbm():
    return pl.BlockSpec(memory_space=pltpu.HBM)


def own_cells(dust, classes, kernels, export_ids):
    cells = dust.shape[0]
    export = export_ids.shape[2]
    rows = cells // LANES
    class_count = kernels.shape[0]
    most = cells // TILE + class_count
    block = jax.ShapeDtypeStruct((export, 2 * LANES), BF16)
    return pl.pallas_call(
        functools.partial(own_kernel, cells),
        out_shape=(jax.ShapeDtypeStruct((2 * cells, LANES), F32), block, block, block, block),
        in_specs=[vmem(), vmem(), hbm(), hbm()],
        out_specs=(hbm(), vmem(), vmem(), vmem(), vmem()),
        scratch_shapes=[
            pltpu.VMEM((2 * cells, LANES), F32),
            pltpu.VMEM((cells, 2 * LANES), BF16),
            pltpu.VMEM(kernels.shape, BF16),
            pltpu.VMEM((2 * most * TILE, LANES), F32),
            pltpu.VMEM((class_count, 2 * LANES, 2 * LANES), BF16),
            pltpu.VMEM((rows + 16, LANES), I32),
            pltpu.SMEM((rows + 16, LANES), I32),
            pltpu.VMEM((4 * export // LANES, LANES), I32),
            pltpu.SMEM((4 * export // LANES, LANES), I32),
            pltpu.VMEM((2 * LANES, LANES), F32),
            pltpu.VMEM((2 * LANES, LANES), F32),
            pltpu.SemaphoreType.DMA,
            pltpu.SemaphoreType.DMA((4,)),
            pltpu.SemaphoreType.DMA,
            pltpu.SemaphoreType.DMA,
        ],
        compiler_params=pltpu.CompilerParams(vmem_limit_bytes=VMEM_MIB * MIB),
        cost_estimate=pl.CostEstimate(flops=9_000_000_000, bytes_accessed=12 * MIB, transcendentals=0),
        name="coagulate_own",
    )(classes.reshape(rows, LANES), export_ids, dust, kernels)


def pairs(start):
    return pl.ds(pl.multiple_of(start, 8), CHUNK, stride=2), pl.ds(start + 1, CHUNK, stride=2)


def face_sums(own_one, own_two, weights, stage, face_count):
    one, two = own_one, own_two
    for f in range(face_count):
        c = jnp.broadcast_to(weights[:, f:f + 1], (CHUNK, LANES))
        one = one + c * (stage[pl.ds(2 * f * CHUNK, CHUNK, stride=2), :] - own_one)
        two = two + c * (stage[pl.ds(2 * f * CHUNK + 1, CHUNK, stride=2), :] - own_two)
    return one, two


def turn_columns(coef, coef8, columns):
    together = 4
    coef8[0:coef.shape[0], :] = coef[...]

    def turn(b, carry):
        for u in range(together):
            at = pl.ds(pl.multiple_of((b * together + u) * LANES, LANES), LANES)
            columns[at, :] = coef8[:, at].T
        return carry

    lax.fori_loop(0, columns.shape[0] // (LANES * together), turn, 0)


def start_faces(faces, faces_v, faces_s, sem):
    lines_of(faces, faces_v, 2)
    copy = pltpu.make_async_copy(faces_v, faces_s, sem)
    copy.start()
    return copy


def start_ghosts(ghosts, landed, sems):
    copies = []
    for k, ghost in enumerate(ghosts):
        copies.append(pltpu.make_async_copy(ghost, landed.at[k], sems.at[k]))
        copies[-1].start()
    return copies


def spread_ghosts(copies, landed, table, first):
    for k, copy in enumerate(copies):
        copy.wait()
        spread_rows(landed.at[k], table, first + k * landed.shape[1], landed.shape[1])


def early_kernel(face_count, cells, late_rows, faces, own, coef, out_any, out, table, stage_a, stage_b, coef8, columns,
                 faces_v, faces_s, sem, face_sem, out_sems):
    copy = pltpu.make_async_copy(own, table.at[pl.ds(0, 2 * cells)], sem)
    copy.start()
    face_copy = start_faces(faces, faces_v, faces_s, face_sem)

    def clear(i, carry):
        table[pl.ds(pl.multiple_of(2 * cells + i * 256, 256), 256), :] = jnp.zeros((256, LANES), F32)
        return carry

    lax.fori_loop(0, 2 * late_rows // 256, clear, 0)
    turn_columns(coef, coef8, columns)
    face_copy.wait()
    flat = faces_s.reshape(face_count * cells)
    steps = small_numbers(faces_s[0, 0])
    copy.wait()

    def pull(i, stage):
        for f in range(face_count):
            for j in range(CHUNK // GROUP):
                group = flat.at[pl.ds(i * CHUNK + (f * cells + j * GROUP), GROUP)]
                for k in range(GROUP):
                    stage[rows2((f * CHUNK + j * GROUP + k) * 2), :] = table[rows2(group[steps[k]]), :]

    def push(i, stage):
        at = pairs(i * (2 * CHUNK))
        weights = columns[pl.ds(pl.multiple_of(i * CHUNK, CHUNK), CHUNK), :]
        one, two = face_sums(table[at[0], :], table[at[1], :], weights, stage, face_count)
        out[at[0], :] = one
        out[at[1], :] = two

    pull(0, stage_a)
    chunks = cells // CHUNK

    def pair(i, carry):
        push(2 * i, stage_a)
        pull(2 * i + 1, stage_b)
        push(2 * i + 1, stage_b)
        pull(jnp.minimum(2 * i + 2, chunks - 1), stage_a)
        return carry

    parts = out_sems.shape[0]
    done = []
    for p in range(parts):
        lax.fori_loop(p * (chunks // 2 // parts), (p + 1) * (chunks // 2 // parts), pair, 0)
        at = pl.ds(p * (2 * cells // parts), 2 * cells // parts)
        done.append(pltpu.make_async_copy(out.at[at], out_any.at[at], out_sems.at[p]))
        done[-1].start()
    for part in done:
        part.wait()


def diffuse_early(faces, own, coef, late_rows):
    face_count, cells = coef.shape
    padded = face_count + -face_count % 8
    return pl.pallas_call(
        functools.partial(early_kernel, face_count, cells, late_rows),
        out_shape=jax.ShapeDtypeStruct((2 * cells, LANES), F32),
        in_specs=[vmem(), hbm(), vmem()],
        out_specs=hbm(),
        scratch_shapes=[
            pltpu.VMEM((2 * cells, LANES), F32),
            pltpu.VMEM((2 * (cells + late_rows), LANES), F32),
            pltpu.VMEM((2 * face_count * CHUNK, LANES), F32),
            pltpu.VMEM((2 * face_count * CHUNK, LANES), F32),
            pltpu.VMEM((padded, cells), F32),
            pltpu.VMEM((cells, padded), F32),
            pltpu.VMEM((face_count * cells // LANES, LANES), I32),
            pltpu.SMEM((face_count * cells // LANES, LANES), I32),
            pltpu.SemaphoreType.DMA,
            pltpu.SemaphoreType.DMA,
            pltpu.SemaphoreType.DMA((4,)),
        ],
        compiler_params=pltpu.CompilerParams(vmem_limit_bytes=VMEM_MIB * MIB),
        cost_estimate=pl.CostEstimate(flops=20_000_000_000, bytes_accessed=16 * MIB, transcendentals=0),
        name="diffuse_early",
    )(faces, own, coef)


def leave_kernel(face_count, cells, faces, mig, counts, own, g0, g1, g2, g3, coef, out, table, landed, stage, own_stage, coef8,
                 columns, coef_stage, faces_v, faces_s, sem, face_sem, ghost_sems):
    ghost_copies = start_ghosts((g0, g1, g2, g3), landed, ghost_sems)
    copy = pltpu.make_async_copy(own, table.at[pl.ds(0, 2 * cells)], sem)
    copy.start()
    face_copy = start_faces(faces, faces_v, faces_s, face_sem)
    turn_columns(coef, coef8, columns)
    spread_ghosts(ghost_copies, landed, table, cells)
    face_copy.wait()
    flat = faces_s.reshape(face_count * cells)
    copy.wait()

    def chunk(i, carry):
        for u in range(CHUNK):
            cell = mig[i, u]
            own_stage[rows2(2 * u), :] = table[rows2(2 * cell), :]
            coef_stage[pl.ds(u, 1), :] = columns[pl.ds(cell, 1), :]
            for f in range(face_count):
                stage[rows2((f * CHUNK + u) * 2), :] = table[rows2(flat.at[pl.ds(f * cells, cells)][cell]), :]
        one, two = face_sums(own_stage[pl.ds(0, CHUNK, stride=2), :], own_stage[pl.ds(1, CHUNK, stride=2), :],
                             coef_stage[...], stage, face_count)
        at = pl.ds(pl.multiple_of(i * CHUNK, CHUNK), CHUNK)
        keep = iota2((CHUNK, LANES), 0) < counts[0, i]
        out[at, 0:LANES] = jnp.where(keep, one, 0.0).astype(BF16)
        out[at, LANES:2 * LANES] = jnp.where(keep, two, 0.0).astype(BF16)
        return carry

    lax.fori_loop(0, out.shape[0] // CHUNK, chunk, 0)


def diffuse_leaving(faces, mig, counts, own, ghosts, coef):
    face_count, cells = coef.shape
    padded = face_count + -face_count % 8
    ghost_rows = sum(g.shape[0] for g in ghosts)
    return pl.pallas_call(
        functools.partial(leave_kernel, face_count, cells),
        out_shape=jax.ShapeDtypeStruct((mig.shape[0] * CHUNK, 2 * LANES), BF16),
        in_specs=[vmem(), smem(), smem()] + [hbm()] * 5 + [vmem()],
        out_specs=vmem(),
        scratch_shapes=[
            pltpu.VMEM((2 * (cells + ghost_rows), LANES), F32),
            pltpu.VMEM((len(ghosts),) + ghosts[0].shape, BF16),
            pltpu.VMEM((2 * face_count * CHUNK, LANES), F32),
            pltpu.VMEM((2 * CHUNK, LANES), F32),
            pltpu.VMEM((padded, cells), F32),
            pltpu.VMEM((cells, padded), F32),
            pltpu.VMEM((CHUNK, padded), F32),
            pltpu.VMEM((face_count * cells // LANES, LANES), I32),
            pltpu.SMEM((face_count * cells // LANES, LANES), I32),
            pltpu.SemaphoreType.DMA,
            pltpu.SemaphoreType.DMA,
            pltpu.SemaphoreType.DMA((len(ghosts),)),
        ],
        compiler_params=pltpu.CompilerParams(vmem_limit_bytes=VMEM_MIB * MIB),
        cost_estimate=pl.CostEstimate(flops=500_000_000, bytes_accessed=8 * MIB, transcendentals=0),
        name="diffuse_leaving",
    )(faces, mig, counts, own, *ghosts, coef)


def list_kernel(face_count, cells, shift, faces, out, turned):
    rows = cells // LANES
    place = iota2((rows, LANES), 0) * LANES + iota2((rows, LANES), 1)
    words = []
    lines_of(faces, turned, 2)
    for f in range(face_count):
        to = turned[f * rows:(f + 1) * rows, :]
        late = to >= 2 * cells
        number = jnp.sum(late.astype(F32), keepdims=True).astype(I32)
        out[face_count * rows + f:face_count * rows + f + 1, :] = jnp.broadcast_to(number, (1, LANES))
        words.append(jnp.where(late, ((2 * place) << shift) + (to - 2 * cells), (2 * cells) << shift))
    size = 2
    while size <= cells:
        apart = size // 2
        while apart >= 1:
            low = (place & apart) == 0
            smaller = (((place >> (size.bit_length() - 1)) ^ (place >> (apart.bit_length() - 1))) & 1) == 0
            for f in range(face_count):
                x = words[f]
                axis, by, length = (1, apart, LANES) if apart < LANES else (0, apart // LANES, rows)
                other = jnp.where(low, pltpu.roll(x, length - by, axis), pltpu.roll(x, by, axis))
                words[f] = jnp.where(smaller, jnp.minimum(x, other), jnp.maximum(x, other))
            apart //= 2
        size *= 2
    for f in range(face_count):
        out[f * rows:(f + 1) * rows, :] = words[f]


def late_lists(faces, shift, after):
    face_count, cells = faces.shape
    rows = face_count * cells // LANES
    return pl.pallas_call(
        lambda faces, after_ref, out, turned: list_kernel(face_count, cells, shift, faces, out, turned),
        out_shape=jax.ShapeDtypeStruct((rows + 8, LANES), I32),
        in_specs=[vmem(), hbm()],
        out_specs=vmem(),
        scratch_shapes=[pltpu.VMEM((rows, LANES), I32)],
        compiler_params=pltpu.CompilerParams(vmem_limit_bytes=VMEM_MIB * MIB),
        cost_estimate=pl.CostEstimate(flops=2_000_000_000, bytes_accessed=1 * MIB, transcendentals=0),
        name="late_lists",
    )(faces, after)


def late_kernel(face_count, cells, shift, lists, coef, early, g0, g1, g2, g3, out, sums, table, landed, coef_v, coef_s, sem,
                ghost_sems, coef_sem):
    ghost_copies = start_ghosts((g0, g1, g2, g3), landed, ghost_sems)
    copy = pltpu.make_async_copy(early, sums.at[pl.ds(0, 2 * cells)], sem)
    copy.start()
    lines_of(coef, coef_v, 1.0)
    coef_copy = pltpu.make_async_copy(coef_v, coef_s, coef_sem)
    coef_copy.start()
    spread_ghosts(ghost_copies, landed, table, 0)
    steps = small_numbers(lists[0])
    coef_copy.wait()
    flat = coef_s.reshape(face_count * cells)
    copy.wait()
    for f in range(face_count):
        def some(i, carry):
            found = []
            for j in range(CHUNK // GROUP):
                group = lists.at[pl.ds(i * CHUNK + (f * cells + j * GROUP), GROUP)]
                for k in range(GROUP):
                    word = group[steps[k]]
                    row = rows2(word >> shift)
                    weight = flat.at[pl.ds(f * cells, cells)][jnp.minimum(word >> (shift + 1), cells - 1)]
                    late = table[rows2(word & ((1 << shift) - 1)), :]
                    found.append((row, sums[row, :] + weight * late))
            for row, value in found:
                sums[row, :] = value
            return carry

        lax.fori_loop(0, (lists[face_count * cells + f * LANES] + (CHUNK - 1)) // CHUNK, some, 0)
    span = 256

    def pack(i, carry):
        at = pl.ds(pl.multiple_of(i * span, span), span)
        out[at, 0:LANES] = sums[pl.ds(pl.multiple_of(i * 2 * span, span), span, stride=2), :].astype(BF16)
        out[at, LANES:2 * LANES] = sums[pl.ds(i * 2 * span + 1, span, stride=2), :].astype(BF16)
        return carry

    lax.fori_loop(0, cells // span, pack, 0)


def diffuse_late(lists, coef, early, ghosts, shift):
    face_count, cells = coef.shape
    ghost_rows = sum(g.shape[0] for g in ghosts)
    return pl.pallas_call(
        functools.partial(late_kernel, face_count, cells, shift),
        out_shape=jax.ShapeDtypeStruct((cells, 2 * LANES), BF16),
        in_specs=[smem(), vmem(), hbm()] + [hbm()] * len(ghosts),
        out_specs=vmem(),
        scratch_shapes=[
            pltpu.VMEM((2 * cells + 16, LANES), F32),
            pltpu.VMEM((2 * ghost_rows, LANES), F32),
            pltpu.VMEM((len(ghosts),) + ghosts[0].shape, BF16),
            pltpu.VMEM((face_count * cells // LANES, LANES), F32),
            pltpu.SMEM((face_count * cells // LANES, LANES), F32),
            pltpu.SemaphoreType.DMA,
            pltpu.SemaphoreType.DMA((len(ghosts),)),
            pltpu.SemaphoreType.DMA,
        ],
        compiler_params=pltpu.CompilerParams(vmem_limit_bytes=VMEM_MIB * MIB),
        cost_estimate=pl.CostEstimate(flops=9_000_000_000, bytes_accessed=24 * MIB, transcendentals=0),
        name="diffuse_late",
    )(lists, coef, early, *ghosts)


def body(dust, classes, kernels, export_ids, faces, face_coef, mig_ids, mig_counts):
    row_width = dust.shape[1]
    export = export_ids.shape[2]
    domains = mig_counts.shape[1]
    capacity = mig_ids.shape[1]
    shift = (8 * export - 1).bit_length()
    own, up, down, left, right = own_cells(dust, classes, kernels, export_ids)
    g0, g1 = passed_along(up, "dx", 1), passed_along(down, "dx", -1)
    g2, g3 = passed_along(left, "dy", 1), passed_along(right, "dy", -1)
    ghosts = (g0, g1, g2, g3)
    faces, face_coef, mig_ids, own = lax.optimization_barrier((faces, face_coef, mig_ids, own))
    early = diffuse_early(faces, own, face_coef, 4 * export)
    lists = late_lists(faces, shift, own)
    leaving = diffuse_leaving(faces, mig_ids, mig_counts, own, ghosts, face_coef)
    arrived = lax.all_to_all(leaving.reshape(domains, capacity, row_width), ("dx", "dy"), split_axis=0, concat_axis=0, tiled=True)
    updated = diffuse_late(lists.reshape(-1), face_coef, early, ghosts, shift)
    return (updated, arrived.reshape(domains * capacity, row_width))


def solution(mesh):
    return jax.shard_map(
        body,
        mesh=mesh,
        in_specs=(
            P(("dx", "dy"), None),
            P(("dx", "dy")),
            P(),
            P(("dx", "dy"), None, None),
            P(None, ("dx", "dy")),
            P(None, ("dx", "dy")),
            P(("dx", "dy"), None),
            P(("dx", "dy"), None),
        ),
        out_specs=(P(("dx", "dy"), None), P(("dx", "dy"), None)),
        check_vma=False,
    )
```

time: 117 us -> 87.8 us (0.75)
  waiting for transfers between devices: 19.2 us -> 0.01 us
  local copies, waits for them, and re-layouts: 11.8 us -> 3.3 us
  Pallas kernels: 68.7 us -> 72.1 us
  starting transfers between devices: 14.2 us -> 11.1 us
  other arithmetic: 1.65 us -> 0 us
    pallas_call x2 -> x4, Pallas kernels: 28.4 us -> 51.5 us  [the longest x1 22.1 us: diffuse_early(): pl.pallas_call(functools.partial(early_kernel, face_count, cells, late_ro...]
    pallas_call x1, Pallas kernels: 40.4 us -> 20.6 us  [own_cells(): pl.pallas_call(functools.partial(own_kernel, cells), out_shape=(jax.Shape...]
    ppermute x4, waiting for transfers between devices: 19.2 us -> 0.01 us  [passed_along(): return lax.ppermute(block, axis, route)]
    unnamed x24 -> x11, local copies, waits for them, and re-layouts: 10.4 us -> 2.63 us
    all_to_all x1, starting transfers between devices: 6.53 us -> 3.29 us  [body(): lax.all_to_all(leaving.reshape(domains, capacity, row_width), ('dx', 'dy'...]
    slice x1 -> x0, local copies, waits for them, and re-layouts: 1.31 us -> none  [body(): ghosts.append(passed_along(blocks[direction], 'dy', offset))]
  transfers between devices with their start and end apart: 5 -> 5, of which waited for: 2 -> 0; matrix products, arithmetic and copies ran while one was open for 1% -> 1% of each run, Pallas kernels for 19% -> 50%
where the time goes in v2:
time: 87.8 us; the launch traced here: 87.3 us
  Pallas kernels  72.1 us (82%)
  starting transfers between devices  11.1 us (13%)
  local copies, waits for them, and re-layouts  3.3 us (4%)
    pallas_call x1, Pallas kernels, diffuse_early(): pl.pallas_call(functools.partial(early_kernel, face_count, cells, late_ro...  22.1 us
    pallas_call x1, Pallas kernels, own_cells(): pl.pallas_call(functools.partial(own_kernel, cells), out_shape=(jax.Shape...  20.6 us
    pallas_call x1, Pallas kernels, diffuse_late(): pl.pallas_call(functools.partial(late_kernel, face_count, cells, shift),...  14.7 us
    pallas_call x1, Pallas kernels, diffuse_leaving(): pl.pallas_call(functools.partial(leave_kernel, face_count, cells), out_sh...  8.08 us
    ppermute x4, starting transfers between devices, passed_along(): return lax.ppermute(block, axis, route)  7.81 us
    pallas_call x1, Pallas kernels, late_lists(): pl.pallas_call(lambda faces, after_ref, out, turned: list_kernel(face_cou...  6.7 us
    all_to_all x1, starting transfers between devices, body(): lax.all_to_all(leaving.reshape(domains, capacity, row_width), ('dx', 'dy'...  3.29 us
    unnamed x11, local copies, waits for them, and re-layouts  2.63 us
  transfers between devices with their start and end apart: 5, of which 0 were waited for; matrix products, arithmetic and copies ran while one was open for 1% of the time, Pallas kernels for 50%

profile of v2, /device:TPU:0, one launch (start us, length us, event | category | flops | bytes accessed | tf_op | source)
XLA Modules:
  0.0 87.3 jit_solution(18204381524709121733)
XLA Ops:
  0.6 20.6 %coagulate_own.1 = (f32[8192,128]{1,0:T(8,128)}, bf16[1024,256]{1,0:T(8,128)(2,1)}, bf16[1024,256]{1,0:T(8,128)(2,1)}, bf16[1024,256]{1,0:T(8,128)(2,1)}, bf16[1024,256]{1,0:T(8,128)(2,1)}) custom-call(s32[32,128]{1,0:T(8,128)} %bitcast.6, s32[1,4,1024]{2,1,0:T(4,128)} %exp_ref.1, bf16[4096,256]{1,0:T(8,128)(2,1)} %dust_any.1, bf16[8,2,128,128]{3,2,1,0:T(8,128)(2,1)} %kern_any.1), custom_call_target="tpu_custom_call" | custom-call | flops 8999999488 | bytes 12582912 | tf_op jit(solution)/shard_map/coagulate_own/pallas_call | solution.py:241
  21.2 3.1 %collective-permute-start = (bf16[1024,256]{1,0:T(8,128)(2,1)}, bf16[1024,256]{1,0:T(8,128)(2,1)S(1)}, u32[]{:S(2)}, u32[]{:S(2)}) collective-permute-start(bf16[1024,256]{1,0:T(8,128)(2,1)} %get-tuple-element.15), channel_id=1, source_target_pairs={{24,0},{0,8},{8,16},{16,24},{25,1},{1,9},{9,17},{17,25},{26,2},{2,... | collective-permute-start | bytes 1572872 | tf_op jit(solution)/shard_map/ppermute | solution.py:25
  24.3 2.1 %collective-permute-start.1 = (bf16[1024,256]{1,0:T(8,128)(2,1)}, bf16[1024,256]{1,0:T(8,128)(2,1)S(1)}, u32[]{:S(2)}, u32[]{:S(2)}) collective-permute-start(bf16[1024,256]{1,0:T(8,128)(2,1)} %get-tuple-element.16), channel_id=1, source_target_pairs={{8,0},{16,8},{24,16},{0,24},{9,1},{17,9},{25,17},{1,25},{10,2},{18... | collective-permute-start | bytes 1572872 | tf_op jit(solution)/shard_map/ppermute | solution.py:25
  26.4 0.0 collective-permute-start.2
  26.4 2.6 %collective-permute-start.3 = (bf16[1024,256]{1,0:T(8,128)(2,1)}, bf16[1024,256]{1,0:T(8,128)(2,1)S(1)}, u32[]{:S(2)}, u32[]{:S(2)}) collective-permute-start(bf16[1024,256]{1,0:T(8,128)(2,1)} %get-tuple-element.18), channel_id=1, source_target_pairs={{1,0},{2,1},{3,2},{4,3},{5,4},{6,5},{7,6},{0,7},{9,8},{10,9},{11,1... | collective-permute-start | bytes 1572872 | tf_op jit(solution)/shard_map/ppermute | solution.py:25
  29.1 0.0 copy-start.4
  29.1 22.1 %diffuse_early.1.early = f32[8192,128]{1,0:T(8,128)} custom-call(s32[6,4096]{1,0:T(8,128)} %faces.2, f32[8192,128]{1,0:T(8,128)} %get-tuple-element.13.after_ref.own, f32[6,4096]{1,0:T(8,128)} %coef.2), custom_call_target="tpu_custom_call" | custom-call | flops 20000000000 | bytes 16777216 | tf_op jit(solution)/shard_map/diffuse_early/pallas_call | solution.py:371
  51.1 0.0 copy-done.4
  51.1 0.7 copy.10.mig
  51.8 6.7 %late_lists.1 = s32[200,128]{1,0:T(8,128)} custom-call(s32[6,4096]{1,0:T(8,128)} %faces.2, f32[8192,128]{1,0:T(8,128)} %get-tuple-element.13.after_ref.own), custom_call_target="tpu_custom_call" | custom-call | flops 2000000000 | bytes 1048576 | tf_op jit(solution)/shard_map/late_lists/pallas_call | solution.py:485
  58.5 0.0 collective-permute-done.g0
  58.5 0.0 copy-start
  58.5 0.0 collective-permute-done.1.g1
  58.5 0.0 copy-start.1
  58.5 0.0 collective-permute-done.2.g2
  58.5 0.0 copy-start.2
  58.5 0.0 collective-permute-done.3.g3
  58.6 0.8 copy-done
  59.3 0.2 copy-done.1
  59.5 0.1 copy-done.2
  59.6 0.0 copy-start.3
  59.6 0.8 copy-done.3
  60.5 8.1 %diffuse_leaving.1 = bf16[512,256]{1,0:T(8,128)(2,1)} custom-call(s32[6,4096]{1,0:T(8,128)} %faces.2, s32[32,16]{1,0:T(8,128)} %copy.10.mig, s32[1,32]{1,0:T(1,128)} %counts.1, f32[8192,128]{1,0:T(8,128)} %get-tuple-element.13.after_ref.own, bf16[1024,256]{1,0:T(8,128)(2,1)} %copy-done, bf16[1024,256]{1,0:T(8,128)(2,1)} %copy-done.1, ...), custom_call_target="tpu_custom_call" | custom-call | flops 500000000 | bytes 8388608 | tf_op jit(solution)/shard_map/diffuse_leaving/pallas_call | solution.py:429
  68.6 3.3 %all-to-all-start = ((bf16[32,16,256]{2,1,0:T(8,128)(2,1)}), bf16[32,16,256]{2,1,0:T(8,128)(2,1)S(1)}, u32[]{:S(2)}, u32[]{:S(2)}) async-start(bf16[32,16,256]{2,1,0:T(8,128)(2,1)} %bitcast.4), calls=%async_computation | async-start | bytes 524288 | tf_op jit(solution)/shard_map/all_to_all | solution.py:575
  71.9 14.7 %diffuse_late.1 = bf16[4096,256]{1,0:T(8,128)(2,1)} custom-call(s32[25600]{0:T(1024)} %bitcast.7, f32[6,4096]{1,0:T(8,128)} %coef.2, f32[8192,128]{1,0:T(8,128)} %diffuse_early.1.early, bf16[1024,256]{1,0:T(8,128)(2,1)} %copy-done, bf16[1024,256]{1,0:T(8,128)(2,1)} %copy-done.1, bf16[1024,256]{1,0:T(8,128)(2,1)} %copy-done.2, bf16[1024,256]{1,0:T(8,128)(2,1)} %copy-done.3), custom_call_target="tpu_custom_call" | custom-call | flops 8999999488 | bytes 25165824 | tf_op jit(solution)/shard_map/diffuse_late/pallas_call | solution.py:540
  86.6 0.0 all-to-all-done
  86.6 0.7 copy.12
Async XLA Ops:
  21.2 37.3 %collective-permute-start = (bf16[1024,256]{1,0:T(8,128)(2,1)}, bf16[1024,256]{1,0:T(8,128)(2,1)S(1)}, u32[]{:S(2)}, u32[]{:S(2)}) collective-permute-start(bf16[1024,256]{1,0:T(8,128)(2,1)} %get-tuple-element.15), channel_id=1, source_target_pairs={{24,0},{0,8},{8,16},{16,24},{25,1},{1,9},{9,17},{17,25},{26,2},{2,... | collective-permute-start | bytes 1572872 | tf_op jit(solution)/shard_map/ppermute | solution.py:25
  24.3 34.2 %collective-permute-start.1 = (bf16[1024,256]{1,0:T(8,128)(2,1)}, bf16[1024,256]{1,0:T(8,128)(2,1)S(1)}, u32[]{:S(2)}, u32[]{:S(2)}) collective-permute-start(bf16[1024,256]{1,0:T(8,128)(2,1)} %get-tuple-element.16), channel_id=1, source_target_pairs={{8,0},{16,8},{24,16},{0,24},{9,1},{17,9},{25,17},{1,25},{10,2},{18... | collective-permute-start | bytes 1572872 | tf_op jit(solution)/shard_map/ppermute | solution.py:25
  26.4 32.1 %collective-permute-start.2 = (bf16[1024,256]{1,0:T(8,128)(2,1)}, bf16[1024,256]{1,0:T(8,128)(2,1)S(1)}, u32[]{:S(2)}, u32[]{:S(2)}) collective-permute-start(bf16[1024,256]{1,0:T(8,128)(2,1)} %get-tuple-element.17), channel_id=1, source_target_pairs={{7,0},{0,1},{1,2},{2,3},{3,4},{4,5},{5,6},{6,7},{15,8},{8,9},{9,10... | collective-permute-start | bytes 1572872 | tf_op jit(solution)/shard_map/ppermute | solution.py:25
  26.4 32.1 %collective-permute-start.3 = (bf16[1024,256]{1,0:T(8,128)(2,1)}, bf16[1024,256]{1,0:T(8,128)(2,1)S(1)}, u32[]{:S(2)}, u32[]{:S(2)}) collective-permute-start(bf16[1024,256]{1,0:T(8,128)(2,1)} %get-tuple-element.18), channel_id=1, source_target_pairs={{1,0},{2,1},{3,2},{4,3},{5,4},{6,5},{7,6},{0,7},{9,8},{10,9},{11,1... | collective-permute-start | bytes 1572872 | tf_op jit(solution)/shard_map/ppermute | solution.py:25
  29.1 22.1 %copy-start.4 = (s32[32,16]{0,1:T(8,128)S(1)}, s32[32,16]{0,1:T(8,128)}, u32[]{:S(2)}) copy-start(s32[32,16]{0,1:T(8,128)} %param.14) | copy-start | bytes 6148
  58.5 0.8 copy-start
  58.5 1.0 %copy-start.1 = (bf16[1024,256]{1,0:T(8,128)(2,1)}, bf16[1024,256]{1,0:T(8,128)(2,1)S(1)}, u32[]{:S(2)}) copy-start(bf16[1024,256]{1,0:T(8,128)(2,1)S(1)} %collective-permute-done.1.g1) | copy-start | bytes 1572868
  58.5 1.1 %copy-start.2 = (bf16[1024,256]{1,0:T(8,128)(2,1)}, bf16[1024,256]{1,0:T(8,128)(2,1)S(1)}, u32[]{:S(2)}) copy-start(bf16[1024,256]{1,0:T(8,128)(2,1)S(1)} %collective-permute-done.2.g2) | copy-start | bytes 1572868
  59.6 0.8 copy-start.3
  68.6 18.0 %all-to-all-start = ((bf16[32,16,256]{2,1,0:T(8,128)(2,1)}), bf16[32,16,256]{2,1,0:T(8,128)(2,1)S(1)}, u32[]{:S(2)}, u32[]{:S(2)}) async-start(bf16[32,16,256]{2,1,0:T(8,128)(2,1)} %bitcast.4), calls=%async_computation | async-start | bytes 524288 | tf_op jit(solution)/shard_map/all_to_all | solution.py:575

commit v3 on v2

--- a/solution.py
+++ b/solution.py
@@ -12,11 +12,15 @@
 GROUP = 8
 TILE = 576
 CHUNK = 16
+BATCH = 32
+FIRST_LINES = 16
 F32 = jnp.float32
 BF16 = jnp.bfloat16
 I32 = jnp.int32
+KIB = 1 << 10
 MIB = 1 << 20
-VMEM_MIB = 60
+VMEM_KIB = 65330
+LESS_VMEM_KIB = 61440
 
 
 def passed_along(block, axis, distance):
@@ -29,9 +33,9 @@
     return lax.broadcasted_iota(I32, shape, dim)
 
 
-def small_numbers(none_negative):
-    unit = jnp.minimum(none_negative, 0) + 1
-    return [unit * k for k in range(GROUP)]
+def small_numbers(none_negative, count=GROUP, apart=1):
+    unit = jnp.minimum(none_negative, 0) + apart
+    return [unit * k for k in range(count)]
 
 
 def lines_of(source, lines, times):
@@ -106,31 +110,35 @@
     return one.astype(BF16), two.astype(BF16)
 
 
-def send_rows(ids, line, steps, table, outbound, stages):
-    span = stages[0].shape[0] // 2
-    spans = outbound.shape[0] // span
-
-    def pull(i, stage):
+def send_rows(ids, steps, table, outbound, stages):
+    span = LANES
+    lines = ids.shape[0]
+
+    def pull(line, stage):
         for j in range(span // GROUP):
-            group = ids.at[line + i, pl.ds(j * GROUP, GROUP)]
+            group = ids.at[line, pl.ds(j * GROUP, GROUP)]
             for k in range(GROUP):
                 stage[rows2((j * GROUP + k) * 2), :] = table[rows2(group[steps[k]]), :]
 
-    def push(i, stage):
+    def push(block, i, stage):
         at = pl.ds(pl.multiple_of(i * span, span), span)
-        outbound[at, 0:LANES] = stage[pl.ds(0, span, stride=2), :].astype(BF16)
-        outbound[at, LANES:2 * LANES] = stage[pl.ds(1, span, stride=2), :].astype(BF16)
+        block[at, 0:LANES] = stage[pl.ds(0, span, stride=2), :].astype(BF16)
+        block[at, LANES:2 * LANES] = stage[pl.ds(1, span, stride=2), :].astype(BF16)
 
     pull(0, stages[0])
-
-    def pair(i, carry):
-        push(2 * i, stages[0])
-        pull(2 * i + 1, stages[1])
-        push(2 * i + 1, stages[1])
-        pull(jnp.minimum(2 * i + 2, spans - 1), stages[0])
-        return carry
-
-    lax.fori_loop(0, spans // 2, pair, 0)
+    first = 0
+    for block in outbound:
+        spans = block.shape[0] // span
+
+        def pair(i, carry):
+            push(block, 2 * i, stages[0])
+            pull(first + 2 * i + 1, stages[1])
+            push(block, 2 * i + 1, stages[1])
+            pull(jnp.minimum(first + 2 * i + 2, lines - 1), stages[0])
+            return carry
+
+        lax.fori_loop(0, spans // 2, pair, 0)
+        first += spans
 
 
 def own_kernel(cells, cls_ref, exp_ref, dust_any, kern_any, out_any, out_up, out_down, out_left, out_right,
@@ -146,7 +154,6 @@
         at = pl.ds(p * part, part)
         dust_copies.append(pltpu.make_async_copy(dust_any.at[at], dust.at[at], dust_sems.at[p]))
         dust_copies[-1].start()
-    export_lines = exp_ref.shape[2] // LANES
     lines_of(exp_ref.at[0], exp_v, 2)
     exp_copy = pltpu.make_async_copy(exp_v, exp_s, exp_sem)
     exp_copy.start()
@@ -214,8 +221,7 @@
     lax.fori_loop(0, rows, gather, 0)
     out_copy = pltpu.make_async_copy(out, out_any, sem)
     out_copy.start()
-    for k, block in enumerate((out_up, out_down, out_left, out_right)):
-        send_rows(exp_s, k * export_lines, steps, out, block, (stage_a, stage_b))
+    send_rows(exp_s, steps, out, (out_up, out_down, out_left, out_right), (stage_a, stage_b))
     out_copy.wait()
 
 
@@ -225,6 +231,10 @@
 
 def smem():
     return pl.BlockSpec(memory_space=pltpu.SMEM)
+
+
+def anywhere():
+    return pl.BlockSpec(memory_space=pl.ANY)
 
 
 def hbm():
@@ -260,7 +270,7 @@
             pltpu.SemaphoreType.DMA,
             pltpu.SemaphoreType.DMA,
         ],
-        compiler_params=pltpu.CompilerParams(vmem_limit_bytes=VMEM_MIB * MIB),
+        compiler_params=pltpu.CompilerParams(vmem_limit_bytes=VMEM_KIB * KIB),
         cost_estimate=pl.CostEstimate(flops=9_000_000_000, bytes_accessed=12 * MIB, transcendentals=0),
         name="coagulate_own",
     )(classes.reshape(rows, LANES), export_ids, dust, kernels)
@@ -281,7 +291,8 @@
 
 def turn_columns(coef, coef8, columns):
     together = 4
-    coef8[0:coef.shape[0], :] = coef[...]
+    if coef is not None:
+        coef8[0:coef.shape[0], :] = coef[...]
 
     def turn(b, carry):
         for u in range(together):
@@ -313,8 +324,84 @@
         spread_rows(landed.at[k], table, first + k * landed.shape[1], landed.shape[1])
 
 
-def early_kernel(face_count, cells, late_rows, faces, own, coef, out_any, out, table, stage_a, stage_b, coef8, columns,
-                 faces_v, faces_s, sem, face_sem, out_sems):
+def late_lists(face_count, cells, shift, out, counts, lines):
+    per_face = cells // LANES
+    blocks = per_face // 8
+    lane, sub = iota2((8, LANES), 1), iota2((8, LANES), 0)
+    words = []
+    for f in range(face_count):
+        number = None
+        words.append([])
+        for v in range(blocks):
+            first = f * per_face + v * 8
+            to = lines[first:first + 8, :]
+            late = to >= 2 * cells
+            cell = (sub + v * 8) * LANES + lane
+            words[f].append(jnp.where(late, (cell << shift) + (to - 2 * cells), cells << shift))
+            counted = late.astype(F32)
+            number = counted if number is None else number + counted
+        number = jnp.sum(number, keepdims=True).astype(I32)
+        counts[f:f + 1, :] = jnp.broadcast_to(number, (1, LANES))
+    block_bits = blocks.bit_length() - 1
+
+    def bit(b, v):
+        if b < block_bits:
+            return bool((v >> b) & 1)
+        if b < block_bits + 3:
+            return ((sub >> (b - block_bits)) & 1) == 1
+        if b < block_bits + 3 + 7:
+            return ((lane >> (b - block_bits - 3)) & 1) == 1
+        return False
+
+    def pick(where_true, a, b):
+        if isinstance(where_true, bool):
+            return a if where_true else b
+        return jnp.where(where_true, a, b)
+
+    def same(a, b):
+        if isinstance(a, bool) and isinstance(b, bool):
+            return a == b
+        if isinstance(a, bool):
+            a, b = b, a
+        if isinstance(b, bool):
+            return a if b else jnp.logical_not(a)
+        return jnp.logical_not(jnp.logical_xor(a, b))
+
+    bits = cells.bit_length() - 1
+    for size_bit in range(1, bits + 1):
+        for b in range(size_bit - 1, -1, -1):
+            for v in range(blocks):
+                if b < block_bits and bit(b, v):
+                    continue
+                down = bit(size_bit, v)
+                if b >= block_bits:
+                    high = bit(b, v)
+                    largest = jnp.logical_not(same(high, down)) if not isinstance(down, bool) else same(high, not down)
+                for f in range(face_count):
+                    x = words[f][v]
+                    if b < block_bits:
+                        w = v ^ (1 << b)
+                        y = words[f][w]
+                        least, most = jnp.minimum(x, y), jnp.maximum(x, y)
+                        words[f][v] = pick(down, most, least)
+                        words[f][w] = pick(down, least, most)
+                        continue
+                    axis, by, length = (0, 1 << (b - block_bits), 8)
+                    if b >= block_bits + 3:
+                        axis, by, length = (1, 1 << (b - block_bits - 3), LANES)
+                    other = pltpu.roll(x, by, axis)
+                    if 2 * by < length:
+                        other = jnp.where(high, other, pltpu.roll(x, length - by, axis))
+                    words[f][v] = pick(largest, jnp.maximum(x, other), jnp.minimum(x, other))
+    for f in range(face_count):
+        word = jnp.concatenate(words[f], axis=0)
+        both = jnp.concatenate([word >> shift, word & ((1 << shift) - 1)], axis=0)
+        out[f * LANES:(f + 1) * LANES, 0:2 * per_face] = both.T
+
+
+def early_kernel(face_count, cells, late_rows, shift, faces, mig, own, coef, out_any, mig_sums, mig_coef, mig_late, lists, counts,
+                 out, table,
+                 stage_a, stage_b, coef8, columns, late8, late_columns, mig_columns, faces_v, faces_s, sem, face_sem, out_sems):
     copy = pltpu.make_async_copy(own, table.at[pl.ds(0, 2 * cells)], sem)
     copy.start()
     face_copy = start_faces(faces, faces_v, faces_s, face_sem)
@@ -325,6 +412,9 @@
 
     lax.fori_loop(0, 2 * late_rows // 256, clear, 0)
     turn_columns(coef, coef8, columns)
+    late8[0:face_count, :] = jnp.where(faces[...] >= cells, 2 * (faces[...] - cells), 2 * late_rows)
+    turn_columns(None, late8, late_columns)
+    late_lists(face_count, cells, shift, lists, counts, faces_v)
     face_copy.wait()
     flat = faces_s.reshape(face_count * cells)
     steps = small_numbers(faces_s[0, 0])
@@ -361,18 +451,42 @@
         at = pl.ds(p * (2 * cells // parts), 2 * cells // parts)
         done.append(pltpu.make_async_copy(out.at[at], out_any.at[at], out_sems.at[p]))
         done[-1].start()
+
+    def leaving(i, carry):
+        for u in range(CHUNK):
+            cell = mig[u, i]
+            at = i * CHUNK + u
+            mig_sums[rows2(2 * at), :] = out[rows2(2 * cell), :]
+            mig_coef[pl.ds(at, 1), :] = columns[pl.ds(cell, 1), :]
+            mig_columns[pl.ds(at, 1), :] = late_columns[pl.ds(cell, 1), :]
+        return carry
+
+    lax.fori_loop(0, mig.shape[1], leaving, 0)
+    lines = mig_columns.shape[0] // LANES
+    for i in range(lines):
+        turned = mig_columns[i * LANES:(i + 1) * LANES, :].T
+        for f in range(face_count):
+            mig_late[f * lines + i:f * lines + i + 1, :] = turned[f:f + 1, :]
     for part in done:
         part.wait()
 
 
-def diffuse_early(faces, own, coef, late_rows):
+def diffuse_early(faces, mig, own, coef, late_rows, shift):
     face_count, cells = coef.shape
     padded = face_count + -face_count % 8
+    leaving = mig.shape[0] * mig.shape[1]
     return pl.pallas_call(
-        functools.partial(early_kernel, face_count, cells, late_rows),
-        out_shape=jax.ShapeDtypeStruct((2 * cells, LANES), F32),
-        in_specs=[vmem(), hbm(), vmem()],
-        out_specs=hbm(),
+        functools.partial(early_kernel, face_count, cells, late_rows, shift),
+        out_shape=(
+            jax.ShapeDtypeStruct((2 * cells, LANES), F32),
+            jax.ShapeDtypeStruct((2 * leaving, LANES), F32),
+            jax.ShapeDtypeStruct((leaving, padded), F32),
+            jax.ShapeDtypeStruct((face_count * leaving // LANES, LANES), I32),
+            jax.ShapeDtypeStruct((face_count * LANES, LANES), I32),
+            jax.ShapeDtypeStruct((8, LANES), I32),
+        ),
+        in_specs=[vmem(), smem(), hbm(), vmem()],
+        out_specs=(hbm(), vmem(), vmem(), vmem(), vmem(), vmem()),
         scratch_shapes=[
             pltpu.VMEM((2 * cells, LANES), F32),
             pltpu.VMEM((2 * (cells + late_rows), LANES), F32),
@@ -380,149 +494,149 @@
             pltpu.VMEM((2 * face_count * CHUNK, LANES), F32),
             pltpu.VMEM((padded, cells), F32),
             pltpu.VMEM((cells, padded), F32),
+            pltpu.VMEM((padded, cells), I32),
+            pltpu.VMEM((cells, padded), I32),
+            pltpu.VMEM((leaving, padded), I32),
             pltpu.VMEM((face_count * cells // LANES, LANES), I32),
             pltpu.SMEM((face_count * cells // LANES, LANES), I32),
             pltpu.SemaphoreType.DMA,
             pltpu.SemaphoreType.DMA,
             pltpu.SemaphoreType.DMA((4,)),
         ],
-        compiler_params=pltpu.CompilerParams(vmem_limit_bytes=VMEM_MIB * MIB),
+        compiler_params=pltpu.CompilerParams(vmem_limit_bytes=VMEM_KIB * KIB),
         cost_estimate=pl.CostEstimate(flops=20_000_000_000, bytes_accessed=16 * MIB, transcendentals=0),
         name="diffuse_early",
-    )(faces, own, coef)
-
-
-def leave_kernel(face_count, cells, faces, mig, counts, own, g0, g1, g2, g3, coef, out, table, landed, stage, own_stage, coef8,
-                 columns, coef_stage, faces_v, faces_s, sem, face_sem, ghost_sems):
+    )(faces, mig, own, coef)
+
+
+def leave_kernel(face_count, late_any, counts, sums_any, coef_any, g0, g1, g2, g3, out, table, landed, stage_a, stage_b,
+                 late_s, mig_sums, mig_coef, late_sem, sums_sem, coef_sem, ghost_sems):
     ghost_copies = start_ghosts((g0, g1, g2, g3), landed, ghost_sems)
-    copy = pltpu.make_async_copy(own, table.at[pl.ds(0, 2 * cells)], sem)
-    copy.start()
-    face_copy = start_faces(faces, faces_v, faces_s, face_sem)
-    turn_columns(coef, coef8, columns)
-    spread_ghosts(ghost_copies, landed, table, cells)
-    face_copy.wait()
-    flat = faces_s.reshape(face_count * cells)
-    copy.wait()
-
-    def chunk(i, carry):
-        for u in range(CHUNK):
-            cell = mig[i, u]
-            own_stage[rows2(2 * u), :] = table[rows2(2 * cell), :]
-            coef_stage[pl.ds(u, 1), :] = columns[pl.ds(cell, 1), :]
-            for f in range(face_count):
-                stage[rows2((f * CHUNK + u) * 2), :] = table[rows2(flat.at[pl.ds(f * cells, cells)][cell]), :]
-        one, two = face_sums(own_stage[pl.ds(0, CHUNK, stride=2), :], own_stage[pl.ds(1, CHUNK, stride=2), :],
-                             coef_stage[...], stage, face_count)
-        at = pl.ds(pl.multiple_of(i * CHUNK, CHUNK), CHUNK)
+    copies = [
+        pltpu.make_async_copy(late_any, late_s, late_sem),
+        pltpu.make_async_copy(sums_any, mig_sums, sums_sem),
+        pltpu.make_async_copy(coef_any, mig_coef, coef_sem),
+    ]
+    for copy in copies:
+        copy.start()
+    ghost_rows = landed.shape[0] * landed.shape[1]
+    table[2 * ghost_rows:2 * ghost_rows + 8, :] = jnp.zeros((8, LANES), F32)
+    spread_ghosts(ghost_copies, landed, table, 0)
+    for copy in copies:
+        copy.wait()
+    cells = out.shape[0]
+    mig_late = late_s.reshape(face_count * cells)
+    steps = small_numbers(late_s[0, 0])
+    chunks = cells // CHUNK
+
+    def pull(i, stage):
+        for f in range(face_count):
+            for j in range(CHUNK // GROUP):
+                group = mig_late.at[pl.ds(i * CHUNK + (f * cells + j * GROUP), GROUP)]
+                for k in range(GROUP):
+                    stage[rows2((f * CHUNK + j * GROUP + k) * 2), :] = table[rows2(group[steps[k]]), :]
+
+    def push(i, stage):
+        at = pairs(i * (2 * CHUNK))
+        here = pl.ds(pl.multiple_of(i * CHUNK, CHUNK), CHUNK)
+        one, two = mig_sums[at[0], :], mig_sums[at[1], :]
+        weights = mig_coef[here, :]
+        for f in range(face_count):
+            c = jnp.broadcast_to(weights[:, f:f + 1], (CHUNK, LANES))
+            one = one + c * stage[pl.ds(2 * f * CHUNK, CHUNK, stride=2), :]
+            two = two + c * stage[pl.ds(2 * f * CHUNK + 1, CHUNK, stride=2), :]
         keep = iota2((CHUNK, LANES), 0) < counts[0, i]
-        out[at, 0:LANES] = jnp.where(keep, one, 0.0).astype(BF16)
-        out[at, LANES:2 * LANES] = jnp.where(keep, two, 0.0).astype(BF16)
-        return carry
-
-    lax.fori_loop(0, out.shape[0] // CHUNK, chunk, 0)
-
-
-def diffuse_leaving(faces, mig, counts, own, ghosts, coef):
-    face_count, cells = coef.shape
-    padded = face_count + -face_count % 8
+        out[here, 0:LANES] = jnp.where(keep, one, 0.0).astype(BF16)
+        out[here, LANES:2 * LANES] = jnp.where(keep, two, 0.0).astype(BF16)
+
+    pull(0, stage_a)
+
+    def pair(i, carry):
+        push(2 * i, stage_a)
+        pull(2 * i + 1, stage_b)
+        push(2 * i + 1, stage_b)
+        pull(jnp.minimum(2 * i + 2, chunks - 1), stage_a)
+        return carry
+
+    lax.fori_loop(0, chunks // 2, pair, 0)
+
+
+def diffuse_leaving(mig_late, counts, mig_sums, mig_coef, ghosts, face_count):
     ghost_rows = sum(g.shape[0] for g in ghosts)
     return pl.pallas_call(
-        functools.partial(leave_kernel, face_count, cells),
-        out_shape=jax.ShapeDtypeStruct((mig.shape[0] * CHUNK, 2 * LANES), BF16),
-        in_specs=[vmem(), smem(), smem()] + [hbm()] * 5 + [vmem()],
+        functools.partial(leave_kernel, face_count),
+        out_shape=jax.ShapeDtypeStruct((mig_coef.shape[0], 2 * LANES), BF16),
+        in_specs=[anywhere(), smem(), anywhere(), anywhere()] + [anywhere()] * 4,
         out_specs=vmem(),
         scratch_shapes=[
-            pltpu.VMEM((2 * (cells + ghost_rows), LANES), F32),
+            pltpu.VMEM((2 * ghost_rows + 8, LANES), F32),
             pltpu.VMEM((len(ghosts),) + ghosts[0].shape, BF16),
             pltpu.VMEM((2 * face_count * CHUNK, LANES), F32),
-            pltpu.VMEM((2 * CHUNK, LANES), F32),
-            pltpu.VMEM((padded, cells), F32),
-            pltpu.VMEM((cells, padded), F32),
-            pltpu.VMEM((CHUNK, padded), F32),
-            pltpu.VMEM((face_count * cells // LANES, LANES), I32),
-            pltpu.SMEM((face_count * cells // LANES, LANES), I32),
+            pltpu.VMEM((2 * face_count * CHUNK, LANES), F32),
+            pltpu.SMEM(mig_late.shape, I32),
+            pltpu.VMEM(mig_sums.shape, F32),
+            pltpu.VMEM(mig_coef.shape, F32),
+            pltpu.SemaphoreType.DMA,
             pltpu.SemaphoreType.DMA,
             pltpu.SemaphoreType.DMA,
             pltpu.SemaphoreType.DMA((len(ghosts),)),
         ],
-        compiler_params=pltpu.CompilerParams(vmem_limit_bytes=VMEM_MIB * MIB),
+        compiler_params=pltpu.CompilerParams(vmem_limit_bytes=VMEM_KIB * KIB),
         cost_estimate=pl.CostEstimate(flops=500_000_000, bytes_accessed=8 * MIB, transcendentals=0),
         name="diffuse_leaving",
-    )(faces, mig, counts, own, *ghosts, coef)
-
-
-def list_kernel(face_count, cells, shift, faces, out, turned):
-    rows = cells // LANES
-    place = iota2((rows, LANES), 0) * LANES + iota2((rows, LANES), 1)
-    words = []
-    lines_of(faces, turned, 2)
-    for f in range(face_count):
-        to = turned[f * rows:(f + 1) * rows, :]
-        late = to >= 2 * cells
-        number = jnp.sum(late.astype(F32), keepdims=True).astype(I32)
-        out[face_count * rows + f:face_count * rows + f + 1, :] = jnp.broadcast_to(number, (1, LANES))
-        words.append(jnp.where(late, ((2 * place) << shift) + (to - 2 * cells), (2 * cells) << shift))
-    size = 2
-    while size <= cells:
-        apart = size // 2
-        while apart >= 1:
-            low = (place & apart) == 0
-            smaller = (((place >> (size.bit_length() - 1)) ^ (place >> (apart.bit_length() - 1))) & 1) == 0
-            for f in range(face_count):
-                x = words[f]
-                axis, by, length = (1, apart, LANES) if apart < LANES else (0, apart // LANES, rows)
-                other = jnp.where(low, pltpu.roll(x, length - by, axis), pltpu.roll(x, by, axis))
-                words[f] = jnp.where(smaller, jnp.minimum(x, other), jnp.maximum(x, other))
-            apart //= 2
-        size *= 2
-    for f in range(face_count):
-        out[f * rows:(f + 1) * rows, :] = words[f]
-
-
-def late_lists(faces, shift, after):
-    face_count, cells = faces.shape
-    rows = face_count * cells // LANES
-    return pl.pallas_call(
-        lambda faces, after_ref, out, turned: list_kernel(face_count, cells, shift, faces, out, turned),
-        out_shape=jax.ShapeDtypeStruct((rows + 8, LANES), I32),
-        in_specs=[vmem(), hbm()],
-        out_specs=vmem(),
-        scratch_shapes=[pltpu.VMEM((rows, LANES), I32)],
-        compiler_params=pltpu.CompilerParams(vmem_limit_bytes=VMEM_MIB * MIB),
-        cost_estimate=pl.CostEstimate(flops=2_000_000_000, bytes_accessed=1 * MIB, transcendentals=0),
-        name="late_lists",
-    )(faces, after)
-
-
-def late_kernel(face_count, cells, shift, lists, coef, early, g0, g1, g2, g3, out, sums, table, landed, coef_v, coef_s, sem,
-                ghost_sems, coef_sem):
+    )(mig_late, counts, mig_sums, mig_coef, *ghosts)
+
+
+def late_kernel(face_count, cells, lists, counts, coef, early, g0, g1, g2, g3, out_any, out, sums, table, landed, coef_v, coef_s,
+                lists_s, counts_s, sem, ghost_sems, coef_sem, list_sems, count_sem, out_sems):
     ghost_copies = start_ghosts((g0, g1, g2, g3), landed, ghost_sems)
     copy = pltpu.make_async_copy(early, sums.at[pl.ds(0, 2 * cells)], sem)
     copy.start()
+    count_copy = pltpu.make_async_copy(counts, counts_s, count_sem)
+    count_copy.start()
+    list_copies = []
+    for f in range(face_count):
+        part = pltpu.make_async_copy(lists.at[pl.ds(f * LANES, FIRST_LINES)], lists_s.at[f, pl.ds(0, FIRST_LINES)], list_sems.at[f])
+        part.start()
+        list_copies.append(part)
     lines_of(coef, coef_v, 1.0)
     coef_copy = pltpu.make_async_copy(coef_v, coef_s, coef_sem)
     coef_copy.start()
     spread_ghosts(ghost_copies, landed, table, 0)
-    steps = small_numbers(lists[0])
+    count_copy.wait()
+    steps = small_numbers(counts_s[0, 0])
+    for part in list_copies:
+        part.wait()
     coef_copy.wait()
-    flat = coef_s.reshape(face_count * cells)
+    flat = coef_s.reshape(coef_s.shape[0] * LANES)
     copy.wait()
     for f in range(face_count):
+        weights = flat.at[pl.ds(f * cells, cells + LANES)]
+        number = counts_s[f, 0]
+
+        @pl.when(number > FIRST_LINES * BATCH)
+        def _():
+            rest = LANES - FIRST_LINES
+            more = pltpu.make_async_copy(
+                lists.at[pl.ds(f * LANES + FIRST_LINES, rest)], lists_s.at[f, pl.ds(FIRST_LINES, rest)], list_sems.at[f])
+            more.start()
+            more.wait()
+
         def some(i, carry):
-            found = []
-            for j in range(CHUNK // GROUP):
-                group = lists.at[pl.ds(i * CHUNK + (f * cells + j * GROUP), GROUP)]
+            for j in range(BATCH // GROUP):
+                found = []
+                of_cells = lists_s.at[f, i, pl.ds(j * GROUP, GROUP)]
+                of_rows = lists_s.at[f, i, pl.ds(BATCH + j * GROUP, GROUP)]
                 for k in range(GROUP):
-                    word = group[steps[k]]
-                    row = rows2(word >> shift)
-                    weight = flat.at[pl.ds(f * cells, cells)][jnp.minimum(word >> (shift + 1), cells - 1)]
-                    late = table[rows2(word & ((1 << shift) - 1)), :]
-                    found.append((row, sums[row, :] + weight * late))
-            for row, value in found:
-                sums[row, :] = value
+                    cell = of_cells[steps[k]]
+                    row = rows2(2 * cell)
+                    late = table[rows2(of_rows[steps[k]]), :]
+                    found.append((row, sums[row, :] + weights[cell] * late))
+                for row, value in found:
+                    sums[row, :] = value
             return carry
 
-        lax.fori_loop(0, (lists[face_count * cells + f * LANES] + (CHUNK - 1)) // CHUNK, some, 0)
+        lax.fori_loop(0, (number + (BATCH - 1)) // BATCH, some, 0)
     span = 256
 
     def pack(i, carry):
@@ -531,31 +645,46 @@
         out[at, LANES:2 * LANES] = sums[pl.ds(i * 2 * span + 1, span, stride=2), :].astype(BF16)
         return carry
 
-    lax.fori_loop(0, cells // span, pack, 0)
-
-
-def diffuse_late(lists, coef, early, ghosts, shift):
+    parts = out_sems.shape[0]
+    spans = cells // span // parts
+    done = []
+    for p in range(parts):
+        lax.fori_loop(p * spans, (p + 1) * spans, pack, 0)
+        at = pl.ds(p * (cells // parts), cells // parts)
+        done.append(pltpu.make_async_copy(out.at[at], out_any.at[at], out_sems.at[p]))
+        done[-1].start()
+    for part in done:
+        part.wait()
+
+
+def diffuse_late(lists, counts, coef, early, ghosts):
     face_count, cells = coef.shape
     ghost_rows = sum(g.shape[0] for g in ghosts)
     return pl.pallas_call(
-        functools.partial(late_kernel, face_count, cells, shift),
+        functools.partial(late_kernel, face_count, cells),
         out_shape=jax.ShapeDtypeStruct((cells, 2 * LANES), BF16),
-        in_specs=[smem(), vmem(), hbm()] + [hbm()] * len(ghosts),
-        out_specs=vmem(),
+        in_specs=[anywhere(), anywhere(), vmem(), hbm()] + [anywhere()] * len(ghosts),
+        out_specs=hbm(),
         scratch_shapes=[
+            pltpu.VMEM((cells, 2 * LANES), BF16),
             pltpu.VMEM((2 * cells + 16, LANES), F32),
             pltpu.VMEM((2 * ghost_rows, LANES), F32),
             pltpu.VMEM((len(ghosts),) + ghosts[0].shape, BF16),
-            pltpu.VMEM((face_count * cells // LANES, LANES), F32),
-            pltpu.SMEM((face_count * cells // LANES, LANES), F32),
+            pltpu.VMEM((face_count * cells // LANES + 8, LANES), F32),
+            pltpu.SMEM((face_count * cells // LANES + 8, LANES), F32),
+            pltpu.SMEM((face_count, LANES, LANES), I32),
+            pltpu.SMEM((8, LANES), I32),
             pltpu.SemaphoreType.DMA,
             pltpu.SemaphoreType.DMA((len(ghosts),)),
             pltpu.SemaphoreType.DMA,
+            pltpu.SemaphoreType.DMA((face_count,)),
+            pltpu.SemaphoreType.DMA,
+            pltpu.SemaphoreType.DMA((4,)),
         ],
-        compiler_params=pltpu.CompilerParams(vmem_limit_bytes=VMEM_MIB * MIB),
+        compiler_params=pltpu.CompilerParams(vmem_limit_bytes=LESS_VMEM_KIB * KIB),
         cost_estimate=pl.CostEstimate(flops=9_000_000_000, bytes_accessed=24 * MIB, transcendentals=0),
         name="diffuse_late",
-    )(lists, coef, early, *ghosts)
+    )(lists, counts, coef, early, *ghosts)
 
 
 def body(dust, classes, kernels, export_ids, faces, face_coef, mig_ids, mig_counts):
@@ -569,11 +698,11 @@
     g2, g3 = passed_along(left, "dy", 1), passed_along(right, "dy", -1)
     ghosts = (g0, g1, g2, g3)
     faces, face_coef, mig_ids, own = lax.optimization_barrier((faces, face_coef, mig_ids, own))
-    early = diffuse_early(faces, own, face_coef, 4 * export)
-    lists = late_lists(faces, shift, own)
-    leaving = diffuse_leaving(faces, mig_ids, mig_counts, own, ghosts, face_coef)
+    mig = mig_ids.T
+    early, mig_sums, mig_coef, mig_late, lists, list_counts = diffuse_early(faces, mig, own, face_coef, 4 * export, shift)
+    leaving = diffuse_leaving(mig_late, mig_counts, mig_sums, mig_coef, ghosts, face_coef.shape[0])
     arrived = lax.all_to_all(leaving.reshape(domains, capacity, row_width), ("dx", "dy"), split_axis=0, concat_axis=0, tiled=True)
-    updated = diffuse_late(lists.reshape(-1), face_coef, early, ghosts, shift)
+    updated = diffuse_late(lists, list_counts, face_coef, early, ghosts)
     return (updated, arrived.reshape(domains * capacity, row_width))
 
 

time: 87.8 us -> 75.9 us (0.86)
  Pallas kernels: 72.1 us -> 62.8 us
  local copies, waits for them, and re-layouts: 3.3 us -> 0.7 us
    pallas_call x3 -> x2, Pallas kernels: 29.5 us -> 15.8 us  [the longest x1 10.4 us: diffuse_late(): pl.pallas_call(functools.partial(late_kernel, face_count, cells), out_sha...]
    pallas_call x1, Pallas kernels: 22.1 us -> 26.6 us  [diffuse_early(): pl.pallas_call(functools.partial(early_kernel, face_count, cells, late_ro...]
    unnamed x11 -> x1, local copies, waits for them, and re-layouts: 2.63 us -> 0.7 us
  transfers between devices with their start and end apart: 5 -> 5, of which waited for: 0 -> 1; matrix products, arithmetic and copies ran while one was open for 1% -> 0% of each run, Pallas kernels for 50% -> 49%
where the time goes in v3:
time: 75.9 us; the launch traced here: 75.5 us
  Pallas kernels  62.8 us (83%)
  starting transfers between devices  11.1 us (15%)
    pallas_call x1, Pallas kernels, diffuse_early(): pl.pallas_call(functools.partial(early_kernel, face_count, cells, late_ro...  26.6 us
    pallas_call x1, Pallas kernels, own_cells(): pl.pallas_call(functools.partial(own_kernel, cells), out_shape=(jax.Shape...  20.3 us
    pallas_call x1, Pallas kernels, diffuse_late(): pl.pallas_call(functools.partial(late_kernel, face_count, cells), out_sha...  10.4 us
    ppermute x4, starting transfers between devices, passed_along(): return lax.ppermute(block, axis, route)  7.82 us
    pallas_call x1, Pallas kernels, diffuse_leaving(): pl.pallas_call(functools.partial(leave_kernel, face_count), out_shape=jax...  5.42 us
    all_to_all x1, starting transfers between devices, body(): lax.all_to_all(leaving.reshape(domains, capacity, row_width), ('dx', 'dy'...  3.31 us
  transfers between devices with their start and end apart: 5, of which 1 were waited for; matrix products, arithmetic and copies ran while one was open for 0% of the time, Pallas kernels for 49%

profile of v3, /device:TPU:0, one launch (start us, length us, event | category | flops | bytes accessed | tf_op | source)
XLA Modules:
  0.0 75.5 jit_solution(2741968845298543179)
XLA Ops:
  0.6 20.3 %coagulate_own.1 = (f32[8192,128]{1,0:T(8,128)}, bf16[1024,256]{1,0:T(8,128)(2,1)}, bf16[1024,256]{1,0:T(8,128)(2,1)}, bf16[1024,256]{1,0:T(8,128)(2,1)}, bf16[1024,256]{1,0:T(8,128)(2,1)}) custom-call(s32[32,128]{1,0:T(8,128)} %bitcast.6, s32[1,4,1024]{2,1,0:T(4,128)} %exp_ref.1, bf16[4096,256]{1,0:T(8,128)(2,1)} %dust_any.1, bf16[8,2,128,128]{3,2,1,0:T(8,128)(2,1)} %kern_any.1), custom_call_target="tpu_custom_call" | custom-call | flops 8999999488 | bytes 12582912 | tf_op jit(solution)/shard_map/coagulate_own/pallas_call | solution.py:251
  21.0 3.1 %collective-permute-start = (bf16[1024,256]{1,0:T(8,128)(2,1)}, bf16[1024,256]{1,0:T(8,128)(2,1)}, u32[]{:S(2)}, u32[]{:S(2)}) collective-permute-start(bf16[1024,256]{1,0:T(8,128)(2,1)} %get-tuple-element.25), channel_id=1, source_target_pairs={{24,0},{0,8},{8,16},{16,24},{25,1},{1,9},{9,17},{17,25},{26,2},{2,... | collective-permute-start | bytes 1572872 | tf_op jit(solution)/shard_map/ppermute | solution.py:29
  24.1 2.1 %collective-permute-start.1 = (bf16[1024,256]{1,0:T(8,128)(2,1)}, bf16[1024,256]{1,0:T(8,128)(2,1)}, u32[]{:S(2)}, u32[]{:S(2)}) collective-permute-start(bf16[1024,256]{1,0:T(8,128)(2,1)} %get-tuple-element.26), channel_id=1, source_target_pairs={{8,0},{16,8},{24,16},{0,24},{9,1},{17,9},{25,17},{1,25},{10,2},{18... | collective-permute-start | bytes 1572872 | tf_op jit(solution)/shard_map/ppermute | solution.py:29
  26.2 0.0 collective-permute-start.2
  26.2 2.6 %collective-permute-start.3 = (bf16[1024,256]{1,0:T(8,128)(2,1)}, bf16[1024,256]{1,0:T(8,128)(2,1)}, u32[]{:S(2)}, u32[]{:S(2)}) collective-permute-start(bf16[1024,256]{1,0:T(8,128)(2,1)} %get-tuple-element.28), channel_id=1, source_target_pairs={{1,0},{2,1},{3,2},{4,3},{5,4},{6,5},{7,6},{0,7},{9,8},{10,9},{11,1... | collective-permute-start | bytes 1572872 | tf_op jit(solution)/shard_map/ppermute | solution.py:29
  28.8 26.6 %diffuse_early.1 = (f32[8192,128]{1,0:T(8,128)}, f32[1024,128]{1,0:T(8,128)}, f32[512,8]{1,0:T(8,128)}, s32[24,128]{1,0:T(8,128)}, s32[768,128]{1,0:T(8,128)}, /*index=5*/s32[8,128]{1,0:T(8,128)}) custom-call(s32[6,4096]{1,0:T(8,128)} %faces, s32[16,32]{1,0:T(8,128)} %bitcast.7, f32[8192,128]{1,0:T(8,128)} %get-tuple-element.20.own, f32[6,4096]{1,0:T(8,128)} %coef.1), custom_call_target="tpu_custom_call" | custom-call | flops 20000000000 | bytes 16777216 | tf_op jit(solution)/shard_map/diffuse_early/pallas_call | solution.py:478
  55.4 0.0 collective-permute-done.g0
  55.4 0.0 collective-permute-done.1.g1
  55.4 0.0 collective-permute-done.2.g2
  55.4 0.0 collective-permute-done.3.g3
  55.5 5.4 %diffuse_leaving.1 = bf16[512,256]{1,0:T(8,128)(2,1)} custom-call(s32[24,128]{1,0:T(8,128)} %get-tuple-element.29.late_any, s32[1,32]{1,0:T(1,128)} %counts.1, f32[1024,128]{1,0:T(8,128)} %get-tuple-element.30.sums_any, f32[512,8]{1,0:T(8,128)} %get-tuple-element.31.coef_any, bf16[1024,256]{1,0:T(8,128)(2,1)} %collective-permute-done.g0, ...), custom_call_target="tpu_custom_call" | custom-call | flops 500000000 | bytes 8388608 | tf_op jit(solution)/shard_map/diffuse_leaving/pallas_call | solution.py:566
  60.9 3.3 %all-to-all-start = ((bf16[32,16,256]{2,1,0:T(8,128)(2,1)}), bf16[32,16,256]{2,1,0:T(8,128)(2,1)S(1)}, u32[]{:S(2)}, u32[]{:S(2)}) async-start(bf16[32,16,256]{2,1,0:T(8,128)(2,1)} %bitcast.5), calls=%async_computation | async-start | bytes 524288 | tf_op jit(solution)/shard_map/all_to_all | solution.py:704
  64.2 10.4 %diffuse_late.1 = bf16[4096,256]{1,0:T(8,128)(2,1)} custom-call(s32[768,128]{1,0:T(8,128)} %get-tuple-element.22.lists, s32[8,128]{1,0:T(8,128)} %get-tuple-element.23.counts, f32[6,4096]{1,0:T(8,128)} %coef.1, f32[8192,128]{1,0:T(8,128)} %get-tuple-element.24.early, bf16[1024,256]{1,0:T(8,128)(2,1)} %collective-permute-done.g0, ...), custom_call_target="tpu_custom_call" | custom-call | flops 8999999488 | bytes 25165824 | tf_op jit(solution)/shard_map/diffuse_late/pallas_call | solution.py:663
  74.6 0.2 all-to-all-done
  74.8 0.7 copy.11
Async XLA Ops:
  21.0 34.4 %collective-permute-start = (bf16[1024,256]{1,0:T(8,128)(2,1)}, bf16[1024,256]{1,0:T(8,128)(2,1)}, u32[]{:S(2)}, u32[]{:S(2)}) collective-permute-start(bf16[1024,256]{1,0:T(8,128)(2,1)} %get-tuple-element.25), channel_id=1, source_target_pairs={{24,0},{0,8},{8,16},{16,24},{25,1},{1,9},{9,17},{17,25},{26,2},{2,... | collective-permute-start | bytes 1572872 | tf_op jit(solution)/shard_map/ppermute | solution.py:29
  24.1 31.4 %collective-permute-start.1 = (bf16[1024,256]{1,0:T(8,128)(2,1)}, bf16[1024,256]{1,0:T(8,128)(2,1)}, u32[]{:S(2)}, u32[]{:S(2)}) collective-permute-start(bf16[1024,256]{1,0:T(8,128)(2,1)} %get-tuple-element.26), channel_id=1, source_target_pairs={{8,0},{16,8},{24,16},{0,24},{9,1},{17,9},{25,17},{1,25},{10,2},{18... | collective-permute-start | bytes 1572872 | tf_op jit(solution)/shard_map/ppermute | solution.py:29
  26.2 29.3 %collective-permute-start.2 = (bf16[1024,256]{1,0:T(8,128)(2,1)}, bf16[1024,256]{1,0:T(8,128)(2,1)}, u32[]{:S(2)}, u32[]{:S(2)}) collective-permute-start(bf16[1024,256]{1,0:T(8,128)(2,1)} %get-tuple-element.27), channel_id=1, source_target_pairs={{7,0},{0,1},{1,2},{2,3},{3,4},{4,5},{5,6},{6,7},{15,8},{8,9},{9,10... | collective-permute-start | bytes 1572872 | tf_op jit(solution)/shard_map/ppermute | solution.py:29
  26.2 29.3 %collective-permute-start.3 = (bf16[1024,256]{1,0:T(8,128)(2,1)}, bf16[1024,256]{1,0:T(8,128)(2,1)}, u32[]{:S(2)}, u32[]{:S(2)}) collective-permute-start(bf16[1024,256]{1,0:T(8,128)(2,1)} %get-tuple-element.28), channel_id=1, source_target_pairs={{1,0},{2,1},{3,2},{4,3},{5,4},{6,5},{7,6},{0,7},{9,8},{10,9},{11,1... | collective-permute-start | bytes 1572872 | tf_op jit(solution)/shard_map/ppermute | solution.py:29
  60.9 13.9 %all-to-all-start = ((bf16[32,16,256]{2,1,0:T(8,128)(2,1)}), bf16[32,16,256]{2,1,0:T(8,128)(2,1)S(1)}, u32[]{:S(2)}, u32[]{:S(2)}) async-start(bf16[32,16,256]{2,1,0:T(8,128)(2,1)} %bitcast.5), calls=%async_computation | async-start | bytes 524288 | tf_op jit(solution)/shard_map/all_to_all | solution.py:704

commit v4 on v3

--- a/solution.py
+++ b/solution.py
@@ -13,7 +13,7 @@
 TILE = 576
 CHUNK = 16
 BATCH = 32
-FIRST_LINES = 16
+FIRST_LINES = 4
 F32 = jnp.float32
 BF16 = jnp.bfloat16
 I32 = jnp.int32
@@ -110,7 +110,7 @@
     return one.astype(BF16), two.astype(BF16)
 
 
-def send_rows(ids, steps, table, outbound, stages):
+def send_rows(ids, steps, table, outbound, sent, sems, stages):
     span = LANES
     lines = ids.shape[0]
 
@@ -127,7 +127,8 @@
 
     pull(0, stages[0])
     first = 0
-    for block in outbound:
+    copies = []
+    for number, block in enumerate(outbound):
         spans = block.shape[0] // span
 
         def pair(i, carry):
@@ -139,10 +140,14 @@
 
         lax.fori_loop(0, spans // 2, pair, 0)
         first += spans
-
-
-def own_kernel(cells, cls_ref, exp_ref, dust_any, kern_any, out_any, out_up, out_down, out_left, out_right,
-               out, dust, kern, sorted_rows, weights, places_v, places, exp_v, exp_s, stage_a, stage_b, sem, dust_sems, kern_sem, exp_sem):
+        copies.append(pltpu.make_async_copy(block, sent[number], sems.at[number]))
+        copies[-1].start()
+    for copy in copies:
+        copy.wait()
+
+
+def own_kernel(cells, cls_ref, exp_ref, dust_any, kern_any, out_any, any_up, any_down, any_left, any_right, out_up, out_down,
+               out_left, out_right, send_sems, out, dust, kern, sorted_rows, weights, places_v, places, exp_v, exp_s, stage_a, stage_b, sem, dust_sems, kern_sem, exp_sem):
     class_count = kern.shape[0]
     rows = cells // LANES
     parts = dust_sems.shape[0]
@@ -221,7 +226,8 @@
     lax.fori_loop(0, rows, gather, 0)
     out_copy = pltpu.make_async_copy(out, out_any, sem)
     out_copy.start()
-    send_rows(exp_s, steps, out, (out_up, out_down, out_left, out_right), (stage_a, stage_b))
+    send_rows(exp_s, steps, out, (out_up, out_down, out_left, out_right), (any_up, any_down, any_left, any_right), send_sems,
+              (stage_a, stage_b))
     out_copy.wait()
 
 
@@ -252,8 +258,13 @@
         functools.partial(own_kernel, cells),
         out_shape=(jax.ShapeDtypeStruct((2 * cells, LANES), F32), block, block, block, block),
         in_specs=[vmem(), vmem(), hbm(), hbm()],
-        out_specs=(hbm(), vmem(), vmem(), vmem(), vmem()),
+        out_specs=(hbm(), hbm(), hbm(), hbm(), hbm()),
         scratch_shapes=[
+            pltpu.VMEM(block.shape, BF16),
+            pltpu.VMEM(block.shape, BF16),
+            pltpu.VMEM(block.shape, BF16),
+            pltpu.VMEM(block.shape, BF16),
+            pltpu.SemaphoreType.DMA((4,)),
             pltpu.VMEM((2 * cells, LANES), F32),
             pltpu.VMEM((cells, 2 * LANES), BF16),
             pltpu.VMEM(kernels.shape, BF16),
@@ -289,25 +300,33 @@
     return one, two
 
 
-def turn_columns(coef, coef8, columns):
-    together = 4
-    if coef is not None:
-        coef8[0:coef.shape[0], :] = coef[...]
+def turn_columns(coef, late, both, columns):
+    together = 2
+    padded = both.shape[0] // 2
+    both[0:coef.shape[0], :] = coef[...]
+    both[padded:padded + coef.shape[0], :] = late
 
     def turn(b, carry):
         for u in range(together):
             at = pl.ds(pl.multiple_of((b * together + u) * LANES, LANES), LANES)
-            columns[at, :] = coef8[:, at].T
+            columns[at, :] = both[:, at].T
         return carry
 
     lax.fori_loop(0, columns.shape[0] // (LANES * together), turn, 0)
 
 
-def start_faces(faces, faces_v, faces_s, sem):
+def start_faces(faces, faces_v, faces_s, sems):
     lines_of(faces, faces_v, 2)
-    copy = pltpu.make_async_copy(faces_v, faces_s, sem)
-    copy.start()
-    return copy
+    per_face = faces.shape[1] // LANES
+    parts = sems.shape[0]
+    copies = []
+    for p in range(parts):
+        copies.append([])
+        for f in range(faces.shape[0]):
+            at = pl.ds(f * per_face + p * (per_face // parts), per_face // parts)
+            copies[p].append(pltpu.make_async_copy(faces_v.at[at], faces_s.at[at], sems.at[p, f]))
+            copies[p][f].start()
+    return copies
 
 
 def start_ghosts(ghosts, landed, sems):
@@ -324,98 +343,78 @@
         spread_rows(landed.at[k], table, first + k * landed.shape[1], landed.shape[1])
 
 
-def late_lists(face_count, cells, shift, out, counts, lines):
+def late_lists(face_count, cells, out, out_coef, counts, lines, coef_lines):
     per_face = cells // LANES
-    blocks = per_face // 8
-    lane, sub = iota2((8, LANES), 1), iota2((8, LANES), 0)
-    words = []
+    every = face_count * per_face
+    shift = per_face.bit_length() - 1
+    to = lines[...]
+    late = (to >= 2 * cells).astype(F32)
+    late16 = late.astype(BF16)
+    before = (iota2((LANES, LANES), 0) < iota2((LANES, LANES), 1)).astype(F32).astype(BF16)
+    line_total = dot(late16, jnp.ones((LANES, LANES), BF16)).astype(BF16)
+    a, b = iota2((every, every), 0), iota2((every, every), 1)
+    earlier = jnp.logical_and((a >> shift) == (b >> shift), b < a).astype(F32).astype(BF16)
+    line_start = dot(earlier, line_total)
+    rank = (dot(late16, before) + line_start).astype(I32)
+    place = (iota2((every, LANES), 0) & (per_face - 1)) * LANES + iota2((every, LANES), 1)
+    ahead = jnp.where(to >= 2 * cells, place - rank, 0)
+    lane = iota2((per_face, LANES), 1)
+    where = iota2((per_face, LANES), 0) * LANES + lane
+
+    def from_right(x, digit):
+        if digit >= 7:
+            return pltpu.roll(x, per_face - (1 << (digit - 7)), 0)
+        near = pltpu.roll(x, LANES - (1 << digit), 1)
+        return jnp.where(lane < LANES - (1 << digit), near, pltpu.roll(near, per_face - 1, 0))
+
     for f in range(face_count):
-        number = None
-        words.append([])
-        for v in range(blocks):
-            first = f * per_face + v * 8
-            to = lines[first:first + 8, :]
-            late = to >= 2 * cells
-            cell = (sub + v * 8) * LANES + lane
-            words[f].append(jnp.where(late, (cell << shift) + (to - 2 * cells), cells << shift))
-            counted = late.astype(F32)
-            number = counted if number is None else number + counted
-        number = jnp.sum(number, keepdims=True).astype(I32)
-        counts[f:f + 1, :] = jnp.broadcast_to(number, (1, LANES))
-    block_bits = blocks.bit_length() - 1
-
-    def bit(b, v):
-        if b < block_bits:
-            return bool((v >> b) & 1)
-        if b < block_bits + 3:
-            return ((sub >> (b - block_bits)) & 1) == 1
-        if b < block_bits + 3 + 7:
-            return ((lane >> (b - block_bits - 3)) & 1) == 1
-        return False
-
-    def pick(where_true, a, b):
-        if isinstance(where_true, bool):
-            return a if where_true else b
-        return jnp.where(where_true, a, b)
-
-    def same(a, b):
-        if isinstance(a, bool) and isinstance(b, bool):
-            return a == b
-        if isinstance(a, bool):
-            a, b = b, a
-        if isinstance(b, bool):
-            return a if b else jnp.logical_not(a)
-        return jnp.logical_not(jnp.logical_xor(a, b))
-
-    bits = cells.bit_length() - 1
-    for size_bit in range(1, bits + 1):
-        for b in range(size_bit - 1, -1, -1):
-            for v in range(blocks):
-                if b < block_bits and bit(b, v):
-                    continue
-                down = bit(size_bit, v)
-                if b >= block_bits:
-                    high = bit(b, v)
-                    largest = jnp.logical_not(same(high, down)) if not isinstance(down, bool) else same(high, not down)
-                for f in range(face_count):
-                    x = words[f][v]
-                    if b < block_bits:
-                        w = v ^ (1 << b)
-                        y = words[f][w]
-                        least, most = jnp.minimum(x, y), jnp.maximum(x, y)
-                        words[f][v] = pick(down, most, least)
-                        words[f][w] = pick(down, least, most)
-                        continue
-                    axis, by, length = (0, 1 << (b - block_bits), 8)
-                    if b >= block_bits + 3:
-                        axis, by, length = (1, 1 << (b - block_bits - 3), LANES)
-                    other = pltpu.roll(x, by, axis)
-                    if 2 * by < length:
-                        other = jnp.where(high, other, pltpu.roll(x, length - by, axis))
-                    words[f][v] = pick(largest, jnp.maximum(x, other), jnp.minimum(x, other))
-    for f in range(face_count):
-        word = jnp.concatenate(words[f], axis=0)
-        both = jnp.concatenate([word >> shift, word & ((1 << shift) - 1)], axis=0)
-        out[f * LANES:(f + 1) * LANES, 0:2 * per_face] = both.T
-
-
-def early_kernel(face_count, cells, late_rows, shift, faces, mig, own, coef, out_any, mig_sums, mig_coef, mig_late, lists, counts,
-                 out, table,
-                 stage_a, stage_b, coef8, columns, late8, late_columns, mig_columns, faces_v, faces_s, sem, face_sem, out_sems):
+        at = slice(f * per_face, (f + 1) * per_face)
+        last = (f + 1) * per_face - 1
+        number = (line_start[last:last + 1, :] + line_total[last:last + 1, :].astype(F32)).astype(I32)
+        counts[f:f + 1, :] = number
+        word = (where << 14) + (to[at] - 2 * cells)
+        move = ahead[at]
+        weight = coef_lines[at]
+        for digit in range(cells.bit_length() - 1):
+            next_word, next_move = from_right(word, digit), from_right(move, digit)
+            takes = ((next_move >> digit) & 1) == 1
+            word = jnp.where(takes, next_word, word)
+            weight = jnp.where(takes, from_right(weight, digit), weight)
+            move = jnp.where(takes, next_move, jnp.where(((move >> digit) & 1) == 1, 0, move))
+        used = where < number
+        of_cells = jnp.where(used, (word >> 14) * 2, 2 * cells)
+        out_coef[at, :] = jnp.where(used, weight, 0.0)
+        of_rows = jnp.where(used, word & ((1 << 14) - 1), 0)
+        start = 2 * f * per_face
+        rest = per_face - FIRST_LINES
+        out[start:start + FIRST_LINES, :] = of_cells[:FIRST_LINES]
+        out[start + FIRST_LINES:start + 2 * FIRST_LINES, :] = of_rows[:FIRST_LINES]
+        out[start + 2 * FIRST_LINES:start + 2 * FIRST_LINES + rest, :] = of_cells[FIRST_LINES:]
+        out[start + 2 * FIRST_LINES + rest:start + 2 * per_face, :] = of_rows[FIRST_LINES:]
+
+
+def early_kernel(face_count, cells, late_rows, faces_any, mig, mig_counts, own, coef_any, out_any, mig_sums, mig_coef, mig_late, lists,
+                 list_coef, counts, out, faces, coef, coef_v, input_sems, table,
+                 stage_a, stage_b, both, columns, faces_v, faces_s, sem, face_sem, out_sems):
+    inputs = [pltpu.make_async_copy(faces_any, faces, input_sems.at[0]), pltpu.make_async_copy(coef_any, coef, input_sems.at[1])]
+    for one in inputs:
+        one.start()
     copy = pltpu.make_async_copy(own, table.at[pl.ds(0, 2 * cells)], sem)
     copy.start()
-    face_copy = start_faces(faces, faces_v, faces_s, face_sem)
+    for one in inputs:
+        one.wait()
+    face_copies = start_faces(faces, faces_v, faces_s, face_sem)
 
     def clear(i, carry):
         table[pl.ds(pl.multiple_of(2 * cells + i * 256, 256), 256), :] = jnp.zeros((256, LANES), F32)
         return carry
 
     lax.fori_loop(0, 2 * late_rows // 256, clear, 0)
-    turn_columns(coef, coef8, columns)
-    late8[0:face_count, :] = jnp.where(faces[...] >= cells, 2 * (faces[...] - cells), 2 * late_rows)
-    turn_columns(None, late8, late_columns)
-    late_lists(face_count, cells, shift, lists, counts, faces_v)
-    face_copy.wait()
+    turn_columns(coef, jnp.where(faces[...] >= cells, 2 * (faces[...] - cells), 2 * late_rows).astype(F32), both, columns)
+    lines_of(coef, coef_v, 1.0)
+    late_lists(face_count, cells, lists, list_coef, counts, faces_v, coef_v)
+    for part in face_copies[0]:
+        part.wait()
     flat = faces_s.reshape(face_count * cells)
     steps = small_numbers(faces_s[0, 0])
     copy.wait()
@@ -447,6 +446,9 @@
     parts = out_sems.shape[0]
     done = []
     for p in range(parts):
+        if p + 1 < parts:
+            for part in face_copies[p + 1]:
+                part.wait()
         lax.fori_loop(p * (chunks // 2 // parts), (p + 1) * (chunks // 2 // parts), pair, 0)
         at = pl.ds(p * (2 * cells // parts), 2 * cells // parts)
         done.append(pltpu.make_async_copy(out.at[at], out_any.at[at], out_sems.at[p]))
@@ -458,58 +460,62 @@
             at = i * CHUNK + u
             mig_sums[rows2(2 * at), :] = out[rows2(2 * cell), :]
             mig_coef[pl.ds(at, 1), :] = columns[pl.ds(cell, 1), :]
-            mig_columns[pl.ds(at, 1), :] = late_columns[pl.ds(cell, 1), :]
         return carry
 
     lax.fori_loop(0, mig.shape[1], leaving, 0)
-    lines = mig_columns.shape[0] // LANES
+    lines = mig_coef.shape[0] // LANES
+    padded = both.shape[0] // 2
     for i in range(lines):
-        turned = mig_columns[i * LANES:(i + 1) * LANES, :].T
+        turned = mig_coef[i * LANES:(i + 1) * LANES, :].T.astype(I32)
         for f in range(face_count):
-            mig_late[f * lines + i:f * lines + i + 1, :] = turned[f:f + 1, :]
+            mig_late[f * lines + i:f * lines + i + 1, :] = turned[padded + f:padded + f + 1, :]
+    last = face_count * lines
+    mig_late[last:last + 1, 0:mig_counts.shape[1]] = mig_counts[...]
     for part in done:
         part.wait()
 
 
-def diffuse_early(faces, mig, own, coef, late_rows, shift):
+def diffuse_early(faces, mig, counts, own, coef, late_rows):
     face_count, cells = coef.shape
     padded = face_count + -face_count % 8
     leaving = mig.shape[0] * mig.shape[1]
     return pl.pallas_call(
-        functools.partial(early_kernel, face_count, cells, late_rows, shift),
+        functools.partial(early_kernel, face_count, cells, late_rows),
         out_shape=(
             jax.ShapeDtypeStruct((2 * cells, LANES), F32),
             jax.ShapeDtypeStruct((2 * leaving, LANES), F32),
-            jax.ShapeDtypeStruct((leaving, padded), F32),
-            jax.ShapeDtypeStruct((face_count * leaving // LANES, LANES), I32),
-            jax.ShapeDtypeStruct((face_count * LANES, LANES), I32),
+            jax.ShapeDtypeStruct((leaving, 2 * padded), F32),
+            jax.ShapeDtypeStruct((face_count * leaving // LANES + 8, LANES), I32),
+            jax.ShapeDtypeStruct((2 * face_count * cells // LANES, LANES), I32),
+            jax.ShapeDtypeStruct((face_count * cells // LANES, LANES), F32),
             jax.ShapeDtypeStruct((8, LANES), I32),
         ),
-        in_specs=[vmem(), smem(), hbm(), vmem()],
-        out_specs=(hbm(), vmem(), vmem(), vmem(), vmem(), vmem()),
+        in_specs=[hbm(), smem(), vmem(), hbm(), hbm()],
+        out_specs=(hbm(), vmem(), vmem(), vmem(), vmem(), vmem(), vmem()),
         scratch_shapes=[
             pltpu.VMEM((2 * cells, LANES), F32),
+            pltpu.VMEM((face_count, cells), I32),
+            pltpu.VMEM((face_count, cells), F32),
+            pltpu.VMEM((face_count * cells // LANES, LANES), F32),
+            pltpu.SemaphoreType.DMA((2,)),
             pltpu.VMEM((2 * (cells + late_rows), LANES), F32),
             pltpu.VMEM((2 * face_count * CHUNK, LANES), F32),
             pltpu.VMEM((2 * face_count * CHUNK, LANES), F32),
-            pltpu.VMEM((padded, cells), F32),
-            pltpu.VMEM((cells, padded), F32),
-            pltpu.VMEM((padded, cells), I32),
-            pltpu.VMEM((cells, padded), I32),
-            pltpu.VMEM((leaving, padded), I32),
+            pltpu.VMEM((2 * padded, cells), F32),
+            pltpu.VMEM((cells, 2 * padded), F32),
             pltpu.VMEM((face_count * cells // LANES, LANES), I32),
             pltpu.SMEM((face_count * cells // LANES, LANES), I32),
             pltpu.SemaphoreType.DMA,
-            pltpu.SemaphoreType.DMA,
+            pltpu.SemaphoreType.DMA((4, face_count)),
             pltpu.SemaphoreType.DMA((4,)),
         ],
         compiler_params=pltpu.CompilerParams(vmem_limit_bytes=VMEM_KIB * KIB),
         cost_estimate=pl.CostEstimate(flops=20_000_000_000, bytes_accessed=16 * MIB, transcendentals=0),
         name="diffuse_early",
-    )(faces, mig, own, coef)
-
-
-def leave_kernel(face_count, late_any, counts, sums_any, coef_any, g0, g1, g2, g3, out, table, landed, stage_a, stage_b,
+    )(faces, mig, counts, own, coef)
+
+
+def leave_kernel(face_count, late_any, sums_any, coef_any, g0, g1, g2, g3, out, table, landed, stage_a, stage_b,
                  late_s, mig_sums, mig_coef, late_sem, sums_sem, coef_sem, ghost_sems):
     ghost_copies = start_ghosts((g0, g1, g2, g3), landed, ghost_sems)
     copies = [
@@ -525,7 +531,7 @@
     for copy in copies:
         copy.wait()
     cells = out.shape[0]
-    mig_late = late_s.reshape(face_count * cells)
+    mig_late = late_s.reshape(late_s.shape[0] * LANES)
     steps = small_numbers(late_s[0, 0])
     chunks = cells // CHUNK
 
@@ -545,7 +551,7 @@
             c = jnp.broadcast_to(weights[:, f:f + 1], (CHUNK, LANES))
             one = one + c * stage[pl.ds(2 * f * CHUNK, CHUNK, stride=2), :]
             two = two + c * stage[pl.ds(2 * f * CHUNK + 1, CHUNK, stride=2), :]
-        keep = iota2((CHUNK, LANES), 0) < counts[0, i]
+        keep = iota2((CHUNK, LANES), 0) < mig_late[face_count * cells + i]
         out[here, 0:LANES] = jnp.where(keep, one, 0.0).astype(BF16)
         out[here, LANES:2 * LANES] = jnp.where(keep, two, 0.0).astype(BF16)
 
@@ -561,12 +567,12 @@
     lax.fori_loop(0, chunks // 2, pair, 0)
 
 
-def diffuse_leaving(mig_late, counts, mig_sums, mig_coef, ghosts, face_count):
+def diffuse_leaving(mig_late, mig_sums, mig_coef, ghosts, face_count):
     ghost_rows = sum(g.shape[0] for g in ghosts)
     return pl.pallas_call(
         functools.partial(leave_kernel, face_count),
         out_shape=jax.ShapeDtypeStruct((mig_coef.shape[0], 2 * LANES), BF16),
-        in_specs=[anywhere(), smem(), anywhere(), anywhere()] + [anywhere()] * 4,
+        in_specs=[anywhere()] * 7,
         out_specs=vmem(),
         scratch_shapes=[
             pltpu.VMEM((2 * ghost_rows + 8, LANES), F32),
@@ -584,11 +590,11 @@
         compiler_params=pltpu.CompilerParams(vmem_limit_bytes=VMEM_KIB * KIB),
         cost_estimate=pl.CostEstimate(flops=500_000_000, bytes_accessed=8 * MIB, transcendentals=0),
         name="diffuse_leaving",
-    )(mig_late, counts, mig_sums, mig_coef, *ghosts)
-
-
-def late_kernel(face_count, cells, lists, counts, coef, early, g0, g1, g2, g3, out_any, out, sums, table, landed, coef_v, coef_s,
-                lists_s, counts_s, sem, ghost_sems, coef_sem, list_sems, count_sem, out_sems):
+    )(mig_late, mig_sums, mig_coef, *ghosts)
+
+
+def late_kernel(face_count, cells, lists, list_coef, counts, early, g0, g1, g2, g3, out_any, out, sums, table, landed, lists_s,
+                coef_s, counts_s, sem, ghost_sems, coef_sems, list_sems, count_sem, out_sems):
     ghost_copies = start_ghosts((g0, g1, g2, g3), landed, ghost_sems)
     copy = pltpu.make_async_copy(early, sums.at[pl.ds(0, 2 * cells)], sem)
     copy.start()
@@ -596,47 +602,67 @@
     count_copy.start()
     list_copies = []
     for f in range(face_count):
-        part = pltpu.make_async_copy(lists.at[pl.ds(f * LANES, FIRST_LINES)], lists_s.at[f, pl.ds(0, FIRST_LINES)], list_sems.at[f])
+        first = pl.ds(2 * f * cells // LANES, 2 * FIRST_LINES)
+        part = pltpu.make_async_copy(lists.at[first], lists_s.at[f, pl.ds(0, 2 * FIRST_LINES)], list_sems.at[f])
         part.start()
         list_copies.append(part)
-    lines_of(coef, coef_v, 1.0)
-    coef_copy = pltpu.make_async_copy(coef_v, coef_s, coef_sem)
-    coef_copy.start()
+        first = pl.ds(f * cells // LANES, 2 * FIRST_LINES)
+        part = pltpu.make_async_copy(list_coef.at[first], coef_s.at[f, pl.ds(0, 2 * FIRST_LINES)], coef_sems.at[f])
+        part.start()
+        list_copies.append(part)
     spread_ghosts(ghost_copies, landed, table, 0)
     count_copy.wait()
     steps = small_numbers(counts_s[0, 0])
     for part in list_copies:
         part.wait()
-    coef_copy.wait()
-    flat = coef_s.reshape(coef_s.shape[0] * LANES)
     copy.wait()
     for f in range(face_count):
-        weights = flat.at[pl.ds(f * cells, cells + LANES)]
         number = counts_s[f, 0]
 
-        @pl.when(number > FIRST_LINES * BATCH)
+        per_line = LANES // BATCH
+        line_shift = per_line.bit_length() - 1
+        split = FIRST_LINES * per_line
+        rest = 2 * cells // LANES - 2 * FIRST_LINES
+
+        def add(cell_line, row_line, coef_line, lane):
+            for j in range(BATCH // GROUP):
+                found = []
+                of_cells = lists_s.at[f, cell_line, pl.ds(lane + j * GROUP, GROUP)]
+                of_rows = lists_s.at[f, row_line, pl.ds(lane + j * GROUP, GROUP)]
+                weights = coef_s.at[f, coef_line, pl.ds(lane + j * GROUP, GROUP)]
+                for k in range(GROUP):
+                    row = rows2(of_cells[steps[k]])
+                    late = table[rows2(of_rows[steps[k]]), :]
+                    found.append((row, sums[row, :] + weights[steps[k]] * late))
+                for row, value in found:
+                    sums[row, :] = value
+
+        def near(i, carry):
+            line = i >> line_shift
+            add(line, line + FIRST_LINES, line, (i & (per_line - 1)) * BATCH)
+            return carry
+
+        def far(i, carry):
+            line = (i >> line_shift) + FIRST_LINES
+            add(line, line + rest // 2, line - FIRST_LINES, (i & (per_line - 1)) * BATCH)
+            return carry
+
+        batches = (number + (BATCH - 1)) // BATCH
+        lax.fori_loop(0, jnp.minimum(batches, split), near, 0)
+
+        @pl.when(batches > split)
         def _():
-            rest = LANES - FIRST_LINES
-            more = pltpu.make_async_copy(
-                lists.at[pl.ds(f * LANES + FIRST_LINES, rest)], lists_s.at[f, pl.ds(FIRST_LINES, rest)], list_sems.at[f])
+            at = pl.ds(2 * f * cells // LANES + 2 * FIRST_LINES, rest)
+            more = pltpu.make_async_copy(lists.at[at], lists_s.at[f, pl.ds(2 * FIRST_LINES, rest)], list_sems.at[f])
             more.start()
             more.wait()
-
-        def some(i, carry):
-            for j in range(BATCH // GROUP):
-                found = []
-                of_cells = lists_s.at[f, i, pl.ds(j * GROUP, GROUP)]
-                of_rows = lists_s.at[f, i, pl.ds(BATCH + j * GROUP, GROUP)]
-                for k in range(GROUP):
-                    cell = of_cells[steps[k]]
-                    row = rows2(2 * cell)
-                    late = table[rows2(of_rows[steps[k]]), :]
-                    found.append((row, sums[row, :] + weights[cell] * late))
-                for row, value in found:
-                    sums[row, :] = value
-            return carry
-
-        lax.fori_loop(0, (number + (BATCH - 1)) // BATCH, some, 0)
+            rest_coef = cells // LANES - 2 * FIRST_LINES
+            at = pl.ds(f * cells // LANES + 2 * FIRST_LINES, rest_coef)
+            more = pltpu.make_async_copy(list_coef.at[at], coef_s.at[f, pl.ds(2 * FIRST_LINES, rest_coef)], coef_sems.at[f])
+            more.start()
+            more.wait()
+            lax.fori_loop(split, batches, far, 0)
+
     span = 256
 
     def pack(i, carry):
@@ -657,26 +683,25 @@
         part.wait()
 
 
-def diffuse_late(lists, counts, coef, early, ghosts):
-    face_count, cells = coef.shape
+def diffuse_late(lists, list_coef, counts, early, ghosts, face_count):
+    cells = early.shape[0] // 2
     ghost_rows = sum(g.shape[0] for g in ghosts)
     return pl.pallas_call(
         functools.partial(late_kernel, face_count, cells),
         out_shape=jax.ShapeDtypeStruct((cells, 2 * LANES), BF16),
-        in_specs=[anywhere(), anywhere(), vmem(), hbm()] + [anywhere()] * len(ghosts),
+        in_specs=[hbm(), hbm(), hbm(), hbm()] + [anywhere()] * len(ghosts),
         out_specs=hbm(),
         scratch_shapes=[
             pltpu.VMEM((cells, 2 * LANES), BF16),
             pltpu.VMEM((2 * cells + 16, LANES), F32),
             pltpu.VMEM((2 * ghost_rows, LANES), F32),
             pltpu.VMEM((len(ghosts),) + ghosts[0].shape, BF16),
-            pltpu.VMEM((face_count * cells // LANES + 8, LANES), F32),
-            pltpu.SMEM((face_count * cells // LANES + 8, LANES), F32),
-            pltpu.SMEM((face_count, LANES, LANES), I32),
+            pltpu.SMEM((face_count, 2 * cells // LANES, LANES), I32),
+            pltpu.SMEM((face_count, cells // LANES, LANES), F32),
             pltpu.SMEM((8, LANES), I32),
             pltpu.SemaphoreType.DMA,
             pltpu.SemaphoreType.DMA((len(ghosts),)),
-            pltpu.SemaphoreType.DMA,
+            pltpu.SemaphoreType.DMA((face_count,)),
             pltpu.SemaphoreType.DMA((face_count,)),
             pltpu.SemaphoreType.DMA,
             pltpu.SemaphoreType.DMA((4,)),
@@ -684,7 +709,7 @@
         compiler_params=pltpu.CompilerParams(vmem_limit_bytes=LESS_VMEM_KIB * KIB),
         cost_estimate=pl.CostEstimate(flops=9_000_000_000, bytes_accessed=24 * MIB, transcendentals=0),
         name="diffuse_late",
-    )(lists, counts, coef, early, *ghosts)
+    )(lists, list_coef, counts, early, *ghosts)
 
 
 def body(dust, classes, kernels, export_ids, faces, face_coef, mig_ids, mig_counts):
@@ -692,17 +717,16 @@
     export = export_ids.shape[2]
     domains = mig_counts.shape[1]
     capacity = mig_ids.shape[1]
-    shift = (8 * export - 1).bit_length()
     own, up, down, left, right = own_cells(dust, classes, kernels, export_ids)
     g0, g1 = passed_along(up, "dx", 1), passed_along(down, "dx", -1)
     g2, g3 = passed_along(left, "dy", 1), passed_along(right, "dy", -1)
     ghosts = (g0, g1, g2, g3)
     faces, face_coef, mig_ids, own = lax.optimization_barrier((faces, face_coef, mig_ids, own))
     mig = mig_ids.T
-    early, mig_sums, mig_coef, mig_late, lists, list_counts = diffuse_early(faces, mig, own, face_coef, 4 * export, shift)
-    leaving = diffuse_leaving(mig_late, mig_counts, mig_sums, mig_coef, ghosts, face_coef.shape[0])
+    early, mig_sums, mig_coef, mig_late, lists, list_coef, list_counts = diffuse_early(faces, mig, mig_counts, own, face_coef, 4 * export)
+    leaving = diffuse_leaving(mig_late, mig_sums, mig_coef, ghosts, face_coef.shape[0])
     arrived = lax.all_to_all(leaving.reshape(domains, capacity, row_width), ("dx", "dy"), split_axis=0, concat_axis=0, tiled=True)
-    updated = diffuse_late(lists, list_counts, face_coef, early, ghosts)
+    updated = diffuse_late(lists, list_coef, list_counts, early, ghosts, face_coef.shape[0])
     return (updated, arrived.reshape(domains * capacity, row_width))
 
 

time: 75.9 us -> 73.5 us (0.968)
  Pallas kernels: 62.8 us -> 59.7 us
    pallas_call x1, Pallas kernels: 26.6 us -> 25.3 us  [diffuse_early(): pl.pallas_call(functools.partial(early_kernel, face_count, cells, late_ro...]
  transfers between devices with their start and end apart: 5 -> 5, of which waited for: 1 -> 1; matrix products, arithmetic and copies ran while one was open for 0% -> 0% of each run, Pallas kernels for 49% -> 48%
where the time goes in v4:
time: 73.5 us; the launch traced here: 73 us
  Pallas kernels  59.7 us (81%)
  starting transfers between devices  11.1 us (15%)
  waiting for transfers between devices  0.79 us (1%)
    pallas_call x1, Pallas kernels, diffuse_early(): pl.pallas_call(functools.partial(early_kernel, face_count, cells, late_ro...  25.3 us
    pallas_call x1, Pallas kernels, own_cells(): pl.pallas_call(functools.partial(own_kernel, cells), out_shape=(jax.Shape...  19.9 us
    pallas_call x1, Pallas kernels, diffuse_late(): pl.pallas_call(functools.partial(late_kernel, face_count, cells), out_sha...  9.81 us
    ppermute x4, starting transfers between devices, passed_along(): return lax.ppermute(block, axis, route)  7.82 us
    pallas_call x1, Pallas kernels, diffuse_leaving(): pl.pallas_call(functools.partial(leave_kernel, face_count), out_shape=jax...  4.76 us
    all_to_all x1, starting transfers between devices, body(): lax.all_to_all(leaving.reshape(domains, capacity, row_width), ('dx', 'dy'...  3.31 us
  transfers between devices with their start and end apart: 5, of which 1 were waited for; matrix products, arithmetic and copies ran while one was open for 0% of the time, Pallas kernels for 48%

profile of v4, /device:TPU:0, one launch (start us, length us, event | category | flops | bytes accessed | tf_op | source)
XLA Modules:
  0.0 73.0 jit_solution(2634630272610076977)
XLA Ops:
  0.6 19.9 %coagulate_own.1 = (f32[8192,128]{1,0:T(8,128)}, bf16[1024,256]{1,0:T(8,128)(2,1)}, bf16[1024,256]{1,0:T(8,128)(2,1)}, bf16[1024,256]{1,0:T(8,128)(2,1)}, bf16[1024,256]{1,0:T(8,128)(2,1)}) custom-call(s32[32,128]{1,0:T(8,128)} %bitcast.6, s32[1,4,1024]{2,1,0:T(4,128)} %exp_ref.1, bf16[4096,256]{1,0:T(8,128)(2,1)} %dust_any.1, bf16[8,2,128,128]{3,2,1,0:T(8,128)(2,1)} %kern_any.1), custom_call_target="tpu_custom_call" | custom-call | flops 8999999488 | bytes 12582912 | tf_op jit(solution)/shard_map/coagulate_own/pallas_call | solution.py:257
  20.5 3.1 %collective-permute-start = (bf16[1024,256]{1,0:T(8,128)(2,1)}, bf16[1024,256]{1,0:T(8,128)(2,1)}, u32[]{:S(2)}, u32[]{:S(2)}) collective-permute-start(bf16[1024,256]{1,0:T(8,128)(2,1)} %get-tuple-element.27), channel_id=1, source_target_pairs={{24,0},{0,8},{8,16},{16,24},{25,1},{1,9},{9,17},{17,25},{26,2},{2,... | collective-permute-start | bytes 1572872 | tf_op jit(solution)/shard_map/ppermute | solution.py:29
  23.6 2.1 %collective-permute-start.1 = (bf16[1024,256]{1,0:T(8,128)(2,1)}, bf16[1024,256]{1,0:T(8,128)(2,1)}, u32[]{:S(2)}, u32[]{:S(2)}) collective-permute-start(bf16[1024,256]{1,0:T(8,128)(2,1)} %get-tuple-element.28), channel_id=1, source_target_pairs={{8,0},{16,8},{24,16},{0,24},{9,1},{17,9},{25,17},{1,25},{10,2},{18... | collective-permute-start | bytes 1572872 | tf_op jit(solution)/shard_map/ppermute | solution.py:29
  25.7 0.0 collective-permute-start.2
  25.7 2.6 %collective-permute-start.3 = (bf16[1024,256]{1,0:T(8,128)(2,1)}, bf16[1024,256]{1,0:T(8,128)(2,1)}, u32[]{:S(2)}, u32[]{:S(2)}) collective-permute-start(bf16[1024,256]{1,0:T(8,128)(2,1)} %get-tuple-element.30), channel_id=1, source_target_pairs={{1,0},{2,1},{3,2},{4,3},{5,4},{6,5},{7,6},{0,7},{9,8},{10,9},{11,1... | collective-permute-start | bytes 1572872 | tf_op jit(solution)/shard_map/ppermute | solution.py:29
  28.3 25.3 %diffuse_early.1 = (f32[8192,128]{1,0:T(8,128)}, f32[1024,128]{1,0:T(8,128)}, f32[512,16]{1,0:T(8,128)}, s32[32,128]{1,0:T(8,128)}, s32[384,128]{1,0:T(8,128)}, /*index=5*/f32[192,128]{1,0:T(8,128)}, s32[8,128]{1,0:T(8,128)}) custom-call(s32[6,4096]{1,0:T(8,128)} %faces_any, s32[16,32]{1,0:T(8,128)} %bitcast.7, s32[1,32]{1,0:T(1,128)} %mig_counts.1, ...), custom_call_target="tpu_custom_call" | custom-call | flops 20000000000 | bytes 16777216 | tf_op jit(solution)/shard_map/diffuse_early/pallas_call | solution.py:482
  53.6 0.0 collective-permute-done.g0
  53.6 0.0 collective-permute-done.1.g1
  53.6 0.0 collective-permute-done.2.g2
  53.6 0.0 collective-permute-done.3.g3
  53.6 4.8 %diffuse_leaving.1 = bf16[512,256]{1,0:T(8,128)(2,1)} custom-call(s32[32,128]{1,0:T(8,128)} %get-tuple-element.31.late_any, f32[1024,128]{1,0:T(8,128)} %get-tuple-element.32.sums_any, f32[512,16]{1,0:T(8,128)} %get-tuple-element.33.coef_any, bf16[1024,256]{1,0:T(8,128)(2,1)} %collective-permute-done.g0, bf16[1024,256]{1,0:T(8,128)(2,1)} %collective-permute-done.1.g1, ...), custom_call_target="tpu_custom_call" | custom-call | flops 500000000 | bytes 8388608 | tf_op jit(solution)/shard_map/diffuse_leaving/pallas_call | solution.py:572
  58.4 3.3 %all-to-all-start = ((bf16[32,16,256]{2,1,0:T(8,128)(2,1)}), bf16[32,16,256]{2,1,0:T(8,128)(2,1)S(1)}, u32[]{:S(2)}, u32[]{:S(2)}) async-start(bf16[32,16,256]{2,1,0:T(8,128)(2,1)} %bitcast.4), calls=%async_computation | async-start | bytes 524288 | tf_op jit(solution)/shard_map/all_to_all | solution.py:728
  61.7 9.8 %diffuse_late.1 = bf16[4096,256]{1,0:T(8,128)(2,1)} custom-call(s32[384,128]{1,0:T(8,128)} %get-tuple-element.23.lists, f32[192,128]{1,0:T(8,128)} %get-tuple-element.24.list_coef, s32[8,128]{1,0:T(8,128)} %get-tuple-element.25.counts, f32[8192,128]{1,0:T(8,128)} %get-tuple-element.26.early, bf16[1024,256]{1,0:T(8,128)(2,1)} %collective-permute-done.g0, ...), custom_call_target="tpu_custom_call" | custom-call | flops 8999999488 | bytes 25165824 | tf_op jit(solution)/shard_map/diffuse_late/pallas_call | solution.py:689
  71.5 0.8 %all-to-all-done = bf16[32,16,256]{2,1,0:T(8,128)(2,1)S(1)} async-done(((bf16[32,16,256]{2,1,0:T(8,128)(2,1)}), bf16[32,16,256]{2,1,0:T(8,128)(2,1)S(1)}, u32[]{:S(2)}, u32[]{:S(2)}) %all-to-all-start) | async-done | bytes 262176 | tf_op jit(solution)/shard_map/all_to_all | solution.py:728
  72.3 0.7 copy.11
Async XLA Ops:
  20.5 33.1 %collective-permute-start = (bf16[1024,256]{1,0:T(8,128)(2,1)}, bf16[1024,256]{1,0:T(8,128)(2,1)}, u32[]{:S(2)}, u32[]{:S(2)}) collective-permute-start(bf16[1024,256]{1,0:T(8,128)(2,1)} %get-tuple-element.27), channel_id=1, source_target_pairs={{24,0},{0,8},{8,16},{16,24},{25,1},{1,9},{9,17},{17,25},{26,2},{2,... | collective-permute-start | bytes 1572872 | tf_op jit(solution)/shard_map/ppermute | solution.py:29
  23.6 30.0 %collective-permute-start.1 = (bf16[1024,256]{1,0:T(8,128)(2,1)}, bf16[1024,256]{1,0:T(8,128)(2,1)}, u32[]{:S(2)}, u32[]{:S(2)}) collective-permute-start(bf16[1024,256]{1,0:T(8,128)(2,1)} %get-tuple-element.28), channel_id=1, source_target_pairs={{8,0},{16,8},{24,16},{0,24},{9,1},{17,9},{25,17},{1,25},{10,2},{18... | collective-permute-start | bytes 1572872 | tf_op jit(solution)/shard_map/ppermute | solution.py:29
  25.7 27.9 %collective-permute-start.2 = (bf16[1024,256]{1,0:T(8,128)(2,1)}, bf16[1024,256]{1,0:T(8,128)(2,1)}, u32[]{:S(2)}, u32[]{:S(2)}) collective-permute-start(bf16[1024,256]{1,0:T(8,128)(2,1)} %get-tuple-element.29), channel_id=1, source_target_pairs={{7,0},{0,1},{1,2},{2,3},{3,4},{4,5},{5,6},{6,7},{15,8},{8,9},{9,10... | collective-permute-start | bytes 1572872 | tf_op jit(solution)/shard_map/ppermute | solution.py:29
  25.7 27.9 %collective-permute-start.3 = (bf16[1024,256]{1,0:T(8,128)(2,1)}, bf16[1024,256]{1,0:T(8,128)(2,1)}, u32[]{:S(2)}, u32[]{:S(2)}) collective-permute-start(bf16[1024,256]{1,0:T(8,128)(2,1)} %get-tuple-element.30), channel_id=1, source_target_pairs={{1,0},{2,1},{3,2},{4,3},{5,4},{6,5},{7,6},{0,7},{9,8},{10,9},{11,1... | collective-permute-start | bytes 1572872 | tf_op jit(solution)/shard_map/ppermute | solution.py:29
  58.4 13.9 %all-to-all-start = ((bf16[32,16,256]{2,1,0:T(8,128)(2,1)}), bf16[32,16,256]{2,1,0:T(8,128)(2,1)S(1)}, u32[]{:S(2)}, u32[]{:S(2)}) async-start(bf16[32,16,256]{2,1,0:T(8,128)(2,1)} %bitcast.4), calls=%async_computation | async-start | bytes 524288 | tf_op jit(solution)/shard_map/all_to_all | solution.py:728

commit v5 on v4

--- a/solution.py
+++ b/solution.py
@@ -268,14 +268,14 @@
             pltpu.VMEM((2 * cells, LANES), F32),
             pltpu.VMEM((cells, 2 * LANES), BF16),
             pltpu.VMEM(kernels.shape, BF16),
-            pltpu.VMEM((2 * most * TILE, LANES), F32),
+            pltpu.VMEM((2 * most * TILE + 8, LANES), F32),
             pltpu.VMEM((class_count, 2 * LANES, 2 * LANES), BF16),
             pltpu.VMEM((rows + 16, LANES), I32),
             pltpu.SMEM((rows + 16, LANES), I32),
             pltpu.VMEM((4 * export // LANES, LANES), I32),
             pltpu.SMEM((4 * export // LANES, LANES), I32),
-            pltpu.VMEM((2 * LANES, LANES), F32),
-            pltpu.VMEM((2 * LANES, LANES), F32),
+            pltpu.VMEM((2 * LANES + 8, LANES), F32),
+            pltpu.VMEM((2 * LANES + 8, LANES), F32),
             pltpu.SemaphoreType.DMA,
             pltpu.SemaphoreType.DMA((4,)),
             pltpu.SemaphoreType.DMA,
@@ -493,14 +493,14 @@
         in_specs=[hbm(), smem(), vmem(), hbm(), hbm()],
         out_specs=(hbm(), vmem(), vmem(), vmem(), vmem(), vmem(), vmem()),
         scratch_shapes=[
-            pltpu.VMEM((2 * cells, LANES), F32),
+            pltpu.VMEM((2 * cells + 8, LANES), F32),
             pltpu.VMEM((face_count, cells), I32),
             pltpu.VMEM((face_count, cells), F32),
             pltpu.VMEM((face_count * cells // LANES, LANES), F32),
             pltpu.SemaphoreType.DMA((2,)),
             pltpu.VMEM((2 * (cells + late_rows), LANES), F32),
-            pltpu.VMEM((2 * face_count * CHUNK, LANES), F32),
-            pltpu.VMEM((2 * face_count * CHUNK, LANES), F32),
+            pltpu.VMEM((2 * face_count * CHUNK + 8, LANES), F32),
+            pltpu.VMEM((2 * face_count * CHUNK + 8, LANES), F32),
             pltpu.VMEM((2 * padded, cells), F32),
             pltpu.VMEM((cells, 2 * padded), F32),
             pltpu.VMEM((face_count * cells // LANES, LANES), I32),
@@ -520,7 +520,7 @@
     ghost_copies = start_ghosts((g0, g1, g2, g3), landed, ghost_sems)
     copies = [
         pltpu.make_async_copy(late_any, late_s, late_sem),
-        pltpu.make_async_copy(sums_any, mig_sums, sums_sem),
+        pltpu.make_async_copy(sums_any, mig_sums.at[pl.ds(0, sums_any.shape[0])], sums_sem),
         pltpu.make_async_copy(coef_any, mig_coef, coef_sem),
     ]
     for copy in copies:
@@ -577,10 +577,10 @@
         scratch_shapes=[
             pltpu.VMEM((2 * ghost_rows + 8, LANES), F32),
             pltpu.VMEM((len(ghosts),) + ghosts[0].shape, BF16),
-            pltpu.VMEM((2 * face_count * CHUNK, LANES), F32),
-            pltpu.VMEM((2 * face_count * CHUNK, LANES), F32),
+            pltpu.VMEM((2 * face_count * CHUNK + 8, LANES), F32),
+            pltpu.VMEM((2 * face_count * CHUNK + 8, LANES), F32),
             pltpu.SMEM(mig_late.shape, I32),
-            pltpu.VMEM(mig_sums.shape, F32),
+            pltpu.VMEM((mig_sums.shape[0] + 8, LANES), F32),
             pltpu.VMEM(mig_coef.shape, F32),
             pltpu.SemaphoreType.DMA,
             pltpu.SemaphoreType.DMA,
@@ -694,7 +694,7 @@
         scratch_shapes=[
             pltpu.VMEM((cells, 2 * LANES), BF16),
             pltpu.VMEM((2 * cells + 16, LANES), F32),
-            pltpu.VMEM((2 * ghost_rows, LANES), F32),
+            pltpu.VMEM((2 * ghost_rows + 8, LANES), F32),
             pltpu.VMEM((len(ghosts),) + ghosts[0].shape, BF16),
             pltpu.SMEM((face_count, 2 * cells // LANES, LANES), I32),
             pltpu.SMEM((face_count, cells // LANES, LANES), F32),
@@ -704,7 +704,7 @@
             pltpu.SemaphoreType.DMA((face_count,)),
             pltpu.SemaphoreType.DMA((face_count,)),
             pltpu.SemaphoreType.DMA,
-            pltpu.SemaphoreType.DMA((4,)),
+            pltpu.SemaphoreType.DMA((8,)),
         ],
         compiler_params=pltpu.CompilerParams(vmem_limit_bytes=LESS_VMEM_KIB * KIB),
         cost_estimate=pl.CostEstimate(flops=9_000_000_000, bytes_accessed=24 * MIB, transcendentals=0),

time: 73.5 us -> 73.4 us (level)
  no operation moved by 1% of the time
where the time goes in v5:
time: 73.4 us; the launch traced here: 72.9 us
  Pallas kernels  59.7 us (81%)
  starting transfers between devices  11.1 us (15%)
    pallas_call x1, Pallas kernels, diffuse_early(): pl.pallas_call(functools.partial(early_kernel, face_count, cells, late_ro...  25.1 us
    pallas_call x1, Pallas kernels, own_cells(): pl.pallas_call(functools.partial(own_kernel, cells), out_shape=(jax.Shape...  19.9 us
    pallas_call x1, Pallas kernels, diffuse_late(): pl.pallas_call(functools.partial(late_kernel, face_count, cells), out_sha...  9.95 us
    ppermute x4, starting transfers between devices, passed_along(): return lax.ppermute(block, axis, route)  7.81 us
    pallas_call x1, Pallas kernels, diffuse_leaving(): pl.pallas_call(functools.partial(leave_kernel, face_count), out_shape=jax...  4.74 us
    all_to_all x1, starting transfers between devices, body(): lax.all_to_all(leaving.reshape(domains, capacity, row_width), ('dx', 'dy'...  3.32 us
  transfers between devices with their start and end apart: 5, of which 1 were waited for; matrix products, arithmetic and copies ran while one was open for 0% of the time, Pallas kernels for 48%

profile of v5, /device:TPU:0, one launch (start us, length us, event | category | flops | bytes accessed | tf_op | source)
XLA Modules:
  0.0 72.9 jit_solution(9210510358267609686)
XLA Ops:
  0.6 19.9 %coagulate_own.1 = (f32[8192,128]{1,0:T(8,128)}, bf16[1024,256]{1,0:T(8,128)(2,1)}, bf16[1024,256]{1,0:T(8,128)(2,1)}, bf16[1024,256]{1,0:T(8,128)(2,1)}, bf16[1024,256]{1,0:T(8,128)(2,1)}) custom-call(s32[32,128]{1,0:T(8,128)} %bitcast.6, s32[1,4,1024]{2,1,0:T(4,128)} %exp_ref.1, bf16[4096,256]{1,0:T(8,128)(2,1)} %dust_any.1, bf16[8,2,128,128]{3,2,1,0:T(8,128)(2,1)} %kern_any.1), custom_call_target="tpu_custom_call" | custom-call | flops 8999999488 | bytes 12582912 | tf_op jit(solution)/shard_map/coagulate_own/pallas_call | solution.py:257
  20.6 3.1 %collective-permute-start = (bf16[1024,256]{1,0:T(8,128)(2,1)}, bf16[1024,256]{1,0:T(8,128)(2,1)}, u32[]{:S(2)}, u32[]{:S(2)}) collective-permute-start(bf16[1024,256]{1,0:T(8,128)(2,1)} %get-tuple-element.27), channel_id=1, source_target_pairs={{24,0},{0,8},{8,16},{16,24},{25,1},{1,9},{9,17},{17,25},{26,2},{2,... | collective-permute-start | bytes 1572872 | tf_op jit(solution)/shard_map/ppermute | solution.py:29
  23.7 2.1 %collective-permute-start.1 = (bf16[1024,256]{1,0:T(8,128)(2,1)}, bf16[1024,256]{1,0:T(8,128)(2,1)}, u32[]{:S(2)}, u32[]{:S(2)}) collective-permute-start(bf16[1024,256]{1,0:T(8,128)(2,1)} %get-tuple-element.28), channel_id=1, source_target_pairs={{8,0},{16,8},{24,16},{0,24},{9,1},{17,9},{25,17},{1,25},{10,2},{18... | collective-permute-start | bytes 1572872 | tf_op jit(solution)/shard_map/ppermute | solution.py:29
  25.8 0.0 collective-permute-start.2
  25.8 2.6 %collective-permute-start.3 = (bf16[1024,256]{1,0:T(8,128)(2,1)}, bf16[1024,256]{1,0:T(8,128)(2,1)}, u32[]{:S(2)}, u32[]{:S(2)}) collective-permute-start(bf16[1024,256]{1,0:T(8,128)(2,1)} %get-tuple-element.30), channel_id=1, source_target_pairs={{1,0},{2,1},{3,2},{4,3},{5,4},{6,5},{7,6},{0,7},{9,8},{10,9},{11,1... | collective-permute-start | bytes 1572872 | tf_op jit(solution)/shard_map/ppermute | solution.py:29
  28.4 25.1 %diffuse_early.1 = (f32[8192,128]{1,0:T(8,128)}, f32[1024,128]{1,0:T(8,128)}, f32[512,16]{1,0:T(8,128)}, s32[32,128]{1,0:T(8,128)}, s32[384,128]{1,0:T(8,128)}, /*index=5*/f32[192,128]{1,0:T(8,128)}, s32[8,128]{1,0:T(8,128)}) custom-call(s32[6,4096]{1,0:T(8,128)} %faces_any, s32[16,32]{1,0:T(8,128)} %bitcast.7, s32[1,32]{1,0:T(1,128)} %mig_counts.1, ...), custom_call_target="tpu_custom_call" | custom-call | flops 20000000000 | bytes 16777216 | tf_op jit(solution)/shard_map/diffuse_early/pallas_call | solution.py:482
  53.5 0.0 collective-permute-done.g0
  53.5 0.0 collective-permute-done.1.g1
  53.5 0.0 collective-permute-done.2.g2
  53.5 0.0 collective-permute-done.3.g3
  53.5 4.7 %diffuse_leaving.1 = bf16[512,256]{1,0:T(8,128)(2,1)} custom-call(s32[32,128]{1,0:T(8,128)} %get-tuple-element.31.late_any, f32[1024,128]{1,0:T(8,128)} %get-tuple-element.32.sums_any, f32[512,16]{1,0:T(8,128)} %get-tuple-element.33.coef_any, bf16[1024,256]{1,0:T(8,128)(2,1)} %collective-permute-done.g0, bf16[1024,256]{1,0:T(8,128)(2,1)} %collective-permute-done.1.g1, ...), custom_call_target="tpu_custom_call" | custom-call | flops 500000000 | bytes 8388608 | tf_op jit(solution)/shard_map/diffuse_leaving/pallas_call | solution.py:572
  58.3 3.3 %all-to-all-start = ((bf16[32,16,256]{2,1,0:T(8,128)(2,1)}), bf16[32,16,256]{2,1,0:T(8,128)(2,1)S(1)}, u32[]{:S(2)}, u32[]{:S(2)}) async-start(bf16[32,16,256]{2,1,0:T(8,128)(2,1)} %bitcast.4), calls=%async_computation | async-start | bytes 524288 | tf_op jit(solution)/shard_map/all_to_all | solution.py:728
  61.6 9.9 %diffuse_late.1 = bf16[4096,256]{1,0:T(8,128)(2,1)} custom-call(s32[384,128]{1,0:T(8,128)} %get-tuple-element.23.lists, f32[192,128]{1,0:T(8,128)} %get-tuple-element.24.list_coef, s32[8,128]{1,0:T(8,128)} %get-tuple-element.25.counts, f32[8192,128]{1,0:T(8,128)} %get-tuple-element.26.early, bf16[1024,256]{1,0:T(8,128)(2,1)} %collective-permute-done.g0, ...), custom_call_target="tpu_custom_call" | custom-call | flops 8999999488 | bytes 25165824 | tf_op jit(solution)/shard_map/diffuse_late/pallas_call | solution.py:689
  71.5 0.6 all-to-all-done
  72.2 0.7 copy.11
Async XLA Ops:
  20.6 32.9 %collective-permute-start = (bf16[1024,256]{1,0:T(8,128)(2,1)}, bf16[1024,256]{1,0:T(8,128)(2,1)}, u32[]{:S(2)}, u32[]{:S(2)}) collective-permute-start(bf16[1024,256]{1,0:T(8,128)(2,1)} %get-tuple-element.27), channel_id=1, source_target_pairs={{24,0},{0,8},{8,16},{16,24},{25,1},{1,9},{9,17},{17,25},{26,2},{2,... | collective-permute-start | bytes 1572872 | tf_op jit(solution)/shard_map/ppermute | solution.py:29
  23.7 29.8 %collective-permute-start.1 = (bf16[1024,256]{1,0:T(8,128)(2,1)}, bf16[1024,256]{1,0:T(8,128)(2,1)}, u32[]{:S(2)}, u32[]{:S(2)}) collective-permute-start(bf16[1024,256]{1,0:T(8,128)(2,1)} %get-tuple-element.28), channel_id=1, source_target_pairs={{8,0},{16,8},{24,16},{0,24},{9,1},{17,9},{25,17},{1,25},{10,2},{18... | collective-permute-start | bytes 1572872 | tf_op jit(solution)/shard_map/ppermute | solution.py:29
  25.8 27.7 %collective-permute-start.2 = (bf16[1024,256]{1,0:T(8,128)(2,1)}, bf16[1024,256]{1,0:T(8,128)(2,1)}, u32[]{:S(2)}, u32[]{:S(2)}) collective-permute-start(bf16[1024,256]{1,0:T(8,128)(2,1)} %get-tuple-element.29), channel_id=1, source_target_pairs={{7,0},{0,1},{1,2},{2,3},{3,4},{4,5},{5,6},{6,7},{15,8},{8,9},{9,10... | collective-permute-start | bytes 1572872 | tf_op jit(solution)/shard_map/ppermute | solution.py:29
  25.8 27.7 %collective-permute-start.3 = (bf16[1024,256]{1,0:T(8,128)(2,1)}, bf16[1024,256]{1,0:T(8,128)(2,1)}, u32[]{:S(2)}, u32[]{:S(2)}) collective-permute-start(bf16[1024,256]{1,0:T(8,128)(2,1)} %get-tuple-element.30), channel_id=1, source_target_pairs={{1,0},{2,1},{3,2},{4,3},{5,4},{6,5},{7,6},{0,7},{9,8},{10,9},{11,1... | collective-permute-start | bytes 1572872 | tf_op jit(solution)/shard_map/ppermute | solution.py:29
  58.3 13.9 %all-to-all-start = ((bf16[32,16,256]{2,1,0:T(8,128)(2,1)}), bf16[32,16,256]{2,1,0:T(8,128)(2,1)S(1)}, u32[]{:S(2)}, u32[]{:S(2)}) async-start(bf16[32,16,256]{2,1,0:T(8,128)(2,1)} %bitcast.4), calls=%async_computation | async-start | bytes 524288 | tf_op jit(solution)/shard_map/all_to_all | solution.py:728

commit v6 on v5

--- a/solution.py
+++ b/solution.py
@@ -98,16 +98,21 @@
 
 
 def substeps(state, weights):
-    one, two = state[:, :LANES], state[:, LANES:]
     bins = float(LANES)
+    rows = state.shape[0] // 6
+    pieces = [(state[p * rows:(p + 1) * rows, :LANES], state[p * rows:(p + 1) * rows, LANES:]) for p in range(6)]
     for _ in range(SUBSTEPS):
-        operand = jnp.concatenate([one, two], axis=1).astype(BF16)
-        square_one = jnp.sum(one * one, axis=1, keepdims=True)
-        square_two = jnp.sum(two * two, axis=1, keepdims=True)
+        operand = jnp.concatenate([jnp.concatenate(piece, axis=1).astype(BF16) for piece in pieces], axis=0)
         product = dot(operand, weights)
-        one = one + product[:, :LANES] * (1.0 / bins - pl.reciprocal(bins + square_one, approx=True))
-        two = two + product[:, LANES:] * (1.0 / bins - pl.reciprocal(bins + square_two, approx=True))
-    return one.astype(BF16), two.astype(BF16)
+        for p, (one, two) in enumerate(pieces):
+            here = product[p * rows:(p + 1) * rows]
+            square_one = jnp.sum(one * one, axis=1, keepdims=True)
+            square_two = jnp.sum(two * two, axis=1, keepdims=True)
+            one = one + here[:, :LANES] * (1.0 / bins - pl.reciprocal(bins + square_one, approx=True))
+            two = two + here[:, LANES:] * (1.0 / bins - pl.reciprocal(bins + square_two, approx=True))
+            pieces[p] = (one, two)
+    ones, twos = [piece[0] for piece in pieces], [piece[1] for piece in pieces]
+    return jnp.concatenate(ones, axis=0).astype(BF16), jnp.concatenate(twos, axis=0).astype(BF16)
 
 
 def send_rows(ids, steps, table, outbound, sent, sems, stages):
@@ -616,20 +621,21 @@
     for part in list_copies:
         part.wait()
     copy.wait()
+    flat_lists = lists_s.reshape(face_count * 2 * cells)
+    flat_coef = coef_s.reshape(face_count * cells)
     for f in range(face_count):
         number = counts_s[f, 0]
 
         per_line = LANES // BATCH
-        line_shift = per_line.bit_length() - 1
         split = FIRST_LINES * per_line
         rest = 2 * cells // LANES - 2 * FIRST_LINES
 
-        def add(cell_line, row_line, coef_line, lane):
+        def add(cell_at, row_at, coef_at):
             for j in range(BATCH // GROUP):
                 found = []
-                of_cells = lists_s.at[f, cell_line, pl.ds(lane + j * GROUP, GROUP)]
-                of_rows = lists_s.at[f, row_line, pl.ds(lane + j * GROUP, GROUP)]
-                weights = coef_s.at[f, coef_line, pl.ds(lane + j * GROUP, GROUP)]
+                of_cells = flat_lists.at[pl.ds(cell_at + j * GROUP, GROUP)]
+                of_rows = flat_lists.at[pl.ds(row_at + j * GROUP, GROUP)]
+                weights = flat_coef.at[pl.ds(coef_at + j * GROUP, GROUP)]
                 for k in range(GROUP):
                     row = rows2(of_cells[steps[k]])
                     late = table[rows2(of_rows[steps[k]]), :]
@@ -638,13 +644,13 @@
                     sums[row, :] = value
 
         def near(i, carry):
-            line = i >> line_shift
-            add(line, line + FIRST_LINES, line, (i & (per_line - 1)) * BATCH)
+            at = i * BATCH
+            add(at + f * 2 * cells, at + (f * 2 * cells + FIRST_LINES * LANES), at + f * cells)
             return carry
 
         def far(i, carry):
-            line = (i >> line_shift) + FIRST_LINES
-            add(line, line + rest // 2, line - FIRST_LINES, (i & (per_line - 1)) * BATCH)
+            at = i * BATCH
+            add(at + (f * 2 * cells + FIRST_LINES * LANES), at + (f * 2 * cells + cells), at + f * cells)
             return carry
 
         batches = (number + (BATCH - 1)) // BATCH

time: 73.4 us -> 73.2 us (level)
  Pallas kernels: 59.7 us -> 58.5 us
  waiting for transfers between devices: 0.65 us -> 1.65 us
    pallas_call x1, Pallas kernels: 9.95 us -> 8.95 us  [diffuse_late(): pl.pallas_call(functools.partial(late_kernel, face_count, cells), out_sha...]
    all_to_all x1, waiting for transfers between devices: 0.64 us -> 1.64 us  [body(): lax.all_to_all(leaving.reshape(domains, capacity, row_width), ('dx', 'dy'...]
  transfers between devices with their start and end apart: 5 -> 5, of which waited for: 1 -> 1; matrix products, arithmetic and copies ran while one was open for 0% -> 0% of each run, Pallas kernels for 48% -> 47%
where the time goes in v6:
time: 73.2 us; the launch traced here: 72.7 us
  Pallas kernels  58.5 us (80%)
  starting transfers between devices  11.1 us (15%)
  waiting for transfers between devices  1.65 us (2%)
    pallas_call x1, Pallas kernels, diffuse_early(): pl.pallas_call(functools.partial(early_kernel, face_count, cells, late_ro...  25.1 us
    pallas_call x1, Pallas kernels, own_cells(): pl.pallas_call(functools.partial(own_kernel, cells), out_shape=(jax.Shape...  19.8 us
    pallas_call x1, Pallas kernels, diffuse_late(): pl.pallas_call(functools.partial(late_kernel, face_count, cells), out_sha...  8.95 us
    ppermute x4, starting transfers between devices, passed_along(): return lax.ppermute(block, axis, route)  7.82 us
    pallas_call x1, Pallas kernels, diffuse_leaving(): pl.pallas_call(functools.partial(leave_kernel, face_count), out_shape=jax...  4.74 us
    all_to_all x1, starting transfers between devices, body(): lax.all_to_all(leaving.reshape(domains, capacity, row_width), ('dx', 'dy'...  3.33 us
    all_to_all x1, waiting for transfers between devices, body(): lax.all_to_all(leaving.reshape(domains, capacity, row_width), ('dx', 'dy'...  1.64 us
  transfers between devices with their start and end apart: 5, of which 1 were waited for; matrix products, arithmetic and copies ran while one was open for 0% of the time, Pallas kernels for 47%

profile of v6, /device:TPU:0, one launch (start us, length us, event | category | flops | bytes accessed | tf_op | source)
XLA Modules:
  0.0 72.7 jit_solution(17502981811288886577)
XLA Ops:
  0.6 19.8 %coagulate_own.1 = (f32[8192,128]{1,0:T(8,128)}, bf16[1024,256]{1,0:T(8,128)(2,1)}, bf16[1024,256]{1,0:T(8,128)(2,1)}, bf16[1024,256]{1,0:T(8,128)(2,1)}, bf16[1024,256]{1,0:T(8,128)(2,1)}) custom-call(s32[32,128]{1,0:T(8,128)} %bitcast.6, s32[1,4,1024]{2,1,0:T(4,128)} %exp_ref.1, bf16[4096,256]{1,0:T(8,128)(2,1)} %dust_any.1, bf16[8,2,128,128]{3,2,1,0:T(8,128)(2,1)} %kern_any.1), custom_call_target="tpu_custom_call" | custom-call | flops 8999999488 | bytes 12582912 | tf_op jit(solution)/shard_map/coagulate_own/pallas_call | solution.py:262
  20.4 3.1 %collective-permute-start = (bf16[1024,256]{1,0:T(8,128)(2,1)}, bf16[1024,256]{1,0:T(8,128)(2,1)}, u32[]{:S(2)}, u32[]{:S(2)}) collective-permute-start(bf16[1024,256]{1,0:T(8,128)(2,1)} %get-tuple-element.27), channel_id=1, source_target_pairs={{24,0},{0,8},{8,16},{16,24},{25,1},{1,9},{9,17},{17,25},{26,2},{2,... | collective-permute-start | bytes 1572872 | tf_op jit(solution)/shard_map/ppermute | solution.py:29
  23.5 2.1 %collective-permute-start.1 = (bf16[1024,256]{1,0:T(8,128)(2,1)}, bf16[1024,256]{1,0:T(8,128)(2,1)}, u32[]{:S(2)}, u32[]{:S(2)}) collective-permute-start(bf16[1024,256]{1,0:T(8,128)(2,1)} %get-tuple-element.28), channel_id=1, source_target_pairs={{8,0},{16,8},{24,16},{0,24},{9,1},{17,9},{25,17},{1,25},{10,2},{18... | collective-permute-start | bytes 1572872 | tf_op jit(solution)/shard_map/ppermute | solution.py:29
  25.6 0.0 collective-permute-start.2
  25.6 2.6 %collective-permute-start.3 = (bf16[1024,256]{1,0:T(8,128)(2,1)}, bf16[1024,256]{1,0:T(8,128)(2,1)}, u32[]{:S(2)}, u32[]{:S(2)}) collective-permute-start(bf16[1024,256]{1,0:T(8,128)(2,1)} %get-tuple-element.30), channel_id=1, source_target_pairs={{1,0},{2,1},{3,2},{4,3},{5,4},{6,5},{7,6},{0,7},{9,8},{10,9},{11,1... | collective-permute-start | bytes 1572872 | tf_op jit(solution)/shard_map/ppermute | solution.py:29
  28.2 25.1 %diffuse_early.1 = (f32[8192,128]{1,0:T(8,128)}, f32[1024,128]{1,0:T(8,128)}, f32[512,16]{1,0:T(8,128)}, s32[32,128]{1,0:T(8,128)}, s32[384,128]{1,0:T(8,128)}, /*index=5*/f32[192,128]{1,0:T(8,128)}, s32[8,128]{1,0:T(8,128)}) custom-call(s32[6,4096]{1,0:T(8,128)} %faces_any, s32[16,32]{1,0:T(8,128)} %bitcast.7, s32[1,32]{1,0:T(1,128)} %mig_counts.1, ...), custom_call_target="tpu_custom_call" | custom-call | flops 20000000000 | bytes 16777216 | tf_op jit(solution)/shard_map/diffuse_early/pallas_call | solution.py:487
  53.3 0.0 collective-permute-done.g0
  53.3 0.0 collective-permute-done.1.g1
  53.3 0.0 collective-permute-done.2.g2
  53.3 0.0 collective-permute-done.3.g3
  53.4 4.7 %diffuse_leaving.1 = bf16[512,256]{1,0:T(8,128)(2,1)} custom-call(s32[32,128]{1,0:T(8,128)} %get-tuple-element.31.late_any, f32[1024,128]{1,0:T(8,128)} %get-tuple-element.32.sums_any, f32[512,16]{1,0:T(8,128)} %get-tuple-element.33.coef_any, bf16[1024,256]{1,0:T(8,128)(2,1)} %collective-permute-done.g0, bf16[1024,256]{1,0:T(8,128)(2,1)} %collective-permute-done.1.g1, ...), custom_call_target="tpu_custom_call" | custom-call | flops 500000000 | bytes 8388608 | tf_op jit(solution)/shard_map/diffuse_leaving/pallas_call | solution.py:577
  58.1 3.3 %all-to-all-start = ((bf16[32,16,256]{2,1,0:T(8,128)(2,1)}), bf16[32,16,256]{2,1,0:T(8,128)(2,1)S(1)}, u32[]{:S(2)}, u32[]{:S(2)}) async-start(bf16[32,16,256]{2,1,0:T(8,128)(2,1)} %bitcast.4), calls=%async_computation | async-start | bytes 524288 | tf_op jit(solution)/shard_map/all_to_all | solution.py:734
  61.4 9.0 %diffuse_late.1 = bf16[4096,256]{1,0:T(8,128)(2,1)} custom-call(s32[384,128]{1,0:T(8,128)} %get-tuple-element.23.lists, f32[192,128]{1,0:T(8,128)} %get-tuple-element.24.list_coef, s32[8,128]{1,0:T(8,128)} %get-tuple-element.25.counts, f32[8192,128]{1,0:T(8,128)} %get-tuple-element.26.early, bf16[1024,256]{1,0:T(8,128)(2,1)} %collective-permute-done.g0, ...), custom_call_target="tpu_custom_call" | custom-call | flops 8999999488 | bytes 25165824 | tf_op jit(solution)/shard_map/diffuse_late/pallas_call | solution.py:695
  70.4 1.6 %all-to-all-done = bf16[32,16,256]{2,1,0:T(8,128)(2,1)S(1)} async-done(((bf16[32,16,256]{2,1,0:T(8,128)(2,1)}), bf16[32,16,256]{2,1,0:T(8,128)(2,1)S(1)}, u32[]{:S(2)}, u32[]{:S(2)}) %all-to-all-start) | async-done | bytes 262176 | tf_op jit(solution)/shard_map/all_to_all | solution.py:734
  72.0 0.7 copy.11
Async XLA Ops:
  20.4 32.9 %collective-permute-start = (bf16[1024,256]{1,0:T(8,128)(2,1)}, bf16[1024,256]{1,0:T(8,128)(2,1)}, u32[]{:S(2)}, u32[]{:S(2)}) collective-permute-start(bf16[1024,256]{1,0:T(8,128)(2,1)} %get-tuple-element.27), channel_id=1, source_target_pairs={{24,0},{0,8},{8,16},{16,24},{25,1},{1,9},{9,17},{17,25},{26,2},{2,... | collective-permute-start | bytes 1572872 | tf_op jit(solution)/shard_map/ppermute | solution.py:29
  23.5 29.8 %collective-permute-start.1 = (bf16[1024,256]{1,0:T(8,128)(2,1)}, bf16[1024,256]{1,0:T(8,128)(2,1)}, u32[]{:S(2)}, u32[]{:S(2)}) collective-permute-start(bf16[1024,256]{1,0:T(8,128)(2,1)} %get-tuple-element.28), channel_id=1, source_target_pairs={{8,0},{16,8},{24,16},{0,24},{9,1},{17,9},{25,17},{1,25},{10,2},{18... | collective-permute-start | bytes 1572872 | tf_op jit(solution)/shard_map/ppermute | solution.py:29
  25.6 27.7 %collective-permute-start.2 = (bf16[1024,256]{1,0:T(8,128)(2,1)}, bf16[1024,256]{1,0:T(8,128)(2,1)}, u32[]{:S(2)}, u32[]{:S(2)}) collective-permute-start(bf16[1024,256]{1,0:T(8,128)(2,1)} %get-tuple-element.29), channel_id=1, source_target_pairs={{7,0},{0,1},{1,2},{2,3},{3,4},{4,5},{5,6},{6,7},{15,8},{8,9},{9,10... | collective-permute-start | bytes 1572872 | tf_op jit(solution)/shard_map/ppermute | solution.py:29
  25.6 27.7 %collective-permute-start.3 = (bf16[1024,256]{1,0:T(8,128)(2,1)}, bf16[1024,256]{1,0:T(8,128)(2,1)}, u32[]{:S(2)}, u32[]{:S(2)}) collective-permute-start(bf16[1024,256]{1,0:T(8,128)(2,1)} %get-tuple-element.30), channel_id=1, source_target_pairs={{1,0},{2,1},{3,2},{4,3},{5,4},{6,5},{7,6},{0,7},{9,8},{10,9},{11,1... | collective-permute-start | bytes 1572872 | tf_op jit(solution)/shard_map/ppermute | solution.py:29
  58.1 13.9 %all-to-all-start = ((bf16[32,16,256]{2,1,0:T(8,128)(2,1)}), bf16[32,16,256]{2,1,0:T(8,128)(2,1)S(1)}, u32[]{:S(2)}, u32[]{:S(2)}) async-start(bf16[32,16,256]{2,1,0:T(8,128)(2,1)} %bitcast.4), calls=%async_computation | async-start | bytes 524288 | tf_op jit(solution)/shard_map/all_to_all | solution.py:734
